TPU v7x, 32 devices: a whole 2x2x4 slice. The times are simulated.
32 devices in a mesh: grp: 2 (over x), exp: 4 (over y, core), dp: 4 (over z).
Axes of the slice: x: 2, y: 2, z: 4, core: 2. Of those that a mesh axis runs over, the one named last changes fastest.
Arguments:
- tokens: bfloat16 [4096, 4096], P(('grp', 'exp', 'dp')), parts along dimension 0
- expert_ids: int32 [4096, 8], P(('grp', 'exp', 'dp')), parts along dimension 0, may hold values from 0 to 127, as said below
- router_weight: float32 [4096, 8], P(('grp', 'exp', 'dp')), parts along dimension 0, may hold values from 0.05 to 1
- window_ids: int32 [8], P('grp'), parts along dimension 0, may hold values from 0 to 127, as said below
- gate_weight: bfloat16 [8, 4096, 1536], P(('grp', 'exp'), None, 'dp'), parts along dimension 0, may hold values from -0.09375 to 0.09375
- up_weight: bfloat16 [8, 4096, 1536], P(('grp', 'exp'), None, 'dp'), parts along dimension 0, may hold values from -0.09375 to 0.09375
- down_weight: bfloat16 [8, 1536, 4096], P(('grp', 'exp'), 'dp'), parts along dimension 0, may hold values from -0.15625 to 0.15625
Outputs:
- combined: bfloat16 [4096, 4096], P(('grp', 'exp', 'dp')), parts along dimension 0
- gram_out: bfloat16 [8, 4096, 4096], P(('grp', 'exp'), None, 'dp'), parts along dimension 0
There are 2 independent parts, one for each index of `grp`. A program takes and returns all parts, laid end to end along the dimension named above; each array names one. Nothing has to cross between parts.
Inputs may be any that keep to these rules, and one draw needn't show every extreme that they name: `expert_ids`: each row names 8 different experts; in each aligned block of 128 rows (the rows of one device) every window expert is named by 1 to 8 rows, and some window expert by exactly 8 rows in every block. `window_ids`: 4 different experts; experts 0 and 127 are always among them.
All inputs are finite; a program needn't handle non-finite values.
Results may differ from a plain program's by a relative error of at most 0.0058.
Values may be sent and summed in bfloat16 or wider, within the bound.
No kernel may reach another device: no remote copies, remote signals or barrier semaphores. Data moves between devices by JAX's collectives and lax.ppermute only.
A program may use at most 128 MiB of HBM per device.

v0:
```python
import jax
import jax.numpy as jnp
from jax import lax
from jax.sharding import PartitionSpec as P

EXPERTS_ALL = 128
TOPK = 8
CAP = 8


def local(tokens, expert_ids, router_weight, window_ids, gate_weight, up_weight, down_weight):
    tok_count = tokens.shape[0]
    feat_width = tokens.shape[1]
    window_size = window_ids.shape[0]
    owner_count = lax.axis_size("exp")
    shard_count = lax.axis_size("dp")
    matches = expert_ids[:, :, None] == window_ids[None, None, :]
    routed = jnp.any(matches, axis=1).astype(jnp.float32)
    shares = jnp.sum(jnp.where(matches, router_weight[:, :, None], 0.0), axis=1)
    slot_ids = jnp.cumsum(routed, axis=0) - routed
    slot_range = jnp.arange(CAP, dtype=jnp.float32)
    placing = (slot_ids.T[:, None, :] == slot_range[None, :, None]).astype(jnp.float32) * routed.T[
        :, None, :
    ]
    outgoing = jnp.einsum(
        "jct,td->jcd", placing.astype(jnp.bfloat16), tokens, preferred_element_type=jnp.float32
    ).astype(jnp.bfloat16)
    gate_local = gate_weight[0]
    up_local = up_weight[0]
    down_local = down_weight[0]
    copies = jnp.broadcast_to(outgoing[None], (shard_count,) + outgoing.shape)
    arrived = lax.all_to_all(
        lax.all_to_all(copies, "exp", split_axis=1, concat_axis=1, tiled=True),
        "dp",
        split_axis=0,
        concat_axis=0,
        tiled=True,
    )
    row_block = arrived.reshape(-1, feat_width)
    gate_part = jnp.dot(row_block, gate_local, preferred_element_type=jnp.float32)
    up_part = jnp.dot(row_block, up_local, preferred_element_type=jnp.float32)
    hidden = (jax.nn.silu(gate_part) * up_part).astype(jnp.bfloat16)
    regrouped = lax.all_to_all(hidden, "dp", split_axis=0, concat_axis=1, tiled=True)
    summed = jnp.dot(
        regrouped,
        lax.all_gather(down_local, "dp", axis=0, tiled=True),
        preferred_element_type=jnp.float32,
    )
    expert_out = summed.astype(jnp.bfloat16)
    col_width = feat_width // shard_count
    col_start = lax.axis_index("dp") * col_width
    row_block = lax.all_gather(expert_out, "dp", axis=0, tiled=True)
    column_block = lax.dynamic_slice_in_dim(row_block, col_start, col_width, 1)
    gram_sum = lax.dot_general(
        row_block, column_block, (((0,), (0,)), ((), ())), preferred_element_type=jnp.float32
    )
    scaling = EXPERTS_ALL / (TOPK * tok_count * owner_count * shard_count)
    gram_out = (gram_sum * scaling).astype(jnp.bfloat16)[None]
    returned = lax.all_to_all(
        expert_out.reshape(window_size, CAP, feat_width),
        "exp",
        split_axis=0,
        concat_axis=0,
        tiled=True,
    )
    weighted = placing * shares.T[:, None, :]
    combined = jnp.einsum(
        "jct,jcd->td",
        weighted,
        returned.astype(jnp.float32),
        precision=lax.Precision.HIGHEST,
        preferred_element_type=jnp.float32,
    )
    return (combined.astype(jnp.bfloat16), gram_out)


def solution(mesh):
    in_specs = (
        P(("grp", "exp", "dp"), None),
        P(("grp", "exp", "dp"), None),
        P(("grp", "exp", "dp"), None),
        P("grp"),
        P(("grp", "exp"), None, "dp"),
        P(("grp", "exp"), None, "dp"),
        P(("grp", "exp"), "dp", None),
    )
    out_specs = (P(("grp", "exp", "dp"), None), P(("grp", "exp"), None, "dp"))
    return jax.shard_map(local, mesh=mesh, in_specs=in_specs, out_specs=out_specs, check_vma=False)
```

profile of v0, /device:TPU:0, one launch (start us, length us, event | category | flops | bytes accessed | tf_op | source)
XLA Modules:
  0.0 302.7 jit_solution(9146351984388671879)
XLA Ops:
  7.2 0.7 all-gather.6.cloned.1.call-update
  7.9 0.0 all-gather.4.cloned.1.call-start
  8.0 0.0 copy-done.1
  8.0 0.1 compare_reduce_fusion
  8.1 0.1 copy.29
  8.3 0.2 reduce_window_sum.13
  8.5 0.1 copy.30
  8.5 0.1 copy.31
  8.6 1.5 convolution_convert_fusion
  10.1 0.1 broadcast_in_dim.18
  10.2 18.5 %all_to_all.34 = bf16[4,4,8,4096]{3,2,0,1:T(8,128)(2,1)S(1)} all-to-all(bf16[4,4,8,4096]{3,2,0,1:T(8,128)(2,1)S(1)} %broadcast_in_dim.18), channel_id=1, replica_groups=mesh['grp'=2,'exp'=4,'dp'=4] {'exp'}, dimensions={1} | all-to-all | bytes 2097152 | tf_op jit(solution)/shard_map/all_to_all | solution.py:33
  28.7 0.1 copy.32
  28.8 59.6 %all_to_all.35 = bf16[4,4,8,4096]{3,2,1,0:T(8,128)(2,1)S(1)} all-to-all(bf16[4,4,8,4096]{3,2,1,0:T(8,128)(2,1)S(1)} %copy.32), channel_id=1, replica_groups=mesh['grp'=2,'exp'=4,'dp'=4] {'dp'}, dimensions={0} | all-to-all | bytes 2097152 | tf_op jit(solution)/shard_map/all_to_all | solution.py:32
  88.5 0.8 fusion.9
  89.2 0.7 fusion.14
  89.9 16.7 %all_to_all.36 = bf16[4,32,384]{2,1,0:T(8,128)(2,1)S(1)} all-to-all(bf16[4,32,384]{2,1,0:T(8,128)(2,1)S(1)} %bitcast.47), channel_id=1, replica_groups=mesh['grp'=2,'exp'=4,'dp'=4] {'dp'}, dimensions={0} | all-to-all | bytes 196608 | tf_op jit(solution)/shard_map/all_to_all | solution.py:43
  106.7 148.3 %all-gather.6.cloned.1.call-done = bf16[1,1536,4096]{2,1,0:T(8,128)(2,1)} async-done(((bf16[1,384,4096]{2,1,0:T(8,128)(2,1)}), bf16[1,1536,4096]{2,1,0:T(8,128)(2,1)}) %all-gather.6.cloned.1.call-update) | async-done | bytes 12582928 | tf_op jit(solution)/shard_map/all_gather | solution.py:46
  254.9 7.6 %fusion.4 = bf16[32,4096]{1,0:T(8,128)(2,1)} fusion(bf16[32,1536]{1,0:T(8,128)(2,1)S(1)} %bitcast.45, bf16[1,1536,4096]{2,1,0:T(8,128)(2,1)} %all-gather.6.cloned.1.call-done), kind=kOutput, calls=%fused_computation.6 | convolution fusion | flops 402784256 | bytes 12943360 | tf_op jit(solution)/shard_map/dot_general | solution.py:44
  262.6 3.4 %all-to-all-start.3 = ((bf16[4,8,4096]{2,1,0:T(8,128)(2,1)}), bf16[4,8,4096]{2,1,0:T(8,128)(2,1)S(1)}, u32[]{:S(2)}, u32[]{:S(2)}) async-start(bf16[4,8,4096]{2,1,0:T(8,128)(2,1)} %bitcast.44), calls=%async_computation.3 | async-start | bytes 524288 | tf_op jit(solution)/shard_map/all_to_all | solution.py:59
  266.0 0.1 fusion.19
  266.1 5.9 %all-to-all-done.3 = bf16[4,8,4096]{2,1,0:T(8,128)(2,1)S(1)} async-done(((bf16[4,8,4096]{2,1,0:T(8,128)(2,1)}), bf16[4,8,4096]{2,1,0:T(8,128)(2,1)S(1)}, u32[]{:S(2)}, u32[]{:S(2)}) %all-to-all-start.3) | async-done | bytes 262176 | tf_op jit(solution)/shard_map/all_to_all | solution.py:59
  272.0 2.0 fusion.3
  274.0 14.8 %all-gather.4.cloned.1.call-done = bf16[128,4096]{1,0:T(8,128)(2,1)} async-done(((bf16[32,4096]{1,0:T(8,128)(2,1)}), bf16[128,4096]{1,0:T(8,128)(2,1)}) %all-gather.4.cloned.1.call-update) | async-done | bytes 1048592 | tf_op jit(solution)/shard_map/all_gather | solution.py:52
  288.9 7.0 %fusion.2 = bf16[1,4096,1024]{2,1,0:T(8,128)(2,1)} fusion(bf16[128,4096]{1,0:T(8,128)(2,1)} %all-gather.4.cloned.1.call-done, s32[]{:T(128)S(6)} %select_n.8), kind=kOutput, calls=%fused_computation.3 | convolution fusion | flops 1082130432 | bytes 9699332 | tf_op jit(solution)/shard_map/dot_general | solution.py:54
  (14 shorter events, 0.1 us)
Async XLA Ops:
  7.2 81.3 %copy-start = (bf16[1,4096,384]{2,1,0:T(8,128)(2,1)S(1)}, bf16[1,4096,384]{2,1,0:T(8,128)(2,1)}, u32[]{:S(2)}) copy-start(bf16[1,4096,384]{2,1,0:T(8,128)(2,1)} %param.11) | copy-start | bytes 9437188
  7.2 0.8 copy-start.3
  7.2 0.8 copy-start.1
  7.2 247.7 %all-gather.6.cloned.1.call-start = ((), (), s32[]{:S(2)}) async-start(), calls=%async_computation.5 | async-start | bytes 15728640 | tf_op jit(solution)/shard_map/all_gather | solution.py:46
  7.9 280.9 %all-gather.4.cloned.1.call-start = ((), (), s32[]{:S(2)}) async-start(), calls=%async_computation.4 | async-start | bytes 1310720 | tf_op jit(solution)/shard_map/all_gather | solution.py:52
  28.8 60.4 %copy-start.4 = (bf16[1,4096,384]{2,1,0:T(8,128)(2,1)S(1)}, bf16[1,4096,384]{2,1,0:T(8,128)(2,1)}, u32[]{:S(2)}) copy-start(bf16[1,4096,384]{2,1,0:T(8,128)(2,1)} %param.12) | copy-start | bytes 9437188
  254.9 11.1 %copy-start.2 = (f32[128,8]{0,1:T(8,128)S(1)}, f32[128,8]{0,1:T(8,128)}, u32[]{:S(2)}) copy-start(f32[128,8]{0,1:T(8,128)} %param.9) | copy-start | bytes 12292
  262.6 9.4 %all-to-all-start.3 = ((bf16[4,8,4096]{2,1,0:T(8,128)(2,1)}), bf16[4,8,4096]{2,1,0:T(8,128)(2,1)S(1)}, u32[]{:S(2)}, u32[]{:S(2)}) async-start(bf16[4,8,4096]{2,1,0:T(8,128)(2,1)} %bitcast.44), calls=%async_computation.3 | async-start | bytes 524288 | tf_op jit(solution)/shard_map/all_to_all | solution.py:59
Sparse Core Ops, SparseCore 0:
  9.6 245.2 all-gather.5
  262.7 26.0 all-gather.3
where the time goes:
time: 303 us
  waiting for transfers between devices  170 us (56%)
  blocking collectives  94.8 us (31%)
  matrix products  19.6 us (6%)
  between operations  14.2 us (5%)
  starting transfers between devices  3.5 us (1%)
    all_gather x1, waiting for transfers between devices, local(): lax.all_gather(down_local, 'dp', axis=0, tiled=True)  148 us
    all_to_all x1, blocking collectives, local(): lax.all_to_all(lax.all_to_all(copies, 'exp', split_axis=1, concat_axis=1,...  59.6 us
    all_to_all x1, blocking collectives, local(): lax.all_to_all(copies, 'exp', split_axis=1, concat_axis=1, tiled=True)  18.5 us
    all_to_all x1, blocking collectives, local(): lax.all_to_all(hidden, 'dp', split_axis=0, concat_axis=1, tiled=True)  16.7 us
    all_gather x1, waiting for transfers between devices, local(): row_block = lax.all_gather(expert_out, 'dp', axis=0, tiled=True)  14.8 us
    dot_general x1, matrix products, local(): jnp.dot(regrouped, lax.all_gather(down_local, 'dp', axis=0, tiled=True),...  7.63 us
    dot_general x1, matrix products, local(): lax.dot_general(row_block, column_block, (((0,), (0,)), ((), ())), prefer...  7.03 us
  transfers between devices with their start and end apart: 3, of which 3 were waited for; matrix products, arithmetic and copies ran while one was open for 2% of the time, Pallas kernels for 0%

commit v1 on v0

v1 whole, which is shorter than its diff:
```python
import jax
import jax.numpy as jnp
from jax import lax
from jax.sharding import PartitionSpec as P

EXPERTS_ALL = 128
TOPK = 8
CAP = 8


def swap(x, axis, k):
    n = lax.axis_size(axis)
    return lax.ppermute(x, axis, [(i, i ^ k) for i in range(n)])


def gather_blocks(own, axis):
    n = lax.axis_size(axis)
    held = {0: own}
    bit = n // 2
    while bit:
        for r in list(held):
            held[r ^ bit] = swap(held[r], axis, bit)
        bit //= 2
    return [held[r] for r in range(n)]


def reduce_blocks(blocks, axis):
    n = lax.axis_size(axis)
    held = dict(enumerate(blocks))
    bit = 1
    while bit < n:
        keep = [r for r in held if not r & bit]
        keep.sort(reverse=True)
        held = {
            r: held[r] + swap(held[r ^ bit].astype(jnp.bfloat16), axis, bit).astype(jnp.float32)
            for r in keep
        }
        bit *= 2
    return held[0]


def local(tokens, expert_ids, router_weight, window_ids, gate_weight, up_weight, down_weight):
    tok_count, feat_width = tokens.shape
    window_size = window_ids.shape[0]
    owner_count = lax.axis_size("exp")
    shard_count = lax.axis_size("dp")
    slots = lax.axis_index("exp") ^ jnp.arange(window_size, dtype=jnp.int32)
    window = jnp.sum(
        jnp.where(
            slots[:, None] == jnp.arange(window_size, dtype=jnp.int32)[None, :],
            window_ids[None, :],
            0,
        ),
        axis=1,
    )
    matches = expert_ids[:, :, None] == window[None, None, :]
    routed = jnp.any(matches, axis=1).astype(jnp.float32)
    shares = jnp.sum(jnp.where(matches, router_weight[:, :, None], 0.0), axis=1)
    slot_ids = jnp.cumsum(routed, axis=0) - routed
    slot_range = jnp.arange(CAP, dtype=jnp.float32)
    placing = (slot_ids.T[:, None, :] == slot_range[None, :, None]).astype(jnp.float32) * routed.T[
        :, None, :
    ]
    placing = placing.reshape(window_size * CAP, tok_count)
    outgoing = jnp.dot(
        placing.astype(jnp.bfloat16), tokens, preferred_element_type=jnp.float32
    ).astype(jnp.bfloat16)
    pieces = [
        swap(outgoing[k * CAP : (k + 1) * CAP], "exp", k) if k else outgoing[:CAP]
        for k in range(owner_count)
    ]
    own_rows = jnp.concatenate(pieces, axis=0)
    row_block = jnp.concatenate(gather_blocks(own_rows, "dp"), axis=0)
    gate_part = jnp.dot(row_block, gate_weight[0], preferred_element_type=jnp.float32)
    up_part = jnp.dot(row_block, up_weight[0], preferred_element_type=jnp.float32)
    hidden = (jax.nn.silu(gate_part) * up_part).astype(jnp.bfloat16)
    partial = jnp.dot(hidden, down_weight[0], preferred_element_type=jnp.float32)
    own_count = owner_count * CAP
    blocks = [partial[r * own_count : (r + 1) * own_count] for r in range(shard_count)]
    expert_out = reduce_blocks(blocks, "dp").astype(jnp.bfloat16)
    col_width = feat_width // shard_count
    col_start = lax.axis_index("dp") * col_width
    row_block = jnp.concatenate(gather_blocks(expert_out, "dp"), axis=0)
    column_block = lax.dynamic_slice_in_dim(row_block, col_start, col_width, 1)
    gram_sum = lax.dot_general(
        row_block, column_block, (((0,), (0,)), ((), ())), preferred_element_type=jnp.float32
    )
    scaling = EXPERTS_ALL / (TOPK * tok_count * owner_count * shard_count)
    gram_out = (gram_sum * scaling).astype(jnp.bfloat16)[None]
    returned = jnp.concatenate(
        [
            swap(expert_out[k * CAP : (k + 1) * CAP], "exp", k) if k else expert_out[:CAP]
            for k in range(owner_count)
        ],
        axis=0,
    )
    weighted = placing.reshape(window_size, CAP, tok_count) * shares.T[:, None, :]
    combined = lax.dot_general(
        weighted.reshape(window_size * CAP, tok_count),
        returned.astype(jnp.float32),
        (((0,), (0,)), ((), ())),
        precision=lax.Precision.HIGHEST,
        preferred_element_type=jnp.float32,
    )
    return (combined.astype(jnp.bfloat16), gram_out)


def solution(mesh):
    in_specs = (
        P(("grp", "exp", "dp"), None),
        P(("grp", "exp", "dp"), None),
        P(("grp", "exp", "dp"), None),
        P("grp"),
        P(("grp", "exp"), None, "dp"),
        P(("grp", "exp"), None, "dp"),
        P(("grp", "exp"), "dp", None),
    )
    out_specs = (P(("grp", "exp", "dp"), None), P(("grp", "exp"), None, "dp"))
    return jax.shard_map(local, mesh=mesh, in_specs=in_specs, out_specs=out_specs, check_vma=False)
```

time: 303 us -> 96.7 us (0.32)
  waiting for transfers between devices: 170 us -> 54 us
  blocking collectives: 94.8 us -> 0 us
  between operations: 14.2 us -> 0.79 us
  starting transfers between devices: 3.5 us -> 15.9 us
  other arithmetic: 0.37 us -> 5.48 us
  local copies, waits for them, and re-layouts: 0.55 us -> 3.77 us
  matrix products: 19.6 us -> 16.4 us
    all_gather x2 -> x0, waiting for transfers between devices: 163 us -> none  [the longest x1 148 us: local(): lax.all_gather(down_local, 'dp', axis=0, tiled=True)]
    all_to_all x3 -> x0, blocking collectives: 94.8 us -> none  [the longest x1 59.6 us: local(): lax.all_to_all(lax.all_to_all(copies, 'exp', split_axis=1, concat_axis=1,...]
    ppermute x0 -> x15, waiting for transfers between devices: none -> 54 us  [swap(): return lax.ppermute(x, axis, [(i, i ^ k) for i in range(n)])]
    ppermute x0 -> x15, starting transfers between devices: none -> 15.9 us  [swap(): return lax.ppermute(x, axis, [(i, i ^ k) for i in range(n)])]
    all_to_all x1 -> x0, waiting for transfers between devices: 5.9 us -> none  [local(): lax.all_to_all(expert_out.reshape(window_size, CAP, feat_width), 'exp', s...]
    all_to_all x1 -> x0, starting transfers between devices: 3.42 us -> none  [local(): lax.all_to_all(expert_out.reshape(window_size, CAP, feat_width), 'exp', s...]
    dot_general x5 -> x4, matrix products: 12.6 us -> 10.7 us  [the longest x1 5.3 us: local(): jnp.dot(hidden, down_weight[0], preferred_element_type=jnp.float32)]
  transfers between devices with their start and end apart: 3 -> 15, of which waited for: 3 -> 9; matrix products, arithmetic and copies ran while one was open for 2% -> 5% of each run, Pallas kernels for 0% -> 0%
where the time goes in v1:
time: 96.7 us; the launch traced here: 96.3 us
  waiting for transfers between devices  54 us (56%)
  matrix products  16.4 us (17%)
  starting transfers between devices  15.9 us (16%)
  other arithmetic  5.48 us (6%)
  local copies, waits for them, and re-layouts  3.77 us (4%)
    ppermute x15, waiting for transfers between devices, swap(): return lax.ppermute(x, axis, [(i, i ^ k) for i in range(n)])  54 us
    ppermute x15, starting transfers between devices, swap(): return lax.ppermute(x, axis, [(i, i ^ k) for i in range(n)])  15.9 us
    dot_general x1, matrix products, local(): lax.dot_general(row_block, column_block, (((0,), (0,)), ((), ())), prefer...  5.77 us
    dot_general x1, matrix products, local(): jnp.dot(hidden, down_weight[0], preferred_element_type=jnp.float32)  5.3 us
    dot_general x1, matrix products, local(): lax.dot_general(weighted.reshape(window_size * CAP, tok_count), returned....  2.94 us
  transfers between devices with their start and end apart: 15, of which 9 were waited for; matrix products, arithmetic and copies ran while one was open for 5% of the time, Pallas kernels for 0%

profile of v1, /device:TPU:0, one launch (start us, length us, event | category | flops | bytes accessed | tf_op | source)
XLA Modules:
  0.0 96.3 jit_solution(4982283606279242935)
XLA Ops:
  0.7 1.0 %select_reduce_fusion = s32[4]{0:T(128)S(1)} fusion(s32[4]{0:T(128)} %param.10, s32[4]{0:T(128)S(1)} %iota_xor_fusion), kind=kLoop, calls=%fused_computation.52 | loop fusion | flops 44 | bytes 48 | tf_op jit(solution)/shard_map/reduce_sum | solution.py:48
  3.6 1.7 %convolution_convert_fusion.1 = bf16[32,4096]{1,0:T(8,128)(2,1)S(1)} fusion(bf16[128,4096]{1,0:T(8,128)(2,1)} %param.7, f32[4,128]{1,0:T(4,128)S(1)} %copy.15, f32[32]{0:T(128)S(1)} %eq.56, f32[4,128]{1,0:T(4,128)S(1)} %copy.14), kind=kOutput, calls=%fused_computation.3 | convolution fusion | flops 33693696 | bytes 1314944 | tf_op jit(solution)/shard_map/dot_general | solution.py:65
  5.8 2.6 %collective-permute-start.1 = (bf16[8,4096]{1,0:T(8,128)(2,1)S(1)}, bf16[8,4096]{1,0:T(8,128)(2,1)S(1)}, u32[]{:S(2)}, u32[]{:S(2)}) collective-permute-start(bf16[8,4096]{1,0:T(8,128)(2,1)S(1)} %get-tuple-element.11), channel_id=1, source_target_pairs={{0,8},{4,12},{8,0},{12,4},{1,9},{5,13},{9,1},{13,5},{2,10},{6,14},... | collective-permute-start | bytes 196616 | tf_op jit(solution)/shard_map/ppermute | solution.py:13
  8.5 2.6 %collective-permute-done.1 = bf16[8,4096]{1,0:T(8,128)(2,1)S(1)} collective-permute-done((bf16[8,4096]{1,0:T(8,128)(2,1)S(1)}, bf16[8,4096]{1,0:T(8,128)(2,1)S(1)}, u32[]{:S(2)}, u32[]{:S(2)}) %collective-permute-start.1) | collective-permute-done | bytes 65568 | tf_op jit(solution)/shard_map/ppermute | solution.py:13
  11.1 1.4 %collective-permute-done.2 = bf16[8,4096]{1,0:T(8,128)(2,1)S(1)} collective-permute-done((bf16[8,4096]{1,0:T(8,128)(2,1)S(1)}, bf16[8,4096]{1,0:T(8,128)(2,1)S(1)}, u32[]{:S(2)}, u32[]{:S(2)}) %collective-permute-start.2) | collective-permute-done | bytes 65568 | tf_op jit(solution)/shard_map/ppermute | solution.py:13
  12.5 1.6 %collective-permute-start.3 = (bf16[32,4096]{1,0:T(8,128)(2,1)S(1)}, bf16[32,4096]{1,0:T(8,128)(2,1)S(1)}, u32[]{:S(2)}, u32[]{:S(2)}) collective-permute-start(bf16[32,4096]{1,0:T(8,128)(2,1)S(1)} %pad_maximum_fusion.1), channel_id=1, source_target_pairs={{0,1},{1,0},{2,3},{3,2},{4,5},{5,4},{6,7},{7,6},{8,9},{9,8},{10,11... | collective-permute-start | bytes 786440 | tf_op jit(solution)/shard_map/ppermute | solution.py:13
  14.1 2.6 %collective-permute-start.4 = (bf16[32,4096]{1,0:T(8,128)(2,1)S(1)}, bf16[32,4096]{1,0:T(8,128)(2,1)S(1)}, u32[]{:S(2)}, u32[]{:S(2)}) collective-permute-start(bf16[32,4096]{1,0:T(8,128)(2,1)S(1)} %pad_maximum_fusion.1), channel_id=1, source_target_pairs={{0,2},{1,3},{2,0},{3,1},{4,6},{5,7},{6,4},{7,5},{8,10},{9,11},{10,... | collective-permute-start | bytes 786440 | tf_op jit(solution)/shard_map/ppermute | solution.py:13
  16.7 12.0 %collective-permute-done.4 = bf16[32,4096]{1,0:T(8,128)(2,1)S(1)} collective-permute-done((bf16[32,4096]{1,0:T(8,128)(2,1)S(1)}, bf16[32,4096]{1,0:T(8,128)(2,1)S(1)}, u32[]{:S(2)}, u32[]{:S(2)}) %collective-permute-start.4) | collective-permute-done | bytes 262176 | tf_op jit(solution)/shard_map/ppermute | solution.py:13
  29.3 5.9 %collective-permute-done.5 = bf16[32,4096]{1,0:T(8,128)(2,1)S(1)} collective-permute-done((bf16[32,4096]{1,0:T(8,128)(2,1)S(1)}, bf16[32,4096]{1,0:T(8,128)(2,1)S(1)}, u32[]{:S(2)}, u32[]{:S(2)}) %collective-permute-start.5) | collective-permute-done | bytes 262176 | tf_op jit(solution)/shard_map/ppermute | solution.py:13
  36.9 5.3 %fusion.44 = (bf16[128,4096]{1,0:T(8,128)(2,1)}, f32[128,4096]{1,0:T(8,128)}) fusion(bf16[1,384,4096]{2,1,0:T(8,128)(2,1)S(1)} %copy-done, f32[128,384]{1,0:T(8,128)S(1)} %fusion.3, bf16[128,4096]{1,0:T(8,128)(2,1)} %copy-done.1, bf16[1,4096,384]{2,1,0:T(8,128)(2,1)} %param.11), kind=kOutput, calls=%fused_computation.64 | convolution fusion | flops 806125568 | bytes 10682368 | tf_op jit(solution)/shard_map/dot_general | solution.py:77
  42.2 1.1 %fusion.40 = (bf16[32,4096]{1,0:T(8,128)(2,1)S(1)}, bf16[32,4096]{1,0:T(8,128)(2,1)S(1)}) fusion(bf16[128,4096]{1,0:T(8,128)(2,1)} %get-tuple-element.15), kind=kLoop, calls=%fused_computation.60 | loop fusion | bytes 1048576 | tf_op jit(solution)/shard_map/slice | solution.py:79
  43.3 1.6 %collective-permute-start.7 = (bf16[32,4096]{1,0:T(8,128)(2,1)S(1)}, bf16[32,4096]{1,0:T(8,128)(2,1)S(1)}, u32[]{:S(2)}, u32[]{:S(2)}) collective-permute-start(bf16[32,4096]{1,0:T(8,128)(2,1)S(1)} %get-tuple-element.3), channel_id=1, source_target_pairs={{0,1},{1,0},{2,3},{3,2},{4,5},{5,4},{6,7},{7,6},{8,9},{9,8},{10,11... | collective-permute-start | bytes 786440 | tf_op jit(solution)/shard_map/ppermute | solution.py:13
  45.4 10.0 %collective-permute-done.7 = bf16[32,4096]{1,0:T(8,128)(2,1)S(1)} collective-permute-done((bf16[32,4096]{1,0:T(8,128)(2,1)S(1)}, bf16[32,4096]{1,0:T(8,128)(2,1)S(1)}, u32[]{:S(2)}, u32[]{:S(2)}) %collective-permute-start.7) | collective-permute-done | bytes 262176 | tf_op jit(solution)/shard_map/ppermute | solution.py:13
  55.4 1.1 %fusion.7 = bf16[32,4096]{1,0:T(8,128)(2,1)S(1)} fusion(f32[128,4096]{1,0:T(8,128)} %get-tuple-element.16, bf16[32,4096]{1,0:T(8,128)(2,1)S(1)} %collective-permute-done.7), kind=kLoop, calls=%fused_computation.12 | loop fusion | flops 393216 | bytes 1048576 | tf_op jit(solution)/shard_map/convert_element_type | solution.py:35
  56.5 1.1 %collective-permute-start.8 = (bf16[32,4096]{1,0:T(8,128)(2,1)S(1)}, bf16[32,4096]{1,0:T(8,128)(2,1)S(1)}, u32[]{:S(2)}, u32[]{:S(2)}) collective-permute-start(bf16[32,4096]{1,0:T(8,128)(2,1)S(1)} %fusion.7), channel_id=1, source_target_pairs={{0,2},{1,3},{2,0},{3,1},{4,6},{5,7},{6,4},{7,5},{8,10},{9,11},{10,... | collective-permute-start | bytes 786440 | tf_op jit(solution)/shard_map/ppermute | solution.py:13
  58.2 13.8 %collective-permute-done.8 = bf16[32,4096]{1,0:T(8,128)(2,1)S(1)} collective-permute-done((bf16[32,4096]{1,0:T(8,128)(2,1)S(1)}, bf16[32,4096]{1,0:T(8,128)(2,1)S(1)}, u32[]{:S(2)}, u32[]{:S(2)}) %collective-permute-start.8) | collective-permute-done | bytes 262176 | tf_op jit(solution)/shard_map/ppermute | solution.py:13
  72.0 1.1 %fusion.9 = bf16[32,4096]{1,0:T(8,128)(2,1)S(1)} fusion(f32[128,4096]{1,0:T(8,128)} %get-tuple-element.16, bf16[32,4096]{1,0:T(8,128)(2,1)S(1)} %collective-permute-done.8, bf16[32,4096]{1,0:T(8,128)(2,1)S(1)} %collective-permute-done.6), kind=kLoop, calls=%fused_computation.15 | loop fusion | flops 655360 | bytes 1310720 | tf_op jit(solution)/shard_map/convert_element_type | solution.py:80
  73.2 2.7 %collective-permute-start.12 = (bf16[32,4096]{1,0:T(8,128)(2,1)S(1)}, bf16[32,4096]{1,0:T(8,128)(2,1)}, u32[]{:S(2)}, u32[]{:S(2)}) collective-permute-start(bf16[32,4096]{1,0:T(8,128)(2,1)S(1)} %fusion.9), channel_id=1, source_target_pairs={{0,1},{1,0},{2,3},{3,2},{4,5},{5,4},{6,7},{7,6},{8,9},{9,8},{10,11... | collective-permute-start | bytes 786440 | tf_op jit(solution)/shard_map/ppermute | solution.py:13
  77.3 1.4 %collective-permute-start.9 = (bf16[8,4096]{1,0:T(8,128)(2,1)}, bf16[8,4096]{1,0:T(8,128)(2,1)}, u32[]{:S(2)}, u32[]{:S(2)}) collective-permute-start(bf16[8,4096]{1,0:T(8,128)(2,1)} %get-tuple-element.7), channel_id=1, source_target_pairs={{0,4},{4,0},{8,12},{12,8},{1,5},{5,1},{9,13},{13,9},{2,6},{6,2},{1... | collective-permute-start | bytes 196616 | tf_op jit(solution)/shard_map/ppermute | solution.py:13
  78.7 4.0 %collective-permute-done.13 = bf16[32,4096]{1,0:T(8,128)(2,1)} collective-permute-done((bf16[32,4096]{1,0:T(8,128)(2,1)S(1)}, bf16[32,4096]{1,0:T(8,128)(2,1)}, u32[]{:S(2)}, u32[]{:S(2)}) %collective-permute-start.13) | collective-permute-done | bytes 262176 | tf_op jit(solution)/shard_map/ppermute | solution.py:13
  82.8 2.9 %convolution_convert_fusion = bf16[128,4096]{1,0:T(8,128)(2,1)} fusion(bf16[8,4096]{1,0:T(8,128)(2,1)} %collective-permute-done.11, bf16[8,4096]{1,0:T(8,128)(2,1)S(1)} %collective-permute-done.10, bf16[8,4096]{1,0:T(8,128)(2,1)} %collective-permute-done.9, bf16[8,4096]{1,0:T(8,128)(2,1)S(1)} %get-tuple-element.4, f32[4,128]{1,0:T(4,128)S(1)} %bitcast.49, ...), kind=kOutput, calls=%fused_computation.2 | convolution fusion | flops 202911744 | bytes 1316992 | tf_op jit(solution)/shard_map/dot_general | solution.py:98
  85.8 3.6 %collective-permute-done.14 = bf16[32,4096]{1,0:T(8,128)(2,1)} collective-permute-done((bf16[32,4096]{1,0:T(8,128)(2,1)}, bf16[32,4096]{1,0:T(8,128)(2,1)}, u32[]{:S(2)}, u32[]{:S(2)}) %collective-permute-start.14) | collective-permute-done | bytes 262176 | tf_op jit(solution)/shard_map/ppermute | solution.py:13
  89.4 1.2 %pad_maximum_fusion = bf16[128,4096]{1,0:T(8,128)(2,1)S(1)} fusion(bf16[32,4096]{1,0:T(8,128)(2,1)} %collective-permute-done.14, bf16[32,4096]{1,0:T(8,128)(2,1)} %collective-permute-done.13, bf16[32,4096]{1,0:T(8,128)(2,1)} %collective-permute-done.12, bf16[32,4096]{1,0:T(8,128)(2,1)S(1)} %fusion.9), kind=kLoop, calls=%fused_computation.10 | loop fusion | flops 4194304 | bytes 2097152 | tf_op jit(solution)/shard_map/concatenate | solution.py:83
  90.6 5.8 %fusion = bf16[1,4096,1024]{2,1,0:T(8,128)(2,1)} fusion(bf16[128,4096]{1,0:T(8,128)(2,1)S(1)} %pad_maximum_fusion, s32[]{:T(128)S(6)} %select_n.13), kind=kOutput, calls=%fused_computation.1 | convolution fusion | flops 1082130432 | bytes 9699332 | tf_op jit(solution)/shard_map/dot_general | solution.py:85
  (50 shorter events, 7.5 us)
Async XLA Ops:
  0.6 36.2 %copy-start = (bf16[1,384,4096]{2,1,0:T(8,128)(2,1)S(1)}, bf16[1,384,4096]{2,1,0:T(8,128)(2,1)}, u32[]{:S(2)}) copy-start(bf16[1,384,4096]{2,1,0:T(8,128)(2,1)} %param.13) | copy-start | bytes 9437188
  1.6 0.5 copy-start.5
  3.6 32.6 %copy-start.2 = (bf16[1,4096,384]{2,1,0:T(8,128)(2,1)S(1)}, bf16[1,4096,384]{2,1,0:T(8,128)(2,1)}, u32[]{:S(2)}) copy-start(bf16[1,4096,384]{2,1,0:T(8,128)(2,1)} %param.12) | copy-start | bytes 9437188
  5.3 3.2 %collective-permute-start = (bf16[8,4096]{1,0:T(8,128)(2,1)S(1)}, bf16[8,4096]{1,0:T(8,128)(2,1)S(1)}, u32[]{:S(2)}, u32[]{:S(2)}) collective-permute-start(bf16[8,4096]{1,0:T(8,128)(2,1)S(1)} %get-tuple-element.12), channel_id=1, source_target_pairs={{0,4},{4,0},{8,12},{12,8},{1,5},{5,1},{9,13},{13,9},{2,6},{6,2},{1... | collective-permute-start | bytes 196616 | tf_op jit(solution)/shard_map/ppermute | solution.py:13
  5.8 5.3 %collective-permute-start.1 = (bf16[8,4096]{1,0:T(8,128)(2,1)S(1)}, bf16[8,4096]{1,0:T(8,128)(2,1)S(1)}, u32[]{:S(2)}, u32[]{:S(2)}) collective-permute-start(bf16[8,4096]{1,0:T(8,128)(2,1)S(1)} %get-tuple-element.11), channel_id=1, source_target_pairs={{0,8},{4,12},{8,0},{12,4},{1,9},{5,13},{9,1},{13,5},{2,10},{6,14},... | collective-permute-start | bytes 196616 | tf_op jit(solution)/shard_map/ppermute | solution.py:13
  8.4 4.0 %collective-permute-start.2 = (bf16[8,4096]{1,0:T(8,128)(2,1)S(1)}, bf16[8,4096]{1,0:T(8,128)(2,1)S(1)}, u32[]{:S(2)}, u32[]{:S(2)}) collective-permute-start(bf16[8,4096]{1,0:T(8,128)(2,1)S(1)} %get-tuple-element.10), channel_id=1, source_target_pairs={{0,12},{4,8},{8,4},{12,0},{1,13},{5,9},{9,5},{13,1},{2,14},{6,10},... | collective-permute-start | bytes 196616 | tf_op jit(solution)/shard_map/ppermute | solution.py:13
  12.5 16.8 %collective-permute-start.3 = (bf16[32,4096]{1,0:T(8,128)(2,1)S(1)}, bf16[32,4096]{1,0:T(8,128)(2,1)S(1)}, u32[]{:S(2)}, u32[]{:S(2)}) collective-permute-start(bf16[32,4096]{1,0:T(8,128)(2,1)S(1)} %pad_maximum_fusion.1), channel_id=1, source_target_pairs={{0,1},{1,0},{2,3},{3,2},{4,5},{5,4},{6,7},{7,6},{8,9},{9,8},{10,11... | collective-permute-start | bytes 786440 | tf_op jit(solution)/shard_map/ppermute | solution.py:13
  14.1 14.7 %collective-permute-start.4 = (bf16[32,4096]{1,0:T(8,128)(2,1)S(1)}, bf16[32,4096]{1,0:T(8,128)(2,1)S(1)}, u32[]{:S(2)}, u32[]{:S(2)}) collective-permute-start(bf16[32,4096]{1,0:T(8,128)(2,1)S(1)} %pad_maximum_fusion.1), channel_id=1, source_target_pairs={{0,2},{1,3},{2,0},{3,1},{4,6},{5,7},{6,4},{7,5},{8,10},{9,11},{10,... | collective-permute-start | bytes 786440 | tf_op jit(solution)/shard_map/ppermute | solution.py:13
  28.8 6.4 %collective-permute-start.5 = (bf16[32,4096]{1,0:T(8,128)(2,1)S(1)}, bf16[32,4096]{1,0:T(8,128)(2,1)S(1)}, u32[]{:S(2)}, u32[]{:S(2)}) collective-permute-start(bf16[32,4096]{1,0:T(8,128)(2,1)S(1)} %collective-permute-done.4), channel_id=1, source_target_pairs={{0,1},{1,0},{2,3},{3,2},{4,5},{5,4},{6,7},{7,6},{8,9},{9,8},{10,11... | collective-permute-start | bytes 786440 | tf_op jit(solution)/shard_map/ppermute | solution.py:13
  35.2 1.0 %copy-start.1 = (bf16[128,4096]{1,0:T(8,128)(2,1)}, bf16[128,4096]{1,0:T(8,128)(2,1)S(1)}, u32[]{:S(2)}) copy-start(bf16[128,4096]{1,0:T(8,128)(2,1)S(1)} %constant_dynamic-update-slice_fusion) | copy-start | bytes 3145732
  42.2 40.5 %copy-start.3 = (s32[128,8]{0,1:T(8,128)S(1)}, s32[128,8]{0,1:T(8,128)}, u32[]{:S(2)}) copy-start(s32[128,8]{0,1:T(8,128)} %param.8) | copy-start | bytes 12292
  42.2 40.5 %copy-start.4 = (f32[128,8]{0,1:T(8,128)S(1)}, f32[128,8]{0,1:T(8,128)}, u32[]{:S(2)}) copy-start(f32[128,8]{0,1:T(8,128)} %param.9) | copy-start | bytes 12292
  42.2 40.5 %copy-start.6 = (s32[4]{0:T(128)S(1)}, s32[4]{0:T(128)}, u32[]{:S(2)}) copy-start(s32[4]{0:T(128)} %copy-done.5) | copy-start | bytes 52
  43.3 12.1 %collective-permute-start.7 = (bf16[32,4096]{1,0:T(8,128)(2,1)S(1)}, bf16[32,4096]{1,0:T(8,128)(2,1)S(1)}, u32[]{:S(2)}, u32[]{:S(2)}) collective-permute-start(bf16[32,4096]{1,0:T(8,128)(2,1)S(1)} %get-tuple-element.3), channel_id=1, source_target_pairs={{0,1},{1,0},{2,3},{3,2},{4,5},{5,4},{6,7},{7,6},{8,9},{9,8},{10,11... | collective-permute-start | bytes 786440 | tf_op jit(solution)/shard_map/ppermute | solution.py:13
  44.9 13.3 %collective-permute-start.6 = (bf16[32,4096]{1,0:T(8,128)(2,1)S(1)}, bf16[32,4096]{1,0:T(8,128)(2,1)S(1)}, u32[]{:S(2)}, u32[]{:S(2)}) collective-permute-start(bf16[32,4096]{1,0:T(8,128)(2,1)S(1)} %get-tuple-element.2), channel_id=1, source_target_pairs={{0,1},{1,0},{2,3},{3,2},{4,5},{5,4},{6,7},{7,6},{8,9},{9,8},{10,11... | collective-permute-start | bytes 786440 | tf_op jit(solution)/shard_map/ppermute | solution.py:13
  56.5 15.5 %collective-permute-start.8 = (bf16[32,4096]{1,0:T(8,128)(2,1)S(1)}, bf16[32,4096]{1,0:T(8,128)(2,1)S(1)}, u32[]{:S(2)}, u32[]{:S(2)}) collective-permute-start(bf16[32,4096]{1,0:T(8,128)(2,1)S(1)} %fusion.7), channel_id=1, source_target_pairs={{0,2},{1,3},{2,0},{3,1},{4,6},{5,7},{6,4},{7,5},{8,10},{9,11},{10,... | collective-permute-start | bytes 786440 | tf_op jit(solution)/shard_map/ppermute | solution.py:13
  73.2 9.5 %collective-permute-start.13 = (bf16[32,4096]{1,0:T(8,128)(2,1)S(1)}, bf16[32,4096]{1,0:T(8,128)(2,1)}, u32[]{:S(2)}, u32[]{:S(2)}) collective-permute-start(bf16[32,4096]{1,0:T(8,128)(2,1)S(1)} %fusion.9), channel_id=1, source_target_pairs={{0,2},{1,3},{2,0},{3,1},{4,6},{5,7},{6,4},{7,5},{8,10},{9,11},{10,... | collective-permute-start | bytes 786440 | tf_op jit(solution)/shard_map/ppermute | solution.py:13
  73.2 12.5 %collective-permute-start.12 = (bf16[32,4096]{1,0:T(8,128)(2,1)S(1)}, bf16[32,4096]{1,0:T(8,128)(2,1)}, u32[]{:S(2)}, u32[]{:S(2)}) collective-permute-start(bf16[32,4096]{1,0:T(8,128)(2,1)S(1)} %fusion.9), channel_id=1, source_target_pairs={{0,1},{1,0},{2,3},{3,2},{4,5},{5,4},{6,7},{7,6},{8,9},{9,8},{10,11... | collective-permute-start | bytes 786440 | tf_op jit(solution)/shard_map/ppermute | solution.py:13
  76.6 6.3 %collective-permute-start.10 = (bf16[8,4096]{1,0:T(8,128)(2,1)}, bf16[8,4096]{1,0:T(8,128)(2,1)S(1)}, u32[]{:S(2)}, u32[]{:S(2)}) collective-permute-start(bf16[8,4096]{1,0:T(8,128)(2,1)} %get-tuple-element.6), channel_id=1, source_target_pairs={{0,8},{4,12},{8,0},{12,4},{1,9},{5,13},{9,1},{13,5},{2,10},{6,14},... | collective-permute-start | bytes 196616 | tf_op jit(solution)/shard_map/ppermute | solution.py:13
  77.3 5.5 %collective-permute-start.11 = (bf16[8,4096]{1,0:T(8,128)(2,1)}, bf16[8,4096]{1,0:T(8,128)(2,1)}, u32[]{:S(2)}, u32[]{:S(2)}) collective-permute-start(bf16[8,4096]{1,0:T(8,128)(2,1)} %get-tuple-element.5), channel_id=1, source_target_pairs={{0,12},{4,8},{8,4},{12,0},{1,13},{5,9},{9,5},{13,1},{2,14},{6,10},... | collective-permute-start | bytes 196616 | tf_op jit(solution)/shard_map/ppermute | solution.py:13
  77.3 5.5 %collective-permute-start.9 = (bf16[8,4096]{1,0:T(8,128)(2,1)}, bf16[8,4096]{1,0:T(8,128)(2,1)}, u32[]{:S(2)}, u32[]{:S(2)}) collective-permute-start(bf16[8,4096]{1,0:T(8,128)(2,1)} %get-tuple-element.7), channel_id=1, source_target_pairs={{0,4},{4,0},{8,12},{12,8},{1,5},{5,1},{9,13},{13,9},{2,6},{6,2},{1... | collective-permute-start | bytes 196616 | tf_op jit(solution)/shard_map/ppermute | solution.py:13
  82.7 6.7 %collective-permute-start.14 = (bf16[32,4096]{1,0:T(8,128)(2,1)}, bf16[32,4096]{1,0:T(8,128)(2,1)}, u32[]{:S(2)}, u32[]{:S(2)}) collective-permute-start(bf16[32,4096]{1,0:T(8,128)(2,1)} %collective-permute-done.13), channel_id=1, source_target_pairs={{0,1},{1,0},{2,3},{3,2},{4,5},{5,4},{6,7},{7,6},{8,9},{9,8},{10,11... | collective-permute-start | bytes 786440 | tf_op jit(solution)/shard_map/ppermute | solution.py:13

commit v2 on v1

v2 whole, which is shorter than its diff:
```python
import functools

import jax
import jax.numpy as jnp
from jax import lax
from jax.experimental import pallas as pl
from jax.experimental.pallas import tpu as pltpu
from jax.sharding import PartitionSpec as P

EXPERTS_ALL = 128
TOPK = 8
CAP = 8
MIB = 1 << 20
VMEM = pl.BlockSpec(memory_space=pltpu.VMEM)
SMEM = pl.BlockSpec(memory_space=pltpu.SMEM)
HBM = pl.BlockSpec(memory_space=pltpu.HBM)


def in_hbm(x):
    return pltpu.with_memory_space_constraint(x, pltpu.HBM)


def swap(x, axis, k):
    n = lax.axis_size(axis)
    return lax.ppermute(x, axis, [(i, i ^ k) for i in range(n)])


def gather_blocks(own, axis):
    n = lax.axis_size(axis)
    held = {0: own}
    bit = n // 2
    while bit:
        for r in list(held):
            held[r ^ bit] = swap(held[r], axis, bit)
        bit //= 2
    return [held[r] for r in range(n)]


def reduce_blocks(blocks, axis):
    n = lax.axis_size(axis)
    held = dict(enumerate(blocks))
    bit = 1
    while bit < n:
        keep = [r for r in held if not r & bit]
        keep.sort(reverse=True)
        held = {
            r: held[r].astype(jnp.float32)
            + swap(held[r ^ bit].astype(jnp.bfloat16), axis, bit).astype(jnp.float32)
            for r in keep
        }
        bit *= 2
    return held[0]


def pack_kernel(count, place_ref, window_hbm, ids_hbm, weight_hbm, tokens_hbm, *refs):
    pieces, weighted_ref = refs[:count], refs[count]
    window_ref, ids_ref, weight_ref, tokens_ref, sems = refs[count + 1 :]
    tok_count, width = tokens_ref.shape
    step = 1024
    small = [
        pltpu.make_async_copy(source, target, sems.at[i])
        for i, (source, target) in enumerate(
            ((window_hbm, window_ref), (ids_hbm, ids_ref), (weight_hbm, weight_ref))
        )
    ]
    parts = [slice(start, start + step) for start in range(0, width, step)]
    large = [
        pltpu.make_async_copy(tokens_hbm.at[:, part], tokens_ref.at[:, part], sems.at[3 + i])
        for i, part in enumerate(parts)
    ]
    for copy in small + large:
        copy.start()
    for copy in small:
        copy.wait()
    ids = ids_ref[...]
    weights = weight_ref[...]
    routed, shares = [], []
    for k in range(count):
        match = ids == window_ref[place_ref[0] ^ k]
        routed.append(jnp.max(match.astype(jnp.float32), axis=0, keepdims=True))
        shares.append(jnp.sum(jnp.where(match, weights, 0.0), axis=0, keepdims=True))
    earlier = lax.broadcasted_iota(jnp.int32, (tok_count, tok_count), 0) < lax.broadcasted_iota(
        jnp.int32, (tok_count, tok_count), 1
    )
    ranks = jnp.dot(
        jnp.concatenate(routed, axis=0).astype(jnp.bfloat16),
        earlier.astype(jnp.bfloat16),
        preferred_element_type=jnp.float32,
    )
    slot = lax.broadcasted_iota(jnp.int32, (CAP, tok_count), 0).astype(jnp.float32)
    placing = [
        jnp.where(slot == ranks[k : k + 1], jnp.broadcast_to(routed[k], slot.shape), 0.0)
        for k in range(count)
    ]
    weighted = jnp.concatenate([placing[k] * shares[k] for k in range(count)], axis=0)
    high = weighted.astype(jnp.bfloat16)
    rest = weighted - high.astype(jnp.float32)
    middle = rest.astype(jnp.bfloat16)
    low = (rest - middle.astype(jnp.float32)).astype(jnp.bfloat16)
    weighted_ref[...] = jnp.concatenate([high, middle, low], axis=0)
    placed = jnp.concatenate(placing, axis=0).astype(jnp.bfloat16)
    for copy, part in zip(large, parts):
        copy.wait()
        rows = jnp.dot(
            placed, tokens_ref[:, part], preferred_element_type=jnp.float32
        ).astype(jnp.bfloat16)
        for k in range(count):
            pieces[k][:, part] = rows[k * CAP : (k + 1) * CAP]


def pack(place, window_ids, expert_ids, router_weight, tokens):
    count = window_ids.shape[0]
    tok_count, width = tokens.shape
    outs = pl.pallas_call(
        functools.partial(pack_kernel, count),
        out_shape=[jax.ShapeDtypeStruct((CAP, width), jnp.bfloat16)] * count
        + [jax.ShapeDtypeStruct((3 * count * CAP, tok_count), jnp.bfloat16)],
        in_specs=[SMEM] + [HBM] * 4,
        out_specs=[VMEM] * (count + 1),
        scratch_shapes=[
            pltpu.SMEM(window_ids.shape, window_ids.dtype),
            pltpu.VMEM(expert_ids.shape[::-1], expert_ids.dtype),
            pltpu.VMEM(router_weight.shape[::-1], router_weight.dtype),
            pltpu.VMEM(tokens.shape, tokens.dtype),
            pltpu.SemaphoreType.DMA((3 + width // 1024,)),
        ],
        compiler_params=pltpu.CompilerParams(vmem_limit_bytes=8 * MIB),
        cost_estimate=pl.CostEstimate(
            flops=2 * count * CAP * tok_count * width,
            bytes_accessed=2 * tok_count * width * 2,
            transcendentals=0,
        ),
    )(place, *[in_hbm(x) for x in (window_ids, expert_ids.T, router_weight.T, tokens)])
    return outs[:count], outs[count]


def load_kernel(count, *refs):
    sources, targets, sems = refs[:count], refs[-count - 1 : -1], refs[-1]
    copies = [
        pltpu.make_async_copy(source, target, sems.at[i])
        for i, (source, target) in enumerate(zip(sources, targets))
    ]
    for copy in copies:
        copy.start()
    for copy in copies:
        copy.wait()


def load(arrays, after):
    count = len(arrays)
    return pl.pallas_call(
        functools.partial(load_kernel, count),
        out_shape=[jax.ShapeDtypeStruct(x.shape, x.dtype) for x in arrays],
        in_specs=[HBM] * count + [pl.BlockSpec(memory_space=pl.ANY)],
        out_specs=[VMEM] * count,
        scratch_shapes=[pltpu.SemaphoreType.DMA((count,))],
        compiler_params=pltpu.CompilerParams(vmem_limit_bytes=16 * MIB),
        cost_estimate=pl.CostEstimate(
            flops=0,
            bytes_accessed=sum(2 * x.size * x.dtype.itemsize for x in arrays),
            transcendentals=0,
        ),
    )(*[in_hbm(x) for x in arrays], after)


def expert_kernel(count, *refs):
    rows = refs[:count]
    gate_ref, up_ref, down_ref = refs[count : count + 3]
    outs = refs[-count:]
    width = gate_ref.shape[1]
    own = rows[0].shape[0]
    step = 1024
    gate = up = 0.0
    for start in range(0, width, step):
        part = slice(start, start + step)
        x = jnp.concatenate([r[:, part] for r in rows], axis=0)
        gate += jnp.dot(x, gate_ref[0, part, :], preferred_element_type=jnp.float32)
        up += jnp.dot(x, up_ref[0, part, :], preferred_element_type=jnp.float32)
    hidden = (gate / (1.0 + jnp.exp(-gate)) * up).astype(jnp.bfloat16)
    for start in range(0, width, step):
        part = slice(start, start + step)
        y = jnp.dot(hidden, down_ref[0, :, part], preferred_element_type=jnp.float32)
        for r in range(count):
            outs[r][:, part] = y[r * own : (r + 1) * own].astype(outs[r].dtype)


def expert(rows, gate_weight, up_weight, down_weight, after):
    count = len(rows)
    own, width = rows[0].shape
    hidden = gate_weight.shape[2]
    extra = [] if after is None else [after]
    return pl.pallas_call(
        functools.partial(expert_kernel, count),
        out_shape=[
            jax.ShapeDtypeStruct((own, width), jnp.bfloat16 if r & 1 else jnp.float32)
            for r in range(count)
        ],
        in_specs=[VMEM] * (count + 3) + [pl.BlockSpec(memory_space=pl.ANY)] * len(extra),
        out_specs=[VMEM] * count,
        compiler_params=pltpu.CompilerParams(vmem_limit_bytes=24 * MIB),
        cost_estimate=pl.CostEstimate(
            flops=4 * count * own * width * hidden * 3,
            bytes_accessed=3 * width * hidden * 2 + count * own * width * 6,
            transcendentals=count * own * hidden,
        ),
    )(*rows, gate_weight, up_weight, down_weight, *extra)


def combine_kernel(count, *refs):
    rows, weighted_ref, out_ref = refs[:count], refs[count], refs[count + 1]
    weighted = weighted_ref[...]
    width = out_ref.shape[1]
    step = 1024
    for start in range(0, width, step):
        part = slice(start, start + step)
        x = jnp.concatenate([r[:, part] for r in rows], axis=0)
        out_ref[:, part] = lax.dot_general(
            weighted,
            jnp.concatenate([x, x, x], axis=0),
            (((0,), (0,)), ((), ())),
            preferred_element_type=jnp.float32,
        ).astype(out_ref.dtype)


def combine(rows, weighted):
    count = len(rows)
    width = rows[0].shape[1]
    tok_count = weighted.shape[1]
    return pl.pallas_call(
        functools.partial(combine_kernel, count),
        out_shape=jax.ShapeDtypeStruct((tok_count, width), jnp.bfloat16),
        in_specs=[VMEM] * (count + 1),
        out_specs=VMEM,
        compiler_params=pltpu.CompilerParams(vmem_limit_bytes=8 * MIB),
        cost_estimate=pl.CostEstimate(
            flops=2 * weighted.shape[0] * tok_count * width,
            bytes_accessed=2 * tok_count * width * 2,
            transcendentals=0,
        ),
    )(*rows, weighted)


def gram_kernel(count, scaling, place_ref, *refs):
    blocks, out_ref, all_ref, own_ref = refs[:count], refs[count], refs[count + 1], refs[count + 2]
    own = blocks[0].shape[0]
    step = pl.program_id(0)

    @pl.when(step == 0)
    def _():
        for r in range(count):
            all_ref[r * own : (r + 1) * own, :] = blocks[r][...]
        width = own_ref.shape[1]
        own_ref[...] = all_ref[:, pl.ds(pl.multiple_of(place_ref[0] * width, width), width)]

    height = out_ref.shape[1]
    left = all_ref[:, pl.ds(pl.multiple_of(step * height, height), height)]
    out_ref[0] = (
        lax.dot_general(
            left, own_ref[...], (((0,), (0,)), ((), ())), preferred_element_type=jnp.float32
        )
        * scaling
    ).astype(out_ref.dtype)


def gram(place, blocks, col_width, scaling):
    count = len(blocks)
    own, width = blocks[0].shape
    height = 512
    return pl.pallas_call(
        functools.partial(gram_kernel, count, scaling),
        out_shape=jax.ShapeDtypeStruct((1, width, col_width), jnp.bfloat16),
        grid=(width // height,),
        in_specs=[SMEM] + [VMEM] * count,
        out_specs=pl.BlockSpec((1, height, col_width), lambda i: (0, i, 0)),
        scratch_shapes=[
            pltpu.VMEM((count * own, width), jnp.bfloat16),
            pltpu.VMEM((count * own, col_width), jnp.bfloat16),
        ],
        compiler_params=pltpu.CompilerParams(vmem_limit_bytes=32 * MIB),
        cost_estimate=pl.CostEstimate(
            flops=2 * count * own * width * col_width,
            bytes_accessed=width * col_width * 2 + 2 * count * own * width,
            transcendentals=0,
        ),
    )(place, *blocks)


def local(tokens, expert_ids, router_weight, window_ids, gate_weight, up_weight, down_weight):
    tok_count, feat_width = tokens.shape
    owner_count = lax.axis_size("exp")
    shard_count = lax.axis_size("dp")
    exp_place = lax.axis_index("exp").astype(jnp.int32)[None]
    dp_place = lax.axis_index("dp").astype(jnp.int32)[None]
    pieces, weighted = pack(exp_place, window_ids, expert_ids, router_weight, tokens)
    half = owner_count // 2
    gate_weight, up_weight, down_weight = load(
        (gate_weight, up_weight, down_weight), weighted
    )
    pieces = [swap(piece, "exp", k) if k else piece for k, piece in enumerate(pieces)]
    returned = []
    gram_rows = []
    after = None
    for start in range(0, owner_count, half):
        own_rows = jnp.concatenate(pieces[start : start + half], axis=0)
        rows = gather_blocks(own_rows, "dp")
        terms = expert(rows, gate_weight, up_weight, down_weight, after)
        after = terms[0]
        expert_out = reduce_blocks(terms, "dp").astype(jnp.bfloat16)
        gram_rows += gather_blocks(expert_out, "dp")
        for k in range(half):
            piece = expert_out[k * CAP : (k + 1) * CAP]
            returned.append(swap(piece, "exp", start + k) if start + k else piece)
    scaling = EXPERTS_ALL / (TOPK * tok_count * owner_count * shard_count)
    gram_out = gram(dp_place, gram_rows, feat_width // shard_count, scaling)
    combined = combine(returned, weighted)
    return (combined, gram_out)


def solution(mesh):
    in_specs = (
        P(("grp", "exp", "dp"), None),
        P(("grp", "exp", "dp"), None),
        P(("grp", "exp", "dp"), None),
        P("grp"),
        P(("grp", "exp"), None, "dp"),
        P(("grp", "exp"), None, "dp"),
        P(("grp", "exp"), "dp", None),
    )
    out_specs = (P(("grp", "exp", "dp"), None), P(("grp", "exp"), None, "dp"))
    return jax.shard_map(local, mesh=mesh, in_specs=in_specs, out_specs=out_specs, check_vma=False)
```

time: 96.7 us -> 78.9 us (0.82)
  waiting for transfers between devices: 54 us -> 32.5 us
  Pallas kernels: 0 us -> 17 us
  matrix products: 16.4 us -> 0 us
  starting transfers between devices: 15.9 us -> 28.3 us
  other arithmetic: 5.48 us -> 0.14 us
  local copies, waits for them, and re-layouts: 3.77 us -> 0.04 us
    ppermute x15 -> x24, waiting for transfers between devices: 54 us -> 32.5 us  [swap(): return lax.ppermute(x, axis, [(i, i ^ k) for i in range(n)])]
    pallas_call x0 -> x6, Pallas kernels: none -> 17 us  [the longest x1 6.29 us: gram(): pl.pallas_call(functools.partial(gram_kernel, count, scaling), out_shape=...]
    dot_general x5 -> x0, matrix products: 16.4 us -> none  [the longest x1 5.77 us: local(): lax.dot_general(row_block, column_block, (((0,), (0,)), ((), ())), prefer...]
    ppermute x15 -> x24, starting transfers between devices: 15.9 us -> 28.3 us  [swap(): return lax.ppermute(x, axis, [(i, i ^ k) for i in range(n)])]
    slice x3 -> x2, local copies, waits for them, and re-layouts: 1.78 us -> 0.02 us  [local(): piece = expert_out[k * CAP:(k + 1) * CAP]]
    unnamed x19 -> x2, local copies, waits for them, and re-layouts: 1.59 us -> 0.01 us
    concatenate x2 -> x0, other arithmetic: 1.19 us -> none  [the longest x1 1.18 us: local(): row_block = jnp.concatenate(gather_blocks(expert_out, 'dp'), axis=0)]
    reduce_sum x2 -> x0, other arithmetic: 1.08 us -> none  [the longest x1 0.99 us: local(): jnp.sum(jnp.where(slots[:, None] == jnp.arange(window_size, dtype=jnp.int...]
  transfers between devices with their start and end apart: 15 -> 24, of which waited for: 9 -> 12; matrix products, arithmetic and copies ran while one was open for 5% -> 0% of each run, Pallas kernels for 0% -> 11%
where the time goes in v2:
time: 78.9 us; the launch traced here: 78.7 us
  waiting for transfers between devices  32.5 us (41%)
  starting transfers between devices  28.3 us (36%)
  Pallas kernels  17 us (22%)
    ppermute x24, waiting for transfers between devices, swap(): return lax.ppermute(x, axis, [(i, i ^ k) for i in range(n)])  32.5 us
    ppermute x24, starting transfers between devices, swap(): return lax.ppermute(x, axis, [(i, i ^ k) for i in range(n)])  28.3 us
    pallas_call x1, Pallas kernels, gram(): pl.pallas_call(functools.partial(gram_kernel, count, scaling), out_shape=...  6.29 us
    pallas_call x1, Pallas kernels, load(): pl.pallas_call(functools.partial(load_kernel, count), out_shape=[jax.Shap...  3.78 us
    pallas_call x2, Pallas kernels, expert(): pl.pallas_call(functools.partial(expert_kernel, count), out_shape=[jax.Sh...  3.72 us
    pallas_call x1, Pallas kernels, pack(): pl.pallas_call(functools.partial(pack_kernel, count), out_shape=[jax.Shap...  1.73 us
  transfers between devices with their start and end apart: 24, of which 12 were waited for; matrix products, arithmetic and copies ran while one was open for 0% of the time, Pallas kernels for 11%

profile of v2, /device:TPU:0, one launch (start us, length us, event | category | flops | bytes accessed | tf_op | source)
XLA Modules:
  0.0 78.7 jit_solution(4163869638699422363)
XLA Ops:
  0.6 1.7 %shard_map.86 = (bf16[8,4096]{1,0:T(8,128)(2,1)S(1)}, bf16[8,4096]{1,0:T(8,128)(2,1)S(1)}, bf16[8,4096]{1,0:T(8,128)(2,1)S(1)}, bf16[8,4096]{1,0:T(8,128)(2,1)S(1)}, bf16[96,128]{1,0:T(8,128)(2,1)S(1)}) custom-call(s32[1]{0:T(128)} %bitcast.place_ref, s32[4]{0:T(128)} %window_hbm.1, s32[8,128]{1,0:T(8,128)} %bitcast.4, f32[8,128]{1,0:T(8,128)} %bitcast.5, ...), custom_call_target="tpu_custom_call" | custom-call | flops 33554432 | bytes 2097152 | tf_op jit(solution)/shard_map/pallas_call | solution.py:114
  2.9 2.6 %collective-permute-start.8 = (bf16[8,4096]{1,0:T(8,128)(2,1)S(1)}, bf16[8,4096]{1,0:T(8,128)(2,1)S(1)}, u32[]{:S(2)}, u32[]{:S(2)}) collective-permute-start(bf16[8,4096]{1,0:T(8,128)(2,1)S(1)} %get-tuple-element.28), channel_id=1, source_target_pairs={{0,8},{4,12},{8,0},{12,4},{1,9},{5,13},{9,1},{13,5},{2,10},{6,14},... | collective-permute-start | bytes 196616 | tf_op jit(solution)/shard_map/ppermute | solution.py:25
  5.6 2.9 %collective-permute-start.2 = (bf16[16,4096]{1,0:T(8,128)(2,1)S(1)}, bf16[16,4096]{1,0:T(8,128)(2,1)S(1)}, u32[]{:S(2)}, u32[]{:S(2)}) collective-permute-start(bf16[16,4096]{1,0:T(8,128)(2,1)S(1)} %constant_dynamic-update-slice_fusion.refs_0_), channel_id=1, source_target_pairs={{0,2},{1,3},{2,0},{3,1},{4,6},{5,7},{6,4},{7,5},{8,10},{9,11},{10,... | collective-permute-start | bytes 393224 | tf_op jit(solution)/shard_map/ppermute | solution.py:25
  9.5 2.6 %collective-permute-start.11 = (bf16[16,4096]{1,0:T(8,128)(2,1)S(1)}, bf16[16,4096]{1,0:T(8,128)(2,1)S(1)}, u32[]{:S(2)}, u32[]{:S(2)}) collective-permute-start(bf16[16,4096]{1,0:T(8,128)(2,1)S(1)} %constant_dynamic-update-slice_fusion.2.refs_0_), channel_id=1, source_target_pairs={{0,2},{1,3},{2,0},{3,1},{4,6},{5,7},{6,4},{7,5},{8,10},{9,11},{10,... | collective-permute-start | bytes 393224 | tf_op jit(solution)/shard_map/ppermute | solution.py:25
  12.1 1.6 %collective-permute-start.1 = (bf16[16,4096]{1,0:T(8,128)(2,1)S(1)}, bf16[16,4096]{1,0:T(8,128)(2,1)S(1)}, u32[]{:S(2)}, u32[]{:S(2)}) collective-permute-start(bf16[16,4096]{1,0:T(8,128)(2,1)S(1)} %constant_dynamic-update-slice_fusion.refs_0_), channel_id=1, source_target_pairs={{0,1},{1,0},{2,3},{3,2},{4,5},{5,4},{6,7},{7,6},{8,9},{9,8},{10,11... | collective-permute-start | bytes 393224 | tf_op jit(solution)/shard_map/ppermute | solution.py:25
  13.7 4.9 %collective-permute-done.2.refs_2_ = bf16[16,4096]{1,0:T(8,128)(2,1)S(1)} collective-permute-done((bf16[16,4096]{1,0:T(8,128)(2,1)S(1)}, bf16[16,4096]{1,0:T(8,128)(2,1)S(1)}, u32[]{:S(2)}, u32[]{:S(2)}) %collective-permute-start.2) | collective-permute-done | bytes 131104 | tf_op jit(solution)/shard_map/ppermute | solution.py:25
  18.8 3.8 %shard_map.87 = (bf16[1,4096,384]{2,1,0:T(8,128)(2,1)S(1)}, bf16[1,4096,384]{2,1,0:T(8,128)(2,1)S(1)}, bf16[1,384,4096]{2,1,0:T(8,128)(2,1)S(1)}) custom-call(bf16[1,4096,384]{2,1,0:T(8,128)(2,1)} %refs_0_.1, bf16[1,4096,384]{2,1,0:T(8,128)(2,1)} %refs_1_.1, bf16[1,384,4096]{2,1,0:T(8,128)(2,1)} %refs_2_.1, bf16[96,128]{1,0:T(8,128)(2,1)S(1)} %get-tuple-element.20.refs_3_.refs_4_), custom_call_target="tpu_custom_call" | custom-call | bytes 18874368 | tf_op jit(solution)/shard_map/pallas_call | solution.py:151
  22.6 1.8 %collective-permute-start.10 = (bf16[16,4096]{1,0:T(8,128)(2,1)S(1)}, bf16[16,4096]{1,0:T(8,128)(2,1)S(1)}, u32[]{:S(2)}, u32[]{:S(2)}) collective-permute-start(bf16[16,4096]{1,0:T(8,128)(2,1)S(1)} %constant_dynamic-update-slice_fusion.2.refs_0_), channel_id=1, source_target_pairs={{0,1},{1,0},{2,3},{3,2},{4,5},{5,4},{6,7},{7,6},{8,9},{9,8},{10,11... | collective-permute-start | bytes 393224 | tf_op jit(solution)/shard_map/ppermute | solution.py:25
  24.7 1.9 %shard_map.88 = (f32[16,4096]{1,0:T(8,128)S(1)}, bf16[16,4096]{1,0:T(8,128)(2,1)S(1)}, f32[16,4096]{1,0:T(8,128)S(1)}, bf16[16,4096]{1,0:T(8,128)(2,1)S(1)}) custom-call(bf16[16,4096]{1,0:T(8,128)(2,1)S(1)} %constant_dynamic-update-slice_fusion.refs_0_, bf16[16,4096]{1,0:T(8,128)(2,1)S(1)} %collective-permute-done.1.refs_1_, ...), custom_call_target="tpu_custom_call" | custom-call | flops 1207959552 | bytes 11010048 | tf_op jit(solution)/shard_map/pallas_call | solution.py:192
  26.6 1.8 %collective-permute-start.5 = (bf16[16,4096]{1,0:T(8,128)(2,1)S(1)}, bf16[16,4096]{1,0:T(8,128)(2,1)S(1)}, u32[]{:S(2)}, u32[]{:S(2)}) collective-permute-start(bf16[16,4096]{1,0:T(8,128)(2,1)S(1)} %get-tuple-element.27), channel_id=1, source_target_pairs={{0,1},{1,0},{2,3},{3,2},{4,5},{5,4},{6,7},{7,6},{8,9},{9,8},{10,11... | collective-permute-start | bytes 393224 | tf_op jit(solution)/shard_map/ppermute | solution.py:25
  29.1 2.8 %collective-permute-done.12.refs_3_ = bf16[16,4096]{1,0:T(8,128)(2,1)S(1)} collective-permute-done((bf16[16,4096]{1,0:T(8,128)(2,1)S(1)}, bf16[16,4096]{1,0:T(8,128)(2,1)S(1)}, u32[]{:S(2)}, u32[]{:S(2)}) %collective-permute-start.12) | collective-permute-done | bytes 131104 | tf_op jit(solution)/shard_map/ppermute | solution.py:25
  31.9 1.9 %shard_map.89 = (f32[16,4096]{1,0:T(8,128)S(1)}, bf16[16,4096]{1,0:T(8,128)(2,1)S(1)}, f32[16,4096]{1,0:T(8,128)S(1)}, bf16[16,4096]{1,0:T(8,128)(2,1)S(1)}) custom-call(bf16[16,4096]{1,0:T(8,128)(2,1)S(1)} %constant_dynamic-update-slice_fusion.2.refs_0_, bf16[16,4096]{1,0:T(8,128)(2,1)S(1)} %collective-permute-done.10.refs_1_, ...), custom_call_target="tpu_custom_call" | custom-call | flops 1207959552 | bytes 11010048 | tf_op jit(solution)/shard_map/pallas_call | solution.py:192
  33.8 1.8 %collective-permute-start.14 = (bf16[16,4096]{1,0:T(8,128)(2,1)S(1)}, bf16[16,4096]{1,0:T(8,128)(2,1)S(1)}, u32[]{:S(2)}, u32[]{:S(2)}) collective-permute-start(bf16[16,4096]{1,0:T(8,128)(2,1)S(1)} %get-tuple-element.33), channel_id=1, source_target_pairs={{0,1},{1,0},{2,3},{3,2},{4,5},{5,4},{6,7},{7,6},{8,9},{9,8},{10,11... | collective-permute-start | bytes 393224 | tf_op jit(solution)/shard_map/ppermute | solution.py:25
  35.9 3.4 %collective-permute-start.6 = (bf16[16,4096]{1,0:T(8,128)(2,1)S(1)}, bf16[16,4096]{1,0:T(8,128)(2,1)S(1)}, u32[]{:S(2)}, u32[]{:S(2)}) collective-permute-start(bf16[16,4096]{1,0:T(8,128)(2,1)S(1)} %add_convert_fusion.3), channel_id=1, source_target_pairs={{0,2},{1,3},{2,0},{3,1},{4,6},{5,7},{6,4},{7,5},{8,10},{9,11},{10,... | collective-permute-start | bytes 393224 | tf_op jit(solution)/shard_map/ppermute | solution.py:25
  39.3 4.6 %collective-permute-done.14 = bf16[16,4096]{1,0:T(8,128)(2,1)S(1)} collective-permute-done((bf16[16,4096]{1,0:T(8,128)(2,1)S(1)}, bf16[16,4096]{1,0:T(8,128)(2,1)S(1)}, u32[]{:S(2)}, u32[]{:S(2)}) %collective-permute-start.14) | collective-permute-done | bytes 131104 | tf_op jit(solution)/shard_map/ppermute | solution.py:25
  44.6 3.5 %collective-permute-start.19 = (bf16[16,4096]{1,0:T(8,128)(2,1)S(1)}, bf16[16,4096]{1,0:T(8,128)(2,1)S(1)}, u32[]{:S(2)}, u32[]{:S(2)}) collective-permute-start(bf16[16,4096]{1,0:T(8,128)(2,1)S(1)} %add_convert_fusion.2.refs_0_), channel_id=1, source_target_pairs={{0,2},{1,3},{2,0},{3,1},{4,6},{5,7},{6,4},{7,5},{8,10},{9,11},{10,... | collective-permute-start | bytes 393224 | tf_op jit(solution)/shard_map/ppermute | solution.py:25
  48.1 8.0 %collective-permute-done.15 = bf16[16,4096]{1,0:T(8,128)(2,1)S(1)} collective-permute-done((bf16[16,4096]{1,0:T(8,128)(2,1)S(1)}, bf16[16,4096]{1,0:T(8,128)(2,1)S(1)}, u32[]{:S(2)}, u32[]{:S(2)}) %collective-permute-start.15) | collective-permute-done | bytes 131104 | tf_op jit(solution)/shard_map/ppermute | solution.py:25
  56.2 1.6 %collective-permute-start.16 = (bf16[8,4096]{1,0:T(8,128)(2,1)S(1)}, bf16[8,4096]{1,0:T(8,128)(2,1)S(1)}, u32[]{:S(2)}, u32[]{:S(2)}) collective-permute-start(bf16[8,4096]{1,0:T(8,128)(2,1)S(1)} %get-tuple-element.35), channel_id=1, source_target_pairs={{0,8},{4,12},{8,0},{12,4},{1,9},{5,13},{9,1},{13,5},{2,10},{6,14},... | collective-permute-start | bytes 196616 | tf_op jit(solution)/shard_map/ppermute | solution.py:25
  57.8 1.6 %collective-permute-start.18 = (bf16[16,4096]{1,0:T(8,128)(2,1)S(1)}, bf16[16,4096]{1,0:T(8,128)(2,1)S(1)}, u32[]{:S(2)}, u32[]{:S(2)}) collective-permute-start(bf16[16,4096]{1,0:T(8,128)(2,1)S(1)} %add_convert_fusion.2.refs_0_), channel_id=1, source_target_pairs={{0,1},{1,0},{2,3},{3,2},{4,5},{5,4},{6,7},{7,6},{8,9},{9,8},{10,11... | collective-permute-start | bytes 393224 | tf_op jit(solution)/shard_map/ppermute | solution.py:25
  62.7 4.3 %collective-permute-done.17.refs_3_ = bf16[8,4096]{1,0:T(8,128)(2,1)S(1)} collective-permute-done((bf16[8,4096]{1,0:T(8,128)(2,1)S(1)}, bf16[8,4096]{1,0:T(8,128)(2,1)S(1)}, u32[]{:S(2)}, u32[]{:S(2)}) %collective-permute-start.17) | collective-permute-done | bytes 65568 | tf_op jit(solution)/shard_map/ppermute | solution.py:25
  67.0 1.4 %shard_map.90 = bf16[128,4096]{1,0:T(8,128)(2,1)} custom-call(bf16[8,4096]{1,0:T(8,128)(2,1)S(1)} %get-tuple-element.37.refs_0_, bf16[8,4096]{1,0:T(8,128)(2,1)S(1)} %collective-permute-done.7.refs_1_, bf16[8,4096]{1,0:T(8,128)(2,1)S(1)} %collective-permute-done.16.refs_2_, bf16[8,4096]{1,0:T(8,128)(2,1)S(1)} %collective-permute-done.17.refs_3_, ...), custom_call_target="tpu_custom_call" | custom-call | flops 100663296 | bytes 2097152 | tf_op jit(solution)/shard_map/pallas_call | solution.py:229
  68.4 2.5 %collective-permute-done.20.refs_3_ = bf16[16,4096]{1,0:T(8,128)(2,1)S(1)} collective-permute-done((bf16[16,4096]{1,0:T(8,128)(2,1)S(1)}, bf16[16,4096]{1,0:T(8,128)(2,1)S(1)}, u32[]{:S(2)}, u32[]{:S(2)}) %collective-permute-start.20) | collective-permute-done | bytes 131104 | tf_op jit(solution)/shard_map/ppermute | solution.py:25
  70.9 1.5 %collective-permute-done.23.refs_7_ = bf16[16,4096]{1,0:T(8,128)(2,1)S(1)} collective-permute-done((bf16[16,4096]{1,0:T(8,128)(2,1)S(1)}, bf16[16,4096]{1,0:T(8,128)(2,1)S(1)}, u32[]{:S(2)}, u32[]{:S(2)}) %collective-permute-start.23) | collective-permute-done | bytes 131104 | tf_op jit(solution)/shard_map/ppermute | solution.py:25
  72.4 6.3 %shard_map.91 = bf16[1,4096,1024]{2,1,0:T(8,128)(2,1)} custom-call(s32[1]{0:T(128)} %bitcast.3.place_ref, bf16[16,4096]{1,0:T(8,128)(2,1)S(1)} %add_convert_fusion.2.refs_0_, bf16[16,4096]{1,0:T(8,128)(2,1)S(1)} %collective-permute-done.18.refs_1_, bf16[16,4096]{1,0:T(8,128)(2,1)S(1)} %collective-permute-done.19.refs_2_, ...), custom_call_target="tpu_custom_call" | custom-call | flops 1073741824 | bytes 9437184 | tf_op jit(solution)/shard_map/pallas_call | solution.py:269
  (40 shorter events, 7.3 us)
Async XLA Ops:
  2.4 3.2 %collective-permute-start = (bf16[8,4096]{1,0:T(8,128)(2,1)S(1)}, bf16[8,4096]{1,0:T(8,128)(2,1)S(1)}, u32[]{:S(2)}, u32[]{:S(2)}) collective-permute-start(bf16[8,4096]{1,0:T(8,128)(2,1)S(1)} %get-tuple-element.19), channel_id=1, source_target_pairs={{0,4},{4,0},{8,12},{12,8},{1,5},{5,1},{9,13},{13,9},{2,6},{6,2},{1... | collective-permute-start | bytes 196616 | tf_op jit(solution)/shard_map/ppermute | solution.py:25
  2.9 5.6 %collective-permute-start.8 = (bf16[8,4096]{1,0:T(8,128)(2,1)S(1)}, bf16[8,4096]{1,0:T(8,128)(2,1)S(1)}, u32[]{:S(2)}, u32[]{:S(2)}) collective-permute-start(bf16[8,4096]{1,0:T(8,128)(2,1)S(1)} %get-tuple-element.28), channel_id=1, source_target_pairs={{0,8},{4,12},{8,0},{12,4},{1,9},{5,13},{9,1},{13,5},{2,10},{6,14},... | collective-permute-start | bytes 196616 | tf_op jit(solution)/shard_map/ppermute | solution.py:25
  5.5 4.0 %collective-permute-start.9 = (bf16[8,4096]{1,0:T(8,128)(2,1)S(1)}, bf16[8,4096]{1,0:T(8,128)(2,1)S(1)}, u32[]{:S(2)}, u32[]{:S(2)}) collective-permute-start(bf16[8,4096]{1,0:T(8,128)(2,1)S(1)} %get-tuple-element.29), channel_id=1, source_target_pairs={{0,12},{4,8},{8,4},{12,0},{1,13},{5,9},{9,5},{13,1},{2,14},{6,10},... | collective-permute-start | bytes 196616 | tf_op jit(solution)/shard_map/ppermute | solution.py:25
  5.6 13.0 %collective-permute-start.2 = (bf16[16,4096]{1,0:T(8,128)(2,1)S(1)}, bf16[16,4096]{1,0:T(8,128)(2,1)S(1)}, u32[]{:S(2)}, u32[]{:S(2)}) collective-permute-start(bf16[16,4096]{1,0:T(8,128)(2,1)S(1)} %constant_dynamic-update-slice_fusion.refs_0_), channel_id=1, source_target_pairs={{0,2},{1,3},{2,0},{3,1},{4,6},{5,7},{6,4},{7,5},{8,10},{9,11},{10,... | collective-permute-start | bytes 393224 | tf_op jit(solution)/shard_map/ppermute | solution.py:25
  9.5 14.9 %collective-permute-start.11 = (bf16[16,4096]{1,0:T(8,128)(2,1)S(1)}, bf16[16,4096]{1,0:T(8,128)(2,1)S(1)}, u32[]{:S(2)}, u32[]{:S(2)}) collective-permute-start(bf16[16,4096]{1,0:T(8,128)(2,1)S(1)} %constant_dynamic-update-slice_fusion.2.refs_0_), channel_id=1, source_target_pairs={{0,2},{1,3},{2,0},{3,1},{4,6},{5,7},{6,4},{7,5},{8,10},{9,11},{10,... | collective-permute-start | bytes 393224 | tf_op jit(solution)/shard_map/ppermute | solution.py:25
  12.1 12.6 %collective-permute-start.1 = (bf16[16,4096]{1,0:T(8,128)(2,1)S(1)}, bf16[16,4096]{1,0:T(8,128)(2,1)S(1)}, u32[]{:S(2)}, u32[]{:S(2)}) collective-permute-start(bf16[16,4096]{1,0:T(8,128)(2,1)S(1)} %constant_dynamic-update-slice_fusion.refs_0_), channel_id=1, source_target_pairs={{0,1},{1,0},{2,3},{3,2},{4,5},{5,4},{6,7},{7,6},{8,9},{9,8},{10,11... | collective-permute-start | bytes 393224 | tf_op jit(solution)/shard_map/ppermute | solution.py:25
  18.6 6.2 %collective-permute-start.3 = (bf16[16,4096]{1,0:T(8,128)(2,1)S(1)}, bf16[16,4096]{1,0:T(8,128)(2,1)S(1)}, u32[]{:S(2)}, u32[]{:S(2)}) collective-permute-start(bf16[16,4096]{1,0:T(8,128)(2,1)S(1)} %collective-permute-done.2.refs_2_), channel_id=1, source_target_pairs={{0,1},{1,0},{2,3},{3,2},{4,5},{5,4},{6,7},{7,6},{8,9},{9,8},{10,11... | collective-permute-start | bytes 393224 | tf_op jit(solution)/shard_map/ppermute | solution.py:25
  22.6 6.5 %collective-permute-start.10 = (bf16[16,4096]{1,0:T(8,128)(2,1)S(1)}, bf16[16,4096]{1,0:T(8,128)(2,1)S(1)}, u32[]{:S(2)}, u32[]{:S(2)}) collective-permute-start(bf16[16,4096]{1,0:T(8,128)(2,1)S(1)} %constant_dynamic-update-slice_fusion.2.refs_0_), channel_id=1, source_target_pairs={{0,1},{1,0},{2,3},{3,2},{4,5},{5,4},{6,7},{7,6},{8,9},{9,8},{10,11... | collective-permute-start | bytes 393224 | tf_op jit(solution)/shard_map/ppermute | solution.py:25
  24.4 7.5 %collective-permute-start.12 = (bf16[16,4096]{1,0:T(8,128)(2,1)S(1)}, bf16[16,4096]{1,0:T(8,128)(2,1)S(1)}, u32[]{:S(2)}, u32[]{:S(2)}) collective-permute-start(bf16[16,4096]{1,0:T(8,128)(2,1)S(1)} %collective-permute-done.11.refs_2_), channel_id=1, source_target_pairs={{0,1},{1,0},{2,3},{3,2},{4,5},{5,4},{6,7},{7,6},{8,9},{9,8},{10,11... | collective-permute-start | bytes 393224 | tf_op jit(solution)/shard_map/ppermute | solution.py:25
  26.6 9.3 %collective-permute-start.5 = (bf16[16,4096]{1,0:T(8,128)(2,1)S(1)}, bf16[16,4096]{1,0:T(8,128)(2,1)S(1)}, u32[]{:S(2)}, u32[]{:S(2)}) collective-permute-start(bf16[16,4096]{1,0:T(8,128)(2,1)S(1)} %get-tuple-element.27), channel_id=1, source_target_pairs={{0,1},{1,0},{2,3},{3,2},{4,5},{5,4},{6,7},{7,6},{8,9},{9,8},{10,11... | collective-permute-start | bytes 393224 | tf_op jit(solution)/shard_map/ppermute | solution.py:25
  28.4 15.6 %collective-permute-start.4 = (bf16[16,4096]{1,0:T(8,128)(2,1)S(1)}, bf16[16,4096]{1,0:T(8,128)(2,1)S(1)}, u32[]{:S(2)}, u32[]{:S(2)}) collective-permute-start(bf16[16,4096]{1,0:T(8,128)(2,1)S(1)} %get-tuple-element.25), channel_id=1, source_target_pairs={{0,1},{1,0},{2,3},{3,2},{4,5},{5,4},{6,7},{7,6},{8,9},{9,8},{10,11... | collective-permute-start | bytes 393224 | tf_op jit(solution)/shard_map/ppermute | solution.py:25
  33.8 10.2 %collective-permute-start.14 = (bf16[16,4096]{1,0:T(8,128)(2,1)S(1)}, bf16[16,4096]{1,0:T(8,128)(2,1)S(1)}, u32[]{:S(2)}, u32[]{:S(2)}) collective-permute-start(bf16[16,4096]{1,0:T(8,128)(2,1)S(1)} %get-tuple-element.33), channel_id=1, source_target_pairs={{0,1},{1,0},{2,3},{3,2},{4,5},{5,4},{6,7},{7,6},{8,9},{9,8},{10,11... | collective-permute-start | bytes 393224 | tf_op jit(solution)/shard_map/ppermute | solution.py:25
  35.5 12.5 %collective-permute-start.13 = (bf16[16,4096]{1,0:T(8,128)(2,1)S(1)}, bf16[16,4096]{1,0:T(8,128)(2,1)S(1)}, u32[]{:S(2)}, u32[]{:S(2)}) collective-permute-start(bf16[16,4096]{1,0:T(8,128)(2,1)S(1)} %get-tuple-element.31), channel_id=1, source_target_pairs={{0,1},{1,0},{2,3},{3,2},{4,5},{5,4},{6,7},{7,6},{8,9},{9,8},{10,11... | collective-permute-start | bytes 393224 | tf_op jit(solution)/shard_map/ppermute | solution.py:25
  35.9 8.6 %collective-permute-start.6 = (bf16[16,4096]{1,0:T(8,128)(2,1)S(1)}, bf16[16,4096]{1,0:T(8,128)(2,1)S(1)}, u32[]{:S(2)}, u32[]{:S(2)}) collective-permute-start(bf16[16,4096]{1,0:T(8,128)(2,1)S(1)} %add_convert_fusion.3), channel_id=1, source_target_pairs={{0,2},{1,3},{2,0},{3,1},{4,6},{5,7},{6,4},{7,5},{8,10},{9,11},{10,... | collective-permute-start | bytes 393224 | tf_op jit(solution)/shard_map/ppermute | solution.py:25
  44.0 12.1 %collective-permute-start.15 = (bf16[16,4096]{1,0:T(8,128)(2,1)S(1)}, bf16[16,4096]{1,0:T(8,128)(2,1)S(1)}, u32[]{:S(2)}, u32[]{:S(2)}) collective-permute-start(bf16[16,4096]{1,0:T(8,128)(2,1)S(1)} %add_convert_fusion.1), channel_id=1, source_target_pairs={{0,2},{1,3},{2,0},{3,1},{4,6},{5,7},{6,4},{7,5},{8,10},{9,11},{10,... | collective-permute-start | bytes 393224 | tf_op jit(solution)/shard_map/ppermute | solution.py:25
  44.6 16.1 %collective-permute-start.19 = (bf16[16,4096]{1,0:T(8,128)(2,1)S(1)}, bf16[16,4096]{1,0:T(8,128)(2,1)S(1)}, u32[]{:S(2)}, u32[]{:S(2)}) collective-permute-start(bf16[16,4096]{1,0:T(8,128)(2,1)S(1)} %add_convert_fusion.2.refs_0_), channel_id=1, source_target_pairs={{0,2},{1,3},{2,0},{3,1},{4,6},{5,7},{6,4},{7,5},{8,10},{9,11},{10,... | collective-permute-start | bytes 393224 | tf_op jit(solution)/shard_map/ppermute | solution.py:25
  48.1 11.4 %collective-permute-start.7 = (bf16[8,4096]{1,0:T(8,128)(2,1)S(1)}, bf16[8,4096]{1,0:T(8,128)(2,1)S(1)}, u32[]{:S(2)}, u32[]{:S(2)}) collective-permute-start(bf16[8,4096]{1,0:T(8,128)(2,1)S(1)} %get-tuple-element.36), channel_id=1, source_target_pairs={{0,4},{4,0},{8,12},{12,8},{1,5},{5,1},{9,13},{13,9},{2,6},{6,2},{1... | collective-permute-start | bytes 196616 | tf_op jit(solution)/shard_map/ppermute | solution.py:25
  56.1 6.5 %collective-permute-start.22 = (bf16[16,4096]{1,0:T(8,128)(2,1)S(1)}, bf16[16,4096]{1,0:T(8,128)(2,1)S(1)}, u32[]{:S(2)}, u32[]{:S(2)}) collective-permute-start(bf16[16,4096]{1,0:T(8,128)(2,1)S(1)} %add_convert_fusion.refs_4_), channel_id=1, source_target_pairs={{0,2},{1,3},{2,0},{3,1},{4,6},{5,7},{6,4},{7,5},{8,10},{9,11},{10,... | collective-permute-start | bytes 393224 | tf_op jit(solution)/shard_map/ppermute | solution.py:25
  56.2 6.5 %collective-permute-start.16 = (bf16[8,4096]{1,0:T(8,128)(2,1)S(1)}, bf16[8,4096]{1,0:T(8,128)(2,1)S(1)}, u32[]{:S(2)}, u32[]{:S(2)}) collective-permute-start(bf16[8,4096]{1,0:T(8,128)(2,1)S(1)} %get-tuple-element.35), channel_id=1, source_target_pairs={{0,8},{4,12},{8,0},{12,4},{1,9},{5,13},{9,1},{13,5},{2,10},{6,14},... | collective-permute-start | bytes 196616 | tf_op jit(solution)/shard_map/ppermute | solution.py:25
  57.8 10.6 %collective-permute-start.18 = (bf16[16,4096]{1,0:T(8,128)(2,1)S(1)}, bf16[16,4096]{1,0:T(8,128)(2,1)S(1)}, u32[]{:S(2)}, u32[]{:S(2)}) collective-permute-start(bf16[16,4096]{1,0:T(8,128)(2,1)S(1)} %add_convert_fusion.2.refs_0_), channel_id=1, source_target_pairs={{0,1},{1,0},{2,3},{3,2},{4,5},{5,4},{6,7},{7,6},{8,9},{9,8},{10,11... | collective-permute-start | bytes 393224 | tf_op jit(solution)/shard_map/ppermute | solution.py:25
  59.4 9.0 %collective-permute-start.21 = (bf16[16,4096]{1,0:T(8,128)(2,1)S(1)}, bf16[16,4096]{1,0:T(8,128)(2,1)S(1)}, u32[]{:S(2)}, u32[]{:S(2)}) collective-permute-start(bf16[16,4096]{1,0:T(8,128)(2,1)S(1)} %add_convert_fusion.refs_4_), channel_id=1, source_target_pairs={{0,1},{1,0},{2,3},{3,2},{4,5},{5,4},{6,7},{7,6},{8,9},{9,8},{10,11... | collective-permute-start | bytes 393224 | tf_op jit(solution)/shard_map/ppermute | solution.py:25
  60.6 10.3 %collective-permute-start.20 = (bf16[16,4096]{1,0:T(8,128)(2,1)S(1)}, bf16[16,4096]{1,0:T(8,128)(2,1)S(1)}, u32[]{:S(2)}, u32[]{:S(2)}) collective-permute-start(bf16[16,4096]{1,0:T(8,128)(2,1)S(1)} %collective-permute-done.19.refs_2_), channel_id=1, source_target_pairs={{0,1},{1,0},{2,3},{3,2},{4,5},{5,4},{6,7},{7,6},{8,9},{9,8},{10,11... | collective-permute-start | bytes 393224 | tf_op jit(solution)/shard_map/ppermute | solution.py:25
  62.7 9.7 %collective-permute-start.23 = (bf16[16,4096]{1,0:T(8,128)(2,1)S(1)}, bf16[16,4096]{1,0:T(8,128)(2,1)S(1)}, u32[]{:S(2)}, u32[]{:S(2)}) collective-permute-start(bf16[16,4096]{1,0:T(8,128)(2,1)S(1)} %collective-permute-done.22.refs_6_), channel_id=1, source_target_pairs={{0,1},{1,0},{2,3},{3,2},{4,5},{5,4},{6,7},{7,6},{8,9},{9,8},{10,11... | collective-permute-start | bytes 393224 | tf_op jit(solution)/shard_map/ppermute | solution.py:25
  62.7 4.3 %collective-permute-start.17 = (bf16[8,4096]{1,0:T(8,128)(2,1)S(1)}, bf16[8,4096]{1,0:T(8,128)(2,1)S(1)}, u32[]{:S(2)}, u32[]{:S(2)}) collective-permute-start(bf16[8,4096]{1,0:T(8,128)(2,1)S(1)} %get-tuple-element.34), channel_id=1, source_target_pairs={{0,12},{4,8},{8,4},{12,0},{1,13},{5,9},{9,5},{13,1},{2,14},{6,10},... | collective-permute-start | bytes 196616 | tf_op jit(solution)/shard_map/ppermute | solution.py:25

commit v3 on v2

--- a/solution.py
+++ b/solution.py
@@ -25,30 +25,26 @@
     return lax.ppermute(x, axis, [(i, i ^ k) for i in range(n)])
 
 
-def gather_blocks(own, axis):
+def after(x, *others):
+    return lax.optimization_barrier((x, *others))[0] if others else x
+
+
+def bits_of(axis):
     n = lax.axis_size(axis)
-    held = {0: own}
-    bit = n // 2
-    while bit:
-        for r in list(held):
-            held[r ^ bit] = swap(held[r], axis, bit)
-        bit //= 2
-    return [held[r] for r in range(n)]
+    return [1 << i for i in range(n.bit_length() - 1)]
 
 
 def reduce_blocks(blocks, axis):
-    n = lax.axis_size(axis)
     held = dict(enumerate(blocks))
-    bit = 1
-    while bit < n:
+    for bit in bits_of(axis):
         keep = [r for r in held if not r & bit]
         keep.sort(reverse=True)
-        held = {
-            r: held[r].astype(jnp.float32)
-            + swap(held[r ^ bit].astype(jnp.bfloat16), axis, bit).astype(jnp.float32)
-            for r in keep
-        }
-        bit *= 2
+        arrived = {}
+        for r in keep:
+            term = held[r ^ bit].astype(jnp.bfloat16)
+            gates = [arrived[keep[-2]]] if r == 0 and len(keep) > 1 else []
+            arrived[r] = swap(after(term, *gates), axis, bit)
+        held = {r: held[r].astype(jnp.float32) + arrived[r].astype(jnp.float32) for r in keep}
     return held[0]
 
 
@@ -241,40 +237,45 @@
 
 
 def gram_kernel(count, scaling, place_ref, *refs):
-    blocks, out_ref, all_ref, own_ref = refs[:count], refs[count], refs[count + 1], refs[count + 2]
+    blocks = refs[:count]
+    out_hbm, all_ref, own_ref, buffer, sems = refs[count:]
     own = blocks[0].shape[0]
-    step = pl.program_id(0)
-
-    @pl.when(step == 0)
-    def _():
-        for r in range(count):
-            all_ref[r * own : (r + 1) * own, :] = blocks[r][...]
-        width = own_ref.shape[1]
-        own_ref[...] = all_ref[:, pl.ds(pl.multiple_of(place_ref[0] * width, width), width)]
-
-    height = out_ref.shape[1]
-    left = all_ref[:, pl.ds(pl.multiple_of(step * height, height), height)]
-    out_ref[0] = (
-        lax.dot_general(
-            left, own_ref[...], (((0,), (0,)), ((), ())), preferred_element_type=jnp.float32
+    for r in range(count):
+        all_ref[r * own : (r + 1) * own, :] = blocks[r][...]
+    width = own_ref.shape[1]
+    own_ref[...] = all_ref[:, pl.ds(pl.multiple_of(place_ref[0] * width, width), width)]
+    steps, height = buffer.shape[:2]
+    copies = []
+    for i in range(steps):
+        part = slice(i * height, (i + 1) * height)
+        product = lax.dot_general(
+            all_ref[:, part],
+            own_ref[...],
+            (((0,), (0,)), ((), ())),
+            preferred_element_type=jnp.float32,
         )
-        * scaling
-    ).astype(out_ref.dtype)
+        buffer[i] = (product * scaling).astype(buffer.dtype)
+        copies.append(pltpu.make_async_copy(buffer.at[i], out_hbm.at[0, part, :], sems.at[i]))
+        copies[-1].start()
+    for copy in copies:
+        copy.wait()
 
 
 def gram(place, blocks, col_width, scaling):
     count = len(blocks)
     own, width = blocks[0].shape
-    height = 512
+    height = 256
+    steps = width // height
     return pl.pallas_call(
         functools.partial(gram_kernel, count, scaling),
         out_shape=jax.ShapeDtypeStruct((1, width, col_width), jnp.bfloat16),
-        grid=(width // height,),
         in_specs=[SMEM] + [VMEM] * count,
-        out_specs=pl.BlockSpec((1, height, col_width), lambda i: (0, i, 0)),
+        out_specs=HBM,
         scratch_shapes=[
             pltpu.VMEM((count * own, width), jnp.bfloat16),
             pltpu.VMEM((count * own, col_width), jnp.bfloat16),
+            pltpu.VMEM((steps, height, col_width), jnp.bfloat16),
+            pltpu.SemaphoreType.DMA((steps,)),
         ],
         compiler_params=pltpu.CompilerParams(vmem_limit_bytes=32 * MIB),
         cost_estimate=pl.CostEstimate(
@@ -293,23 +294,46 @@
     dp_place = lax.axis_index("dp").astype(jnp.int32)[None]
     pieces, weighted = pack(exp_place, window_ids, expert_ids, router_weight, tokens)
     half = owner_count // 2
-    gate_weight, up_weight, down_weight = load(
-        (gate_weight, up_weight, down_weight), weighted
-    )
     pieces = [swap(piece, "exp", k) if k else piece for k, piece in enumerate(pieces)]
+    bits = bits_of("dp")
+    own = [jnp.concatenate(pieces[:half], axis=0), jnp.concatenate(pieces[half:], axis=0)]
+
+    weights = load((gate_weight, up_weight, down_weight), own[1])
+
+    def first(own, gates):
+        held = {0: own}
+        for bit in reversed(bits):
+            held[bit] = swap(after(own, *gates.get(bit, ())), "dp", bit)
+        return held
+
+    def later(held):
+        for r in range(shard_count):
+            if r not in held:
+                low = r & -r
+                held[r] = swap(held[r ^ low], "dp", low)
+        return [held[r] for r in range(shard_count)]
+
+    a = first(own[0], {})
+    b = first(own[1], {bits[-1]: [a[bit] for bit in bits], bits[0]: [a[bit] for bit in bits]})
+    a[bits[-1]] = after(a[bits[-1]], weights[0])
+    rows_a = later(a)
+    terms_a = expert(rows_a, *weights, None)
+    rows_b = later(b)
+    terms_b = expert(rows_b, *weights, terms_a[0])
+    out_a = reduce_blocks(terms_a, "dp").astype(jnp.bfloat16)
+    a = first(out_a, {})
+    out_b = reduce_blocks(terms_b, "dp").astype(jnp.bfloat16)
+    out_b = after(out_b, *[a[bit] for bit in bits])
+    rows_a = later(a)
+    b = first(out_b, {})
     returned = []
-    gram_rows = []
-    after = None
-    for start in range(0, owner_count, half):
-        own_rows = jnp.concatenate(pieces[start : start + half], axis=0)
-        rows = gather_blocks(own_rows, "dp")
-        terms = expert(rows, gate_weight, up_weight, down_weight, after)
-        after = terms[0]
-        expert_out = reduce_blocks(terms, "dp").astype(jnp.bfloat16)
-        gram_rows += gather_blocks(expert_out, "dp")
-        for k in range(half):
-            piece = expert_out[k * CAP : (k + 1) * CAP]
-            returned.append(swap(piece, "exp", start + k) if start + k else piece)
+    for k in range(owner_count):
+        source = (out_a, out_b)[k // half]
+        piece = source[(k % half) * CAP : (k % half + 1) * CAP]
+        returned.append(swap(piece, "exp", k) if k else piece)
+    b[bits[-1]] = after(b[bits[-1]], *returned[half:])
+    rows_b = later(b)
+    gram_rows = rows_a + rows_b
     scaling = EXPERTS_ALL / (TOPK * tok_count * owner_count * shard_count)
     gram_out = gram(dp_place, gram_rows, feat_width // shard_count, scaling)
     combined = combine(returned, weighted)

time: 78.9 us -> 73.2 us (0.928)
  waiting for transfers between devices: 32.5 us -> 28.5 us
  Pallas kernels: 17 us -> 14.4 us
  starting transfers between devices: 28.3 us -> 29.2 us
    ppermute x24, waiting for transfers between devices: 32.5 us -> 28.5 us  [swap(): return lax.ppermute(x, axis, [(i, i ^ k) for i in range(n)])]
    pallas_call x1, Pallas kernels: 6.29 us -> 3.77 us  [gram(): pl.pallas_call(functools.partial(gram_kernel, count, scaling), out_shape=...]
    ppermute x24, starting transfers between devices: 28.3 us -> 29.2 us  [swap(): return lax.ppermute(x, axis, [(i, i ^ k) for i in range(n)])]
  transfers between devices with their start and end apart: 24 -> 24, of which waited for: 12 -> 12; matrix products, arithmetic and copies ran while one was open for 0% -> 0% of each run, Pallas kernels for 11% -> 12%
where the time goes in v3:
time: 73.2 us; the launch traced here: 73.1 us
  starting transfers between devices  29.2 us (40%)
  waiting for transfers between devices  28.5 us (39%)
  Pallas kernels  14.4 us (20%)
  between operations  0.75 us (1%)
    ppermute x24, starting transfers between devices, swap(): return lax.ppermute(x, axis, [(i, i ^ k) for i in range(n)])  29.2 us
    ppermute x24, waiting for transfers between devices, swap(): return lax.ppermute(x, axis, [(i, i ^ k) for i in range(n)])  28.5 us
    pallas_call x1, Pallas kernels, load(): pl.pallas_call(functools.partial(load_kernel, count), out_shape=[jax.Shap...  3.79 us
    pallas_call x1, Pallas kernels, gram(): pl.pallas_call(functools.partial(gram_kernel, count, scaling), out_shape=...  3.77 us
    pallas_call x2, Pallas kernels, expert(): pl.pallas_call(functools.partial(expert_kernel, count), out_shape=[jax.Sh...  3.72 us
    pallas_call x1, Pallas kernels, pack(): pl.pallas_call(functools.partial(pack_kernel, count), out_shape=[jax.Shap...  1.73 us
  transfers between devices with their start and end apart: 24, of which 12 were waited for; matrix products, arithmetic and copies ran while one was open for 0% of the time, Pallas kernels for 12%

profile of v3, /device:TPU:0, one launch (start us, length us, event | category | flops | bytes accessed | tf_op | source)
XLA Modules:
  0.0 73.1 jit_solution(3656456061883343624)
XLA Ops:
  0.6 1.7 %shard_map.86 = (bf16[8,4096]{1,0:T(8,128)(2,1)S(1)}, bf16[8,4096]{1,0:T(8,128)(2,1)S(1)}, bf16[8,4096]{1,0:T(8,128)(2,1)S(1)}, bf16[8,4096]{1,0:T(8,128)(2,1)S(1)}, bf16[96,128]{1,0:T(8,128)(2,1)S(1)}) custom-call(s32[1]{0:T(128)} %bitcast.place_ref, s32[4]{0:T(128)} %window_hbm.1, s32[8,128]{1,0:T(8,128)} %bitcast.4, f32[8,128]{1,0:T(8,128)} %bitcast.5, ...), custom_call_target="tpu_custom_call" | custom-call | flops 33554432 | bytes 2097152 | tf_op jit(solution)/shard_map/pallas_call | solution.py:110
  2.9 2.6 %collective-permute-start.3 = (bf16[8,4096]{1,0:T(8,128)(2,1)S(1)}, bf16[8,4096]{1,0:T(8,128)(2,1)S(1)}, u32[]{:S(2)}, u32[]{:S(2)}) collective-permute-start(bf16[8,4096]{1,0:T(8,128)(2,1)S(1)} %get-tuple-element.26), channel_id=1, source_target_pairs={{0,8},{4,12},{8,0},{12,4},{1,9},{5,13},{9,1},{13,5},{2,10},{6,14},... | collective-permute-start | bytes 196616 | tf_op jit(solution)/shard_map/ppermute | solution.py:25
  5.6 1.8 %collective-permute-start.1 = (bf16[16,4096]{1,0:T(8,128)(2,1)S(1)}, bf16[16,4096]{1,0:T(8,128)(2,1)S(1)}, u32[]{:S(2)}, u32[]{:S(2)}) collective-permute-start(bf16[16,4096]{1,0:T(8,128)(2,1)S(1)} %constant_dynamic-update-slice_fusion.refs_0_), channel_id=1, source_target_pairs={{0,1},{1,0},{2,3},{3,2},{4,5},{5,4},{6,7},{7,6},{8,9},{9,8},{10,11... | collective-permute-start | bytes 393224 | tf_op jit(solution)/shard_map/ppermute | solution.py:25
  7.4 2.6 %collective-permute-start.2 = (bf16[16,4096]{1,0:T(8,128)(2,1)S(1)}, bf16[16,4096]{1,0:T(8,128)(2,1)S(1)}, u32[]{:S(2)}, u32[]{:S(2)}) collective-permute-start(bf16[16,4096]{1,0:T(8,128)(2,1)S(1)} %constant_dynamic-update-slice_fusion.refs_0_), channel_id=1, source_target_pairs={{0,2},{1,3},{2,0},{3,1},{4,6},{5,7},{6,4},{7,5},{8,10},{9,11},{10,... | collective-permute-start | bytes 393224 | tf_op jit(solution)/shard_map/ppermute | solution.py:25
  10.1 3.8 %shard_map.87 = (bf16[1,4096,384]{2,1,0:T(8,128)(2,1)S(1)}, bf16[1,4096,384]{2,1,0:T(8,128)(2,1)S(1)}, bf16[1,384,4096]{2,1,0:T(8,128)(2,1)S(1)}) custom-call(bf16[1,4096,384]{2,1,0:T(8,128)(2,1)} %refs_0_.1, bf16[1,4096,384]{2,1,0:T(8,128)(2,1)} %refs_1_.1, bf16[1,384,4096]{2,1,0:T(8,128)(2,1)} %refs_2_.1, ...), custom_call_target="tpu_custom_call" | custom-call | bytes 18874368 | tf_op jit(solution)/shard_map/pallas_call | solution.py:147
  13.9 2.8 %collective-permute-done.2.refs_2_ = bf16[16,4096]{1,0:T(8,128)(2,1)S(1)} collective-permute-done((bf16[16,4096]{1,0:T(8,128)(2,1)S(1)}, bf16[16,4096]{1,0:T(8,128)(2,1)S(1)}, u32[]{:S(2)}, u32[]{:S(2)}) %collective-permute-start.2) | collective-permute-done | bytes 131104 | tf_op jit(solution)/shard_map/ppermute | solution.py:25
  17.0 2.7 %collective-permute-start.5 = (bf16[16,4096]{1,0:T(8,128)(2,1)S(1)}, bf16[16,4096]{1,0:T(8,128)(2,1)S(1)}, u32[]{:S(2)}, u32[]{:S(2)}) collective-permute-start(bf16[16,4096]{1,0:T(8,128)(2,1)S(1)} %collective-permute-done.2.refs_2_), channel_id=1, source_target_pairs={{0,1},{1,0},{2,3},{3,2},{4,5},{5,4},{6,7},{7,6},{8,9},{9,8},{10,11... | collective-permute-start | bytes 393224 | tf_op jit(solution)/shard_map/ppermute | solution.py:25
  19.7 4.3 %collective-permute-done.11.refs_2_ = bf16[16,4096]{1,0:T(8,128)(2,1)S(1)} collective-permute-done((bf16[16,4096]{1,0:T(8,128)(2,1)S(1)}, bf16[16,4096]{1,0:T(8,128)(2,1)S(1)}, u32[]{:S(2)}, u32[]{:S(2)}) %collective-permute-start.11) | collective-permute-done | bytes 131104 | tf_op jit(solution)/shard_map/ppermute | solution.py:25
  25.4 1.9 %shard_map.88 = (f32[16,4096]{1,0:T(8,128)S(1)}, bf16[16,4096]{1,0:T(8,128)(2,1)S(1)}, f32[16,4096]{1,0:T(8,128)S(1)}, bf16[16,4096]{1,0:T(8,128)(2,1)S(1)}) custom-call(bf16[16,4096]{1,0:T(8,128)(2,1)S(1)} %constant_dynamic-update-slice_fusion.refs_0_, bf16[16,4096]{1,0:T(8,128)(2,1)S(1)} %collective-permute-done.1.refs_1_, ...), custom_call_target="tpu_custom_call" | custom-call | flops 1207959552 | bytes 11010048 | tf_op jit(solution)/shard_map/pallas_call | solution.py:188
  28.1 2.7 %collective-permute-done.12.refs_3_ = bf16[16,4096]{1,0:T(8,128)(2,1)S(1)} collective-permute-done((bf16[16,4096]{1,0:T(8,128)(2,1)S(1)}, bf16[16,4096]{1,0:T(8,128)(2,1)S(1)}, u32[]{:S(2)}, u32[]{:S(2)}) %collective-permute-start.12) | collective-permute-done | bytes 131104 | tf_op jit(solution)/shard_map/ppermute | solution.py:25
  30.8 1.9 %shard_map.89 = (f32[16,4096]{1,0:T(8,128)S(1)}, bf16[16,4096]{1,0:T(8,128)(2,1)S(1)}, f32[16,4096]{1,0:T(8,128)S(1)}, bf16[16,4096]{1,0:T(8,128)(2,1)S(1)}) custom-call(bf16[16,4096]{1,0:T(8,128)(2,1)S(1)} %constant_dynamic-update-slice_fusion.2.refs_3_.refs_0_, bf16[16,4096]{1,0:T(8,128)(2,1)S(1)} %collective-permute-done.10.refs_1_, ...), custom_call_target="tpu_custom_call" | custom-call | flops 1207959552 | bytes 11010048 | tf_op jit(solution)/shard_map/pallas_call | solution.py:188
  33.7 2.0 %collective-permute-start.8 = (bf16[16,4096]{1,0:T(8,128)(2,1)S(1)}, bf16[16,4096]{1,0:T(8,128)(2,1)S(1)}, u32[]{:S(2)}, u32[]{:S(2)}) collective-permute-start(bf16[16,4096]{1,0:T(8,128)(2,1)S(1)} %add_convert_fusion.3), channel_id=1, source_target_pairs={{0,2},{1,3},{2,0},{3,1},{4,6},{5,7},{6,4},{7,5},{8,10},{9,11},{10,... | collective-permute-start | bytes 393224 | tf_op jit(solution)/shard_map/ppermute | solution.py:25
  36.0 5.3 %collective-permute-done.13 = bf16[16,4096]{1,0:T(8,128)(2,1)S(1)} collective-permute-done((bf16[16,4096]{1,0:T(8,128)(2,1)S(1)}, bf16[16,4096]{1,0:T(8,128)(2,1)S(1)}, u32[]{:S(2)}, u32[]{:S(2)}) %collective-permute-start.13) | collective-permute-done | bytes 131104 | tf_op jit(solution)/shard_map/ppermute | solution.py:25
  41.8 2.9 %collective-permute-start.14 = (bf16[16,4096]{1,0:T(8,128)(2,1)S(1)}, bf16[16,4096]{1,0:T(8,128)(2,1)S(1)}, u32[]{:S(2)}, u32[]{:S(2)}) collective-permute-start(bf16[16,4096]{1,0:T(8,128)(2,1)S(1)} %get-tuple-element.41), channel_id=1, source_target_pairs={{0,1},{1,0},{2,3},{3,2},{4,5},{5,4},{6,7},{7,6},{8,9},{9,8},{10,11... | collective-permute-start | bytes 393224 | tf_op jit(solution)/shard_map/ppermute | solution.py:25
  45.8 2.6 %collective-permute-start.17 = (bf16[16,4096]{1,0:T(8,128)(2,1)S(1)}, bf16[16,4096]{1,0:T(8,128)(2,1)S(1)}, u32[]{:S(2)}, u32[]{:S(2)}) collective-permute-start(bf16[16,4096]{1,0:T(8,128)(2,1)S(1)} %add_convert_fusion.2.refs_0_), channel_id=1, source_target_pairs={{0,2},{1,3},{2,0},{3,1},{4,6},{5,7},{6,4},{7,5},{8,10},{9,11},{10,... | collective-permute-start | bytes 393224 | tf_op jit(solution)/shard_map/ppermute | solution.py:25
  48.3 2.5 %collective-permute-done.15 = bf16[16,4096]{1,0:T(8,128)(2,1)S(1)} collective-permute-done((bf16[16,4096]{1,0:T(8,128)(2,1)S(1)}, bf16[16,4096]{1,0:T(8,128)(2,1)S(1)}, u32[]{:S(2)}, u32[]{:S(2)}) %collective-permute-start.15) | collective-permute-done | bytes 131104 | tf_op jit(solution)/shard_map/ppermute | solution.py:25
  50.9 2.5 %collective-permute-done.16.refs_1_ = bf16[16,4096]{1,0:T(8,128)(2,1)S(1)} collective-permute-done((bf16[16,4096]{1,0:T(8,128)(2,1)S(1)}, bf16[16,4096]{1,0:T(8,128)(2,1)S(1)}, u32[]{:S(2)}, u32[]{:S(2)}) %collective-permute-start.16) | collective-permute-done | bytes 131104 | tf_op jit(solution)/shard_map/ppermute | solution.py:25
  53.4 2.6 %collective-permute-start.22 = (bf16[16,4096]{1,0:T(8,128)(2,1)S(1)}, bf16[16,4096]{1,0:T(8,128)(2,1)S(1)}, u32[]{:S(2)}, u32[]{:S(2)}) collective-permute-start(bf16[16,4096]{1,0:T(8,128)(2,1)S(1)} %add_convert_fusion.refs_4_), channel_id=1, source_target_pairs={{0,2},{1,3},{2,0},{3,1},{4,6},{5,7},{6,4},{7,5},{8,10},{9,11},{10,... | collective-permute-start | bytes 393224 | tf_op jit(solution)/shard_map/ppermute | solution.py:25
  56.1 1.6 %collective-permute-start.18 = (bf16[8,4096]{1,0:T(8,128)(2,1)S(1)}, bf16[8,4096]{1,0:T(8,128)(2,1)S(1)}, u32[]{:S(2)}, u32[]{:S(2)}) collective-permute-start(bf16[8,4096]{1,0:T(8,128)(2,1)S(1)} %get-tuple-element.47), channel_id=1, source_target_pairs={{0,8},{4,12},{8,0},{12,4},{1,9},{5,13},{9,1},{13,5},{2,10},{6,14},... | collective-permute-start | bytes 196616 | tf_op jit(solution)/shard_map/ppermute | solution.py:25
  60.4 1.4 %collective-permute-done.19.refs_3_ = bf16[8,4096]{1,0:T(8,128)(2,1)S(1)} collective-permute-done((bf16[8,4096]{1,0:T(8,128)(2,1)S(1)}, bf16[8,4096]{1,0:T(8,128)(2,1)S(1)}, u32[]{:S(2)}, u32[]{:S(2)}) %collective-permute-start.19) | collective-permute-done | bytes 65568 | tf_op jit(solution)/shard_map/ppermute | solution.py:25
  63.8 1.4 %shard_map.90 = bf16[128,4096]{1,0:T(8,128)(2,1)} custom-call(bf16[8,4096]{1,0:T(8,128)(2,1)S(1)} %get-tuple-element.49.refs_0_, bf16[8,4096]{1,0:T(8,128)(2,1)S(1)} %collective-permute-done.9.refs_1_, bf16[8,4096]{1,0:T(8,128)(2,1)S(1)} %collective-permute-done.18.refs_2_, bf16[8,4096]{1,0:T(8,128)(2,1)S(1)} %collective-permute-done.19.refs_3_, ...), custom_call_target="tpu_custom_call" | custom-call | flops 100663296 | bytes 2097152 | tf_op jit(solution)/shard_map/pallas_call | solution.py:225
  65.3 1.6 %collective-permute-done.20.refs_3_ = bf16[16,4096]{1,0:T(8,128)(2,1)S(1)} collective-permute-done((bf16[16,4096]{1,0:T(8,128)(2,1)S(1)}, bf16[16,4096]{1,0:T(8,128)(2,1)S(1)}, u32[]{:S(2)}, u32[]{:S(2)}) %collective-permute-start.20) | collective-permute-done | bytes 131104 | tf_op jit(solution)/shard_map/ppermute | solution.py:25
  66.8 2.5 %collective-permute-done.23.refs_7_ = bf16[16,4096]{1,0:T(8,128)(2,1)S(1)} collective-permute-done((bf16[16,4096]{1,0:T(8,128)(2,1)S(1)}, bf16[16,4096]{1,0:T(8,128)(2,1)S(1)}, u32[]{:S(2)}, u32[]{:S(2)}) %collective-permute-start.23) | collective-permute-done | bytes 131104 | tf_op jit(solution)/shard_map/ppermute | solution.py:25
  69.3 3.8 %shard_map.91 = bf16[1,4096,1024]{2,1,0:T(8,128)(2,1)} custom-call(s32[1]{0:T(128)} %bitcast.3.place_ref, bf16[16,4096]{1,0:T(8,128)(2,1)S(1)} %add_convert_fusion.2.refs_0_, bf16[16,4096]{1,0:T(8,128)(2,1)S(1)} %collective-permute-done.16.refs_1_, bf16[16,4096]{1,0:T(8,128)(2,1)S(1)} %collective-permute-done.17.refs_2_, ...), custom_call_target="tpu_custom_call" | custom-call | flops 1073741824 | bytes 9437184 | tf_op jit(solution)/shard_map/pallas_call | solution.py:269
  (40 shorter events, 10.8 us)
Async XLA Ops:
  2.4 3.2 %collective-permute-start = (bf16[8,4096]{1,0:T(8,128)(2,1)S(1)}, bf16[8,4096]{1,0:T(8,128)(2,1)S(1)}, u32[]{:S(2)}, u32[]{:S(2)}) collective-permute-start(bf16[8,4096]{1,0:T(8,128)(2,1)S(1)} %get-tuple-element.25), channel_id=1, source_target_pairs={{0,4},{4,0},{8,12},{12,8},{1,5},{5,1},{9,13},{13,9},{2,6},{6,2},{1... | collective-permute-start | bytes 196616 | tf_op jit(solution)/shard_map/ppermute | solution.py:25
  2.9 7.1 %collective-permute-start.3 = (bf16[8,4096]{1,0:T(8,128)(2,1)S(1)}, bf16[8,4096]{1,0:T(8,128)(2,1)S(1)}, u32[]{:S(2)}, u32[]{:S(2)}) collective-permute-start(bf16[8,4096]{1,0:T(8,128)(2,1)S(1)} %get-tuple-element.26), channel_id=1, source_target_pairs={{0,8},{4,12},{8,0},{12,4},{1,9},{5,13},{9,1},{13,5},{2,10},{6,14},... | collective-permute-start | bytes 196616 | tf_op jit(solution)/shard_map/ppermute | solution.py:25
  5.5 4.5 %collective-permute-start.4 = (bf16[8,4096]{1,0:T(8,128)(2,1)S(1)}, bf16[8,4096]{1,0:T(8,128)(2,1)S(1)}, u32[]{:S(2)}, u32[]{:S(2)}) collective-permute-start(bf16[8,4096]{1,0:T(8,128)(2,1)S(1)} %get-tuple-element.27), channel_id=1, source_target_pairs={{0,12},{4,8},{8,4},{12,0},{1,13},{5,9},{9,5},{13,1},{2,14},{6,10},... | collective-permute-start | bytes 196616 | tf_op jit(solution)/shard_map/ppermute | solution.py:25
  5.6 11.1 %collective-permute-start.1 = (bf16[16,4096]{1,0:T(8,128)(2,1)S(1)}, bf16[16,4096]{1,0:T(8,128)(2,1)S(1)}, u32[]{:S(2)}, u32[]{:S(2)}) collective-permute-start(bf16[16,4096]{1,0:T(8,128)(2,1)S(1)} %constant_dynamic-update-slice_fusion.refs_0_), channel_id=1, source_target_pairs={{0,1},{1,0},{2,3},{3,2},{4,5},{5,4},{6,7},{7,6},{8,9},{9,8},{10,11... | collective-permute-start | bytes 393224 | tf_op jit(solution)/shard_map/ppermute | solution.py:25
  7.4 9.2 %collective-permute-start.2 = (bf16[16,4096]{1,0:T(8,128)(2,1)S(1)}, bf16[16,4096]{1,0:T(8,128)(2,1)S(1)}, u32[]{:S(2)}, u32[]{:S(2)}) collective-permute-start(bf16[16,4096]{1,0:T(8,128)(2,1)S(1)} %constant_dynamic-update-slice_fusion.refs_0_), channel_id=1, source_target_pairs={{0,2},{1,3},{2,0},{3,1},{4,6},{5,7},{6,4},{7,5},{8,10},{9,11},{10,... | collective-permute-start | bytes 393224 | tf_op jit(solution)/shard_map/ppermute | solution.py:25
  16.7 7.3 %collective-permute-start.11 = (bf16[16,4096]{1,0:T(8,128)(2,1)S(1)}, bf16[16,4096]{1,0:T(8,128)(2,1)S(1)}, u32[]{:S(2)}, u32[]{:S(2)}) collective-permute-start(bf16[16,4096]{1,0:T(8,128)(2,1)S(1)} %constant_dynamic-update-slice_fusion.2.refs_3_.refs_0_), channel_id=1, source_target_pairs={{0,2},{1,3},{2,0},{3,1},{4,6},{5,7},{6,4},{7,5},{8,10},{9,11},{10,... | collective-permute-start | bytes 393224 | tf_op jit(solution)/shard_map/ppermute | solution.py:25
  17.0 8.4 %collective-permute-start.5 = (bf16[16,4096]{1,0:T(8,128)(2,1)S(1)}, bf16[16,4096]{1,0:T(8,128)(2,1)S(1)}, u32[]{:S(2)}, u32[]{:S(2)}) collective-permute-start(bf16[16,4096]{1,0:T(8,128)(2,1)S(1)} %collective-permute-done.2.refs_2_), channel_id=1, source_target_pairs={{0,1},{1,0},{2,3},{3,2},{4,5},{5,4},{6,7},{7,6},{8,9},{9,8},{10,11... | collective-permute-start | bytes 393224 | tf_op jit(solution)/shard_map/ppermute | solution.py:25
  19.7 8.4 %collective-permute-start.10 = (bf16[16,4096]{1,0:T(8,128)(2,1)S(1)}, bf16[16,4096]{1,0:T(8,128)(2,1)S(1)}, u32[]{:S(2)}, u32[]{:S(2)}) collective-permute-start(bf16[16,4096]{1,0:T(8,128)(2,1)S(1)} %constant_dynamic-update-slice_fusion.2.refs_3_.refs_0_), channel_id=1, source_target_pairs={{0,1},{1,0},{2,3},{3,2},{4,5},{5,4},{6,7},{7,6},{8,9},{9,8},{10,11... | collective-permute-start | bytes 393224 | tf_op jit(solution)/shard_map/ppermute | solution.py:25
  24.0 6.8 %collective-permute-start.12 = (bf16[16,4096]{1,0:T(8,128)(2,1)S(1)}, bf16[16,4096]{1,0:T(8,128)(2,1)S(1)}, u32[]{:S(2)}, u32[]{:S(2)}) collective-permute-start(bf16[16,4096]{1,0:T(8,128)(2,1)S(1)} %collective-permute-done.11.refs_2_), channel_id=1, source_target_pairs={{0,1},{1,0},{2,3},{3,2},{4,5},{5,4},{6,7},{7,6},{8,9},{9,8},{10,11... | collective-permute-start | bytes 393224 | tf_op jit(solution)/shard_map/ppermute | solution.py:25
  27.3 6.4 %collective-permute-start.6 = (bf16[16,4096]{1,0:T(8,128)(2,1)S(1)}, bf16[16,4096]{1,0:T(8,128)(2,1)S(1)}, u32[]{:S(2)}, u32[]{:S(2)}) collective-permute-start(bf16[16,4096]{1,0:T(8,128)(2,1)S(1)} %get-tuple-element.34), channel_id=1, source_target_pairs={{0,1},{1,0},{2,3},{3,2},{4,5},{5,4},{6,7},{7,6},{8,9},{9,8},{10,11... | collective-permute-start | bytes 393224 | tf_op jit(solution)/shard_map/ppermute | solution.py:25
  32.7 8.6 %collective-permute-start.13 = (bf16[16,4096]{1,0:T(8,128)(2,1)S(1)}, bf16[16,4096]{1,0:T(8,128)(2,1)S(1)}, u32[]{:S(2)}, u32[]{:S(2)}) collective-permute-start(bf16[16,4096]{1,0:T(8,128)(2,1)S(1)} %get-tuple-element.40), channel_id=1, source_target_pairs={{0,1},{1,0},{2,3},{3,2},{4,5},{5,4},{6,7},{7,6},{8,9},{9,8},{10,11... | collective-permute-start | bytes 393224 | tf_op jit(solution)/shard_map/ppermute | solution.py:25
  33.7 11.0 %collective-permute-start.8 = (bf16[16,4096]{1,0:T(8,128)(2,1)S(1)}, bf16[16,4096]{1,0:T(8,128)(2,1)S(1)}, u32[]{:S(2)}, u32[]{:S(2)}) collective-permute-start(bf16[16,4096]{1,0:T(8,128)(2,1)S(1)} %add_convert_fusion.3), channel_id=1, source_target_pairs={{0,2},{1,3},{2,0},{3,1},{4,6},{5,7},{6,4},{7,5},{8,10},{9,11},{10,... | collective-permute-start | bytes 393224 | tf_op jit(solution)/shard_map/ppermute | solution.py:25
  35.7 9.0 %collective-permute-start.7 = (bf16[16,4096]{1,0:T(8,128)(2,1)S(1)}, bf16[16,4096]{1,0:T(8,128)(2,1)S(1)}, u32[]{:S(2)}, u32[]{:S(2)}) collective-permute-start(bf16[16,4096]{1,0:T(8,128)(2,1)S(1)} %get-tuple-element.35), channel_id=1, source_target_pairs={{0,1},{1,0},{2,3},{3,2},{4,5},{5,4},{6,7},{7,6},{8,9},{9,8},{10,11... | collective-permute-start | bytes 393224 | tf_op jit(solution)/shard_map/ppermute | solution.py:25
  41.3 9.5 %collective-permute-start.15 = (bf16[16,4096]{1,0:T(8,128)(2,1)S(1)}, bf16[16,4096]{1,0:T(8,128)(2,1)S(1)}, u32[]{:S(2)}, u32[]{:S(2)}) collective-permute-start(bf16[16,4096]{1,0:T(8,128)(2,1)S(1)} %add_convert_fusion.1), channel_id=1, source_target_pairs={{0,2},{1,3},{2,0},{3,1},{4,6},{5,7},{6,4},{7,5},{8,10},{9,11},{10,... | collective-permute-start | bytes 393224 | tf_op jit(solution)/shard_map/ppermute | solution.py:25
  41.8 9.1 %collective-permute-start.14 = (bf16[16,4096]{1,0:T(8,128)(2,1)S(1)}, bf16[16,4096]{1,0:T(8,128)(2,1)S(1)}, u32[]{:S(2)}, u32[]{:S(2)}) collective-permute-start(bf16[16,4096]{1,0:T(8,128)(2,1)S(1)} %get-tuple-element.41), channel_id=1, source_target_pairs={{0,1},{1,0},{2,3},{3,2},{4,5},{5,4},{6,7},{7,6},{8,9},{9,8},{10,11... | collective-permute-start | bytes 393224 | tf_op jit(solution)/shard_map/ppermute | solution.py:25
  44.8 8.7 %collective-permute-start.16 = (bf16[16,4096]{1,0:T(8,128)(2,1)S(1)}, bf16[16,4096]{1,0:T(8,128)(2,1)S(1)}, u32[]{:S(2)}, u32[]{:S(2)}) collective-permute-start(bf16[16,4096]{1,0:T(8,128)(2,1)S(1)} %add_convert_fusion.2.refs_0_), channel_id=1, source_target_pairs={{0,1},{1,0},{2,3},{3,2},{4,5},{5,4},{6,7},{7,6},{8,9},{9,8},{10,11... | collective-permute-start | bytes 393224 | tf_op jit(solution)/shard_map/ppermute | solution.py:25
  45.8 7.7 %collective-permute-start.17 = (bf16[16,4096]{1,0:T(8,128)(2,1)S(1)}, bf16[16,4096]{1,0:T(8,128)(2,1)S(1)}, u32[]{:S(2)}, u32[]{:S(2)}) collective-permute-start(bf16[16,4096]{1,0:T(8,128)(2,1)S(1)} %add_convert_fusion.2.refs_0_), channel_id=1, source_target_pairs={{0,2},{1,3},{2,0},{3,1},{4,6},{5,7},{6,4},{7,5},{8,10},{9,11},{10,... | collective-permute-start | bytes 393224 | tf_op jit(solution)/shard_map/ppermute | solution.py:25
  53.4 8.4 %collective-permute-start.22 = (bf16[16,4096]{1,0:T(8,128)(2,1)S(1)}, bf16[16,4096]{1,0:T(8,128)(2,1)S(1)}, u32[]{:S(2)}, u32[]{:S(2)}) collective-permute-start(bf16[16,4096]{1,0:T(8,128)(2,1)S(1)} %add_convert_fusion.refs_4_), channel_id=1, source_target_pairs={{0,2},{1,3},{2,0},{3,1},{4,6},{5,7},{6,4},{7,5},{8,10},{9,11},{10,... | collective-permute-start | bytes 393224 | tf_op jit(solution)/shard_map/ppermute | solution.py:25
  56.1 4.3 %collective-permute-start.18 = (bf16[8,4096]{1,0:T(8,128)(2,1)S(1)}, bf16[8,4096]{1,0:T(8,128)(2,1)S(1)}, u32[]{:S(2)}, u32[]{:S(2)}) collective-permute-start(bf16[8,4096]{1,0:T(8,128)(2,1)S(1)} %get-tuple-element.47), channel_id=1, source_target_pairs={{0,8},{4,12},{8,0},{12,4},{1,9},{5,13},{9,1},{13,5},{2,10},{6,14},... | collective-permute-start | bytes 196616 | tf_op jit(solution)/shard_map/ppermute | solution.py:25
  57.7 4.2 %collective-permute-start.19 = (bf16[8,4096]{1,0:T(8,128)(2,1)S(1)}, bf16[8,4096]{1,0:T(8,128)(2,1)S(1)}, u32[]{:S(2)}, u32[]{:S(2)}) collective-permute-start(bf16[8,4096]{1,0:T(8,128)(2,1)S(1)} %get-tuple-element.46), channel_id=1, source_target_pairs={{0,12},{4,8},{8,4},{12,0},{1,13},{5,9},{9,5},{13,1},{2,14},{6,10},... | collective-permute-start | bytes 196616 | tf_op jit(solution)/shard_map/ppermute | solution.py:25
  57.7 9.2 %collective-permute-start.21 = (bf16[16,4096]{1,0:T(8,128)(2,1)S(1)}, bf16[16,4096]{1,0:T(8,128)(2,1)S(1)}, u32[]{:S(2)}, u32[]{:S(2)}) collective-permute-start(bf16[16,4096]{1,0:T(8,128)(2,1)S(1)} %add_convert_fusion.refs_4_), channel_id=1, source_target_pairs={{0,1},{1,0},{2,3},{3,2},{4,5},{5,4},{6,7},{7,6},{8,9},{9,8},{10,11... | collective-permute-start | bytes 393224 | tf_op jit(solution)/shard_map/ppermute | solution.py:25
  58.4 8.5 %collective-permute-start.20 = (bf16[16,4096]{1,0:T(8,128)(2,1)S(1)}, bf16[16,4096]{1,0:T(8,128)(2,1)S(1)}, u32[]{:S(2)}, u32[]{:S(2)}) collective-permute-start(bf16[16,4096]{1,0:T(8,128)(2,1)S(1)} %collective-permute-done.17.refs_2_), channel_id=1, source_target_pairs={{0,1},{1,0},{2,3},{3,2},{4,5},{5,4},{6,7},{7,6},{8,9},{9,8},{10,11... | collective-permute-start | bytes 393224 | tf_op jit(solution)/shard_map/ppermute | solution.py:25
  61.8 7.5 %collective-permute-start.23 = (bf16[16,4096]{1,0:T(8,128)(2,1)S(1)}, bf16[16,4096]{1,0:T(8,128)(2,1)S(1)}, u32[]{:S(2)}, u32[]{:S(2)}) collective-permute-start(bf16[16,4096]{1,0:T(8,128)(2,1)S(1)} %collective-permute-done.22.refs_6_), channel_id=1, source_target_pairs={{0,1},{1,0},{2,3},{3,2},{4,5},{5,4},{6,7},{7,6},{8,9},{9,8},{10,11... | collective-permute-start | bytes 393224 | tf_op jit(solution)/shard_map/ppermute | solution.py:25
  62.5 1.3 %collective-permute-start.9 = (bf16[8,4096]{1,0:T(8,128)(2,1)S(1)}, bf16[8,4096]{1,0:T(8,128)(2,1)S(1)}, u32[]{:S(2)}, u32[]{:S(2)}) collective-permute-start(bf16[8,4096]{1,0:T(8,128)(2,1)S(1)} %get-tuple-element.48), channel_id=1, source_target_pairs={{0,4},{4,0},{8,12},{12,8},{1,5},{5,1},{9,13},{13,9},{2,6},{6,2},{1... | collective-permute-start | bytes 196616 | tf_op jit(solution)/shard_map/ppermute | solution.py:25

commit v4 on v3

--- a/solution.py
+++ b/solution.py
@@ -39,12 +39,11 @@
     for bit in bits_of(axis):
         keep = [r for r in held if not r & bit]
         keep.sort(reverse=True)
-        arrived = {}
-        for r in keep:
-            term = held[r ^ bit].astype(jnp.bfloat16)
-            gates = [arrived[keep[-2]]] if r == 0 and len(keep) > 1 else []
-            arrived[r] = swap(after(term, *gates), axis, bit)
-        held = {r: held[r].astype(jnp.float32) + arrived[r].astype(jnp.float32) for r in keep}
+        held = {
+            r: held[r].astype(jnp.float32)
+            + swap(held[r ^ bit].astype(jnp.bfloat16), axis, bit).astype(jnp.float32)
+            for r in keep
+        }
     return held[0]
 
 
@@ -323,7 +322,7 @@
     out_a = reduce_blocks(terms_a, "dp").astype(jnp.bfloat16)
     a = first(out_a, {})
     out_b = reduce_blocks(terms_b, "dp").astype(jnp.bfloat16)
-    out_b = after(out_b, *[a[bit] for bit in bits])
+    out_b = after(out_b, a[bits[0]])
     rows_a = later(a)
     b = first(out_b, {})
     returned = []
@@ -331,7 +330,7 @@
         source = (out_a, out_b)[k // half]
         piece = source[(k % half) * CAP : (k % half + 1) * CAP]
         returned.append(swap(piece, "exp", k) if k else piece)
-    b[bits[-1]] = after(b[bits[-1]], *returned[half:])
+    b[bits[-1]] = after(b[bits[-1]], returned[half])
     rows_b = later(b)
     gram_rows = rows_a + rows_b
     scaling = EXPERTS_ALL / (TOPK * tok_count * owner_count * shard_count)

time: 73.2 us -> 70.3 us (0.960)
  waiting for transfers between devices: 28.5 us -> 26.7 us
  starting transfers between devices: 29.2 us -> 27.7 us
    ppermute x24, waiting for transfers between devices: 28.5 us -> 26.7 us  [swap(): return lax.ppermute(x, axis, [(i, i ^ k) for i in range(n)])]
    ppermute x24, starting transfers between devices: 29.2 us -> 27.7 us  [swap(): return lax.ppermute(x, axis, [(i, i ^ k) for i in range(n)])]
  transfers between devices with their start and end apart: 24 -> 24, of which waited for: 12 -> 11; matrix products, arithmetic and copies ran while one was open for 0% -> 0% of each run, Pallas kernels for 12% -> 13%
where the time goes in v4:
time: 70.3 us; the launch traced here: 69.9 us
  starting transfers between devices  27.7 us (39%)
  waiting for transfers between devices  26.7 us (38%)
  Pallas kernels  14.4 us (20%)
  between operations  0.76 us (1%)
    ppermute x24, starting transfers between devices, swap(): return lax.ppermute(x, axis, [(i, i ^ k) for i in range(n)])  27.7 us
    ppermute x24, waiting for transfers between devices, swap(): return lax.ppermute(x, axis, [(i, i ^ k) for i in range(n)])  26.7 us
    pallas_call x1, Pallas kernels, load(): pl.pallas_call(functools.partial(load_kernel, count), out_shape=[jax.Shap...  3.79 us
    pallas_call x1, Pallas kernels, gram(): pl.pallas_call(functools.partial(gram_kernel, count, scaling), out_shape=...  3.78 us
    pallas_call x2, Pallas kernels, expert(): pl.pallas_call(functools.partial(expert_kernel, count), out_shape=[jax.Sh...  3.72 us
    pallas_call x1, Pallas kernels, pack(): pl.pallas_call(functools.partial(pack_kernel, count), out_shape=[jax.Shap...  1.73 us
    pallas_call x1, Pallas kernels, combine(): pl.pallas_call(functools.partial(combine_kernel, count), out_shape=jax.Sh...  1.43 us
  transfers between devices with their start and end apart: 24, of which 11 were waited for; matrix products, arithmetic and copies ran while one was open for 0% of the time, Pallas kernels for 13%

profile of v4, /device:TPU:0, one launch (start us, length us, event | category | flops | bytes accessed | tf_op | source)
XLA Modules:
  0.0 69.9 jit_solution(9987380167280852200)
XLA Ops:
  0.6 1.7 %shard_map.86 = (bf16[8,4096]{1,0:T(8,128)(2,1)S(1)}, bf16[8,4096]{1,0:T(8,128)(2,1)S(1)}, bf16[8,4096]{1,0:T(8,128)(2,1)S(1)}, bf16[8,4096]{1,0:T(8,128)(2,1)S(1)}, bf16[96,128]{1,0:T(8,128)(2,1)S(1)}) custom-call(s32[1]{0:T(128)} %bitcast.place_ref, s32[4]{0:T(128)} %window_hbm.1, s32[8,128]{1,0:T(8,128)} %bitcast.4, f32[8,128]{1,0:T(8,128)} %bitcast.5, ...), custom_call_target="tpu_custom_call" | custom-call | flops 33554432 | bytes 2097152 | tf_op jit(solution)/shard_map/pallas_call | solution.py:109
  2.9 2.6 %collective-permute-start.3 = (bf16[8,4096]{1,0:T(8,128)(2,1)S(1)}, bf16[8,4096]{1,0:T(8,128)(2,1)S(1)}, u32[]{:S(2)}, u32[]{:S(2)}) collective-permute-start(bf16[8,4096]{1,0:T(8,128)(2,1)S(1)} %get-tuple-element.24), channel_id=1, source_target_pairs={{0,8},{4,12},{8,0},{12,4},{1,9},{5,13},{9,1},{13,5},{2,10},{6,14},... | collective-permute-start | bytes 196616 | tf_op jit(solution)/shard_map/ppermute | solution.py:25
  5.6 1.8 %collective-permute-start.1 = (bf16[16,4096]{1,0:T(8,128)(2,1)S(1)}, bf16[16,4096]{1,0:T(8,128)(2,1)S(1)}, u32[]{:S(2)}, u32[]{:S(2)}) collective-permute-start(bf16[16,4096]{1,0:T(8,128)(2,1)S(1)} %constant_dynamic-update-slice_fusion.refs_0_), channel_id=1, source_target_pairs={{0,1},{1,0},{2,3},{3,2},{4,5},{5,4},{6,7},{7,6},{8,9},{9,8},{10,11... | collective-permute-start | bytes 393224 | tf_op jit(solution)/shard_map/ppermute | solution.py:25
  7.4 2.6 %collective-permute-start.2 = (bf16[16,4096]{1,0:T(8,128)(2,1)S(1)}, bf16[16,4096]{1,0:T(8,128)(2,1)S(1)}, u32[]{:S(2)}, u32[]{:S(2)}) collective-permute-start(bf16[16,4096]{1,0:T(8,128)(2,1)S(1)} %constant_dynamic-update-slice_fusion.refs_0_), channel_id=1, source_target_pairs={{0,2},{1,3},{2,0},{3,1},{4,6},{5,7},{6,4},{7,5},{8,10},{9,11},{10,... | collective-permute-start | bytes 393224 | tf_op jit(solution)/shard_map/ppermute | solution.py:25
  10.1 3.8 %shard_map.87 = (bf16[1,4096,384]{2,1,0:T(8,128)(2,1)S(1)}, bf16[1,4096,384]{2,1,0:T(8,128)(2,1)S(1)}, bf16[1,384,4096]{2,1,0:T(8,128)(2,1)S(1)}) custom-call(bf16[1,4096,384]{2,1,0:T(8,128)(2,1)} %refs_0_.1, bf16[1,4096,384]{2,1,0:T(8,128)(2,1)} %refs_1_.1, bf16[1,384,4096]{2,1,0:T(8,128)(2,1)} %refs_2_.1, ...), custom_call_target="tpu_custom_call" | custom-call | bytes 18874368 | tf_op jit(solution)/shard_map/pallas_call | solution.py:146
  13.9 2.8 %collective-permute-done.2.refs_2_ = bf16[16,4096]{1,0:T(8,128)(2,1)S(1)} collective-permute-done((bf16[16,4096]{1,0:T(8,128)(2,1)S(1)}, bf16[16,4096]{1,0:T(8,128)(2,1)S(1)}, u32[]{:S(2)}, u32[]{:S(2)}) %collective-permute-start.2) | collective-permute-done | bytes 131104 | tf_op jit(solution)/shard_map/ppermute | solution.py:25
  17.0 2.7 %collective-permute-start.5 = (bf16[16,4096]{1,0:T(8,128)(2,1)S(1)}, bf16[16,4096]{1,0:T(8,128)(2,1)S(1)}, u32[]{:S(2)}, u32[]{:S(2)}) collective-permute-start(bf16[16,4096]{1,0:T(8,128)(2,1)S(1)} %collective-permute-done.2.refs_2_), channel_id=1, source_target_pairs={{0,1},{1,0},{2,3},{3,2},{4,5},{5,4},{6,7},{7,6},{8,9},{9,8},{10,11... | collective-permute-start | bytes 393224 | tf_op jit(solution)/shard_map/ppermute | solution.py:25
  19.7 4.3 %collective-permute-done.11.refs_2_ = bf16[16,4096]{1,0:T(8,128)(2,1)S(1)} collective-permute-done((bf16[16,4096]{1,0:T(8,128)(2,1)S(1)}, bf16[16,4096]{1,0:T(8,128)(2,1)S(1)}, u32[]{:S(2)}, u32[]{:S(2)}) %collective-permute-start.11) | collective-permute-done | bytes 131104 | tf_op jit(solution)/shard_map/ppermute | solution.py:25
  25.4 1.9 %shard_map.88 = (f32[16,4096]{1,0:T(8,128)S(1)}, bf16[16,4096]{1,0:T(8,128)(2,1)S(1)}, f32[16,4096]{1,0:T(8,128)S(1)}, bf16[16,4096]{1,0:T(8,128)(2,1)S(1)}) custom-call(bf16[16,4096]{1,0:T(8,128)(2,1)S(1)} %constant_dynamic-update-slice_fusion.refs_0_, bf16[16,4096]{1,0:T(8,128)(2,1)S(1)} %collective-permute-done.1.refs_1_, ...), custom_call_target="tpu_custom_call" | custom-call | flops 1207959552 | bytes 11010048 | tf_op jit(solution)/shard_map/pallas_call | solution.py:187
  29.3 1.4 %collective-permute-done.12.refs_3_ = bf16[16,4096]{1,0:T(8,128)(2,1)S(1)} collective-permute-done((bf16[16,4096]{1,0:T(8,128)(2,1)S(1)}, bf16[16,4096]{1,0:T(8,128)(2,1)S(1)}, u32[]{:S(2)}, u32[]{:S(2)}) %collective-permute-start.12) | collective-permute-done | bytes 131104 | tf_op jit(solution)/shard_map/ppermute | solution.py:25
  30.8 1.9 %shard_map.89 = (f32[16,4096]{1,0:T(8,128)S(1)}, bf16[16,4096]{1,0:T(8,128)(2,1)S(1)}, f32[16,4096]{1,0:T(8,128)S(1)}, bf16[16,4096]{1,0:T(8,128)(2,1)S(1)}) custom-call(bf16[16,4096]{1,0:T(8,128)(2,1)S(1)} %constant_dynamic-update-slice_fusion.2.refs_3_.refs_0_, bf16[16,4096]{1,0:T(8,128)(2,1)S(1)} %collective-permute-done.10.refs_1_, ...), custom_call_target="tpu_custom_call" | custom-call | flops 1207959552 | bytes 11010048 | tf_op jit(solution)/shard_map/pallas_call | solution.py:187
  33.8 2.0 %collective-permute-start.8 = (bf16[16,4096]{1,0:T(8,128)(2,1)S(1)}, bf16[16,4096]{1,0:T(8,128)(2,1)S(1)}, u32[]{:S(2)}, u32[]{:S(2)}) collective-permute-start(bf16[16,4096]{1,0:T(8,128)(2,1)S(1)} %add_convert_fusion.3), channel_id=1, source_target_pairs={{0,2},{1,3},{2,0},{3,1},{4,6},{5,7},{6,4},{7,5},{8,10},{9,11},{10,... | collective-permute-start | bytes 393224 | tf_op jit(solution)/shard_map/ppermute | solution.py:25
  35.7 1.6 %collective-permute-start.13 = (bf16[16,4096]{1,0:T(8,128)(2,1)S(1)}, bf16[16,4096]{1,0:T(8,128)(2,1)S(1)}, u32[]{:S(2)}, u32[]{:S(2)}) collective-permute-start(bf16[16,4096]{1,0:T(8,128)(2,1)S(1)} %get-tuple-element.36), channel_id=1, source_target_pairs={{0,1},{1,0},{2,3},{3,2},{4,5},{5,4},{6,7},{7,6},{8,9},{9,8},{10,11... | collective-permute-start | bytes 393224 | tf_op jit(solution)/shard_map/ppermute | solution.py:25
  37.3 5.5 %collective-permute-done.14 = bf16[16,4096]{1,0:T(8,128)(2,1)S(1)} collective-permute-done((bf16[16,4096]{1,0:T(8,128)(2,1)S(1)}, bf16[16,4096]{1,0:T(8,128)(2,1)S(1)}, u32[]{:S(2)}, u32[]{:S(2)}) %collective-permute-start.14) | collective-permute-done | bytes 131104 | tf_op jit(solution)/shard_map/ppermute | solution.py:25
  43.2 3.2 %collective-permute-start.16 = (bf16[16,4096]{1,0:T(8,128)(2,1)S(1)}, bf16[16,4096]{1,0:T(8,128)(2,1)S(1)}, u32[]{:S(2)}, u32[]{:S(2)}) collective-permute-start(bf16[16,4096]{1,0:T(8,128)(2,1)S(1)} %add_convert_fusion.2.refs_0_), channel_id=1, source_target_pairs={{0,1},{1,0},{2,3},{3,2},{4,5},{5,4},{6,7},{7,6},{8,9},{9,8},{10,11... | collective-permute-start | bytes 393224 | tf_op jit(solution)/shard_map/ppermute | solution.py:25
  46.5 1.5 %collective-permute-done.13 = bf16[16,4096]{1,0:T(8,128)(2,1)S(1)} collective-permute-done((bf16[16,4096]{1,0:T(8,128)(2,1)S(1)}, bf16[16,4096]{1,0:T(8,128)(2,1)S(1)}, u32[]{:S(2)}, u32[]{:S(2)}) %collective-permute-start.13) | collective-permute-done | bytes 131104 | tf_op jit(solution)/shard_map/ppermute | solution.py:25
  48.0 3.6 %collective-permute-done.15 = bf16[16,4096]{1,0:T(8,128)(2,1)S(1)} collective-permute-done((bf16[16,4096]{1,0:T(8,128)(2,1)S(1)}, bf16[16,4096]{1,0:T(8,128)(2,1)S(1)}, u32[]{:S(2)}, u32[]{:S(2)}) %collective-permute-start.15) | collective-permute-done | bytes 131104 | tf_op jit(solution)/shard_map/ppermute | solution.py:25
  52.5 1.6 %collective-permute-start.17 = (bf16[8,4096]{1,0:T(8,128)(2,1)S(1)}, bf16[8,4096]{1,0:T(8,128)(2,1)S(1)}, u32[]{:S(2)}, u32[]{:S(2)}) collective-permute-start(bf16[8,4096]{1,0:T(8,128)(2,1)S(1)} %get-tuple-element.43), channel_id=1, source_target_pairs={{0,8},{4,12},{8,0},{12,4},{1,9},{5,13},{9,1},{13,5},{2,10},{6,14},... | collective-permute-start | bytes 196616 | tf_op jit(solution)/shard_map/ppermute | solution.py:25
  54.0 1.8 %collective-permute-start.21 = (bf16[16,4096]{1,0:T(8,128)(2,1)S(1)}, bf16[16,4096]{1,0:T(8,128)(2,1)S(1)}, u32[]{:S(2)}, u32[]{:S(2)}) collective-permute-start(bf16[16,4096]{1,0:T(8,128)(2,1)S(1)} %add_convert_fusion.refs_4_), channel_id=1, source_target_pairs={{0,1},{1,0},{2,3},{3,2},{4,5},{5,4},{6,7},{7,6},{8,9},{9,8},{10,11... | collective-permute-start | bytes 393224 | tf_op jit(solution)/shard_map/ppermute | solution.py:25
  55.8 2.8 %collective-permute-done.19.refs_2_ = bf16[16,4096]{1,0:T(8,128)(2,1)S(1)} collective-permute-done((bf16[16,4096]{1,0:T(8,128)(2,1)S(1)}, bf16[16,4096]{1,0:T(8,128)(2,1)S(1)}, u32[]{:S(2)}, u32[]{:S(2)}) %collective-permute-start.19) | collective-permute-done | bytes 131104 | tf_op jit(solution)/shard_map/ppermute | solution.py:25
  60.7 1.6 %collective-permute-start.18 = (bf16[8,4096]{1,0:T(8,128)(2,1)S(1)}, bf16[8,4096]{1,0:T(8,128)(2,1)S(1)}, u32[]{:S(2)}, u32[]{:S(2)}) collective-permute-start(bf16[8,4096]{1,0:T(8,128)(2,1)S(1)} %get-tuple-element.42), channel_id=1, source_target_pairs={{0,12},{4,8},{8,4},{12,0},{1,13},{5,9},{9,5},{13,1},{2,14},{6,10},... | collective-permute-start | bytes 196616 | tf_op jit(solution)/shard_map/ppermute | solution.py:25
  62.4 2.3 %collective-permute-done.18.refs_3_ = bf16[8,4096]{1,0:T(8,128)(2,1)S(1)} collective-permute-done((bf16[8,4096]{1,0:T(8,128)(2,1)S(1)}, bf16[8,4096]{1,0:T(8,128)(2,1)S(1)}, u32[]{:S(2)}, u32[]{:S(2)}) %collective-permute-start.18) | collective-permute-done | bytes 65568 | tf_op jit(solution)/shard_map/ppermute | solution.py:25
  64.6 1.4 %shard_map.90 = bf16[128,4096]{1,0:T(8,128)(2,1)} custom-call(bf16[8,4096]{1,0:T(8,128)(2,1)S(1)} %get-tuple-element.45.refs_0_, bf16[8,4096]{1,0:T(8,128)(2,1)S(1)} %collective-permute-done.9.refs_1_, bf16[8,4096]{1,0:T(8,128)(2,1)S(1)} %collective-permute-done.17.refs_2_, bf16[8,4096]{1,0:T(8,128)(2,1)S(1)} %collective-permute-done.18.refs_3_, ...), custom_call_target="tpu_custom_call" | custom-call | flops 100663296 | bytes 2097152 | tf_op jit(solution)/shard_map/pallas_call | solution.py:224
  66.1 3.8 %shard_map.91 = bf16[1,4096,1024]{2,1,0:T(8,128)(2,1)} custom-call(s32[1]{0:T(128)} %bitcast.3.place_ref, bf16[16,4096]{1,0:T(8,128)(2,1)S(1)} %add_convert_fusion.2.refs_0_, bf16[16,4096]{1,0:T(8,128)(2,1)S(1)} %collective-permute-done.16.refs_1_, bf16[16,4096]{1,0:T(8,128)(2,1)S(1)} %collective-permute-done.19.refs_2_, ...), custom_call_target="tpu_custom_call" | custom-call | flops 1073741824 | bytes 9437184 | tf_op jit(solution)/shard_map/pallas_call | solution.py:268
  (40 shorter events, 8.9 us)
Async XLA Ops:
  2.4 3.2 %collective-permute-start = (bf16[8,4096]{1,0:T(8,128)(2,1)S(1)}, bf16[8,4096]{1,0:T(8,128)(2,1)S(1)}, u32[]{:S(2)}, u32[]{:S(2)}) collective-permute-start(bf16[8,4096]{1,0:T(8,128)(2,1)S(1)} %get-tuple-element.23), channel_id=1, source_target_pairs={{0,4},{4,0},{8,12},{12,8},{1,5},{5,1},{9,13},{13,9},{2,6},{6,2},{1... | collective-permute-start | bytes 196616 | tf_op jit(solution)/shard_map/ppermute | solution.py:25
  2.9 7.1 %collective-permute-start.3 = (bf16[8,4096]{1,0:T(8,128)(2,1)S(1)}, bf16[8,4096]{1,0:T(8,128)(2,1)S(1)}, u32[]{:S(2)}, u32[]{:S(2)}) collective-permute-start(bf16[8,4096]{1,0:T(8,128)(2,1)S(1)} %get-tuple-element.24), channel_id=1, source_target_pairs={{0,8},{4,12},{8,0},{12,4},{1,9},{5,13},{9,1},{13,5},{2,10},{6,14},... | collective-permute-start | bytes 196616 | tf_op jit(solution)/shard_map/ppermute | solution.py:25
  5.5 4.5 %collective-permute-start.4 = (bf16[8,4096]{1,0:T(8,128)(2,1)S(1)}, bf16[8,4096]{1,0:T(8,128)(2,1)S(1)}, u32[]{:S(2)}, u32[]{:S(2)}) collective-permute-start(bf16[8,4096]{1,0:T(8,128)(2,1)S(1)} %get-tuple-element.25), channel_id=1, source_target_pairs={{0,12},{4,8},{8,4},{12,0},{1,13},{5,9},{9,5},{13,1},{2,14},{6,10},... | collective-permute-start | bytes 196616 | tf_op jit(solution)/shard_map/ppermute | solution.py:25
  5.6 11.1 %collective-permute-start.1 = (bf16[16,4096]{1,0:T(8,128)(2,1)S(1)}, bf16[16,4096]{1,0:T(8,128)(2,1)S(1)}, u32[]{:S(2)}, u32[]{:S(2)}) collective-permute-start(bf16[16,4096]{1,0:T(8,128)(2,1)S(1)} %constant_dynamic-update-slice_fusion.refs_0_), channel_id=1, source_target_pairs={{0,1},{1,0},{2,3},{3,2},{4,5},{5,4},{6,7},{7,6},{8,9},{9,8},{10,11... | collective-permute-start | bytes 393224 | tf_op jit(solution)/shard_map/ppermute | solution.py:25
  7.4 9.2 %collective-permute-start.2 = (bf16[16,4096]{1,0:T(8,128)(2,1)S(1)}, bf16[16,4096]{1,0:T(8,128)(2,1)S(1)}, u32[]{:S(2)}, u32[]{:S(2)}) collective-permute-start(bf16[16,4096]{1,0:T(8,128)(2,1)S(1)} %constant_dynamic-update-slice_fusion.refs_0_), channel_id=1, source_target_pairs={{0,2},{1,3},{2,0},{3,1},{4,6},{5,7},{6,4},{7,5},{8,10},{9,11},{10,... | collective-permute-start | bytes 393224 | tf_op jit(solution)/shard_map/ppermute | solution.py:25
  16.7 7.3 %collective-permute-start.11 = (bf16[16,4096]{1,0:T(8,128)(2,1)S(1)}, bf16[16,4096]{1,0:T(8,128)(2,1)S(1)}, u32[]{:S(2)}, u32[]{:S(2)}) collective-permute-start(bf16[16,4096]{1,0:T(8,128)(2,1)S(1)} %constant_dynamic-update-slice_fusion.2.refs_3_.refs_0_), channel_id=1, source_target_pairs={{0,2},{1,3},{2,0},{3,1},{4,6},{5,7},{6,4},{7,5},{8,10},{9,11},{10,... | collective-permute-start | bytes 393224 | tf_op jit(solution)/shard_map/ppermute | solution.py:25
  17.0 8.4 %collective-permute-start.5 = (bf16[16,4096]{1,0:T(8,128)(2,1)S(1)}, bf16[16,4096]{1,0:T(8,128)(2,1)S(1)}, u32[]{:S(2)}, u32[]{:S(2)}) collective-permute-start(bf16[16,4096]{1,0:T(8,128)(2,1)S(1)} %collective-permute-done.2.refs_2_), channel_id=1, source_target_pairs={{0,1},{1,0},{2,3},{3,2},{4,5},{5,4},{6,7},{7,6},{8,9},{9,8},{10,11... | collective-permute-start | bytes 393224 | tf_op jit(solution)/shard_map/ppermute | solution.py:25
  19.7 9.7 %collective-permute-start.10 = (bf16[16,4096]{1,0:T(8,128)(2,1)S(1)}, bf16[16,4096]{1,0:T(8,128)(2,1)S(1)}, u32[]{:S(2)}, u32[]{:S(2)}) collective-permute-start(bf16[16,4096]{1,0:T(8,128)(2,1)S(1)} %constant_dynamic-update-slice_fusion.2.refs_3_.refs_0_), channel_id=1, source_target_pairs={{0,1},{1,0},{2,3},{3,2},{4,5},{5,4},{6,7},{7,6},{8,9},{9,8},{10,11... | collective-permute-start | bytes 393224 | tf_op jit(solution)/shard_map/ppermute | solution.py:25
  24.0 6.8 %collective-permute-start.12 = (bf16[16,4096]{1,0:T(8,128)(2,1)S(1)}, bf16[16,4096]{1,0:T(8,128)(2,1)S(1)}, u32[]{:S(2)}, u32[]{:S(2)}) collective-permute-start(bf16[16,4096]{1,0:T(8,128)(2,1)S(1)} %collective-permute-done.11.refs_2_), channel_id=1, source_target_pairs={{0,1},{1,0},{2,3},{3,2},{4,5},{5,4},{6,7},{7,6},{8,9},{9,8},{10,11... | collective-permute-start | bytes 393224 | tf_op jit(solution)/shard_map/ppermute | solution.py:25
  27.3 6.5 %collective-permute-start.7 = (bf16[16,4096]{1,0:T(8,128)(2,1)S(1)}, bf16[16,4096]{1,0:T(8,128)(2,1)S(1)}, u32[]{:S(2)}, u32[]{:S(2)}) collective-permute-start(bf16[16,4096]{1,0:T(8,128)(2,1)S(1)} %get-tuple-element.33), channel_id=1, source_target_pairs={{0,1},{1,0},{2,3},{3,2},{4,5},{5,4},{6,7},{7,6},{8,9},{9,8},{10,11... | collective-permute-start | bytes 393224 | tf_op jit(solution)/shard_map/ppermute | solution.py:25
  28.1 15.1 %collective-permute-start.6 = (bf16[16,4096]{1,0:T(8,128)(2,1)S(1)}, bf16[16,4096]{1,0:T(8,128)(2,1)S(1)}, u32[]{:S(2)}, u32[]{:S(2)}) collective-permute-start(bf16[16,4096]{1,0:T(8,128)(2,1)S(1)} %get-tuple-element.31), channel_id=1, source_target_pairs={{0,1},{1,0},{2,3},{3,2},{4,5},{5,4},{6,7},{7,6},{8,9},{9,8},{10,11... | collective-permute-start | bytes 393224 | tf_op jit(solution)/shard_map/ppermute | solution.py:25
  32.7 10.1 %collective-permute-start.14 = (bf16[16,4096]{1,0:T(8,128)(2,1)S(1)}, bf16[16,4096]{1,0:T(8,128)(2,1)S(1)}, u32[]{:S(2)}, u32[]{:S(2)}) collective-permute-start(bf16[16,4096]{1,0:T(8,128)(2,1)S(1)} %get-tuple-element.38), channel_id=1, source_target_pairs={{0,1},{1,0},{2,3},{3,2},{4,5},{5,4},{6,7},{7,6},{8,9},{9,8},{10,11... | collective-permute-start | bytes 393224 | tf_op jit(solution)/shard_map/ppermute | solution.py:25
  33.8 9.4 %collective-permute-start.8 = (bf16[16,4096]{1,0:T(8,128)(2,1)S(1)}, bf16[16,4096]{1,0:T(8,128)(2,1)S(1)}, u32[]{:S(2)}, u32[]{:S(2)}) collective-permute-start(bf16[16,4096]{1,0:T(8,128)(2,1)S(1)} %add_convert_fusion.3), channel_id=1, source_target_pairs={{0,2},{1,3},{2,0},{3,1},{4,6},{5,7},{6,4},{7,5},{8,10},{9,11},{10,... | collective-permute-start | bytes 393224 | tf_op jit(solution)/shard_map/ppermute | solution.py:25
  35.7 12.2 %collective-permute-start.13 = (bf16[16,4096]{1,0:T(8,128)(2,1)S(1)}, bf16[16,4096]{1,0:T(8,128)(2,1)S(1)}, u32[]{:S(2)}, u32[]{:S(2)}) collective-permute-start(bf16[16,4096]{1,0:T(8,128)(2,1)S(1)} %get-tuple-element.36), channel_id=1, source_target_pairs={{0,1},{1,0},{2,3},{3,2},{4,5},{5,4},{6,7},{7,6},{8,9},{9,8},{10,11... | collective-permute-start | bytes 393224 | tf_op jit(solution)/shard_map/ppermute | solution.py:25
  42.8 8.8 %collective-permute-start.15 = (bf16[16,4096]{1,0:T(8,128)(2,1)S(1)}, bf16[16,4096]{1,0:T(8,128)(2,1)S(1)}, u32[]{:S(2)}, u32[]{:S(2)}) collective-permute-start(bf16[16,4096]{1,0:T(8,128)(2,1)S(1)} %add_convert_fusion.1), channel_id=1, source_target_pairs={{0,2},{1,3},{2,0},{3,1},{4,6},{5,7},{6,4},{7,5},{8,10},{9,11},{10,... | collective-permute-start | bytes 393224 | tf_op jit(solution)/shard_map/ppermute | solution.py:25
  43.2 8.5 %collective-permute-start.16 = (bf16[16,4096]{1,0:T(8,128)(2,1)S(1)}, bf16[16,4096]{1,0:T(8,128)(2,1)S(1)}, u32[]{:S(2)}, u32[]{:S(2)}) collective-permute-start(bf16[16,4096]{1,0:T(8,128)(2,1)S(1)} %add_convert_fusion.2.refs_0_), channel_id=1, source_target_pairs={{0,1},{1,0},{2,3},{3,2},{4,5},{5,4},{6,7},{7,6},{8,9},{9,8},{10,11... | collective-permute-start | bytes 393224 | tf_op jit(solution)/shard_map/ppermute | solution.py:25
  46.4 12.2 %collective-permute-start.19 = (bf16[16,4096]{1,0:T(8,128)(2,1)S(1)}, bf16[16,4096]{1,0:T(8,128)(2,1)S(1)}, u32[]{:S(2)}, u32[]{:S(2)}) collective-permute-start(bf16[16,4096]{1,0:T(8,128)(2,1)S(1)} %add_convert_fusion.2.refs_0_), channel_id=1, source_target_pairs={{0,2},{1,3},{2,0},{3,1},{4,6},{5,7},{6,4},{7,5},{8,10},{9,11},{10,... | collective-permute-start | bytes 393224 | tf_op jit(solution)/shard_map/ppermute | solution.py:25
  51.7 8.4 %collective-permute-start.22 = (bf16[16,4096]{1,0:T(8,128)(2,1)S(1)}, bf16[16,4096]{1,0:T(8,128)(2,1)S(1)}, u32[]{:S(2)}, u32[]{:S(2)}) collective-permute-start(bf16[16,4096]{1,0:T(8,128)(2,1)S(1)} %add_convert_fusion.refs_4_), channel_id=1, source_target_pairs={{0,2},{1,3},{2,0},{3,1},{4,6},{5,7},{6,4},{7,5},{8,10},{9,11},{10,... | collective-permute-start | bytes 393224 | tf_op jit(solution)/shard_map/ppermute | solution.py:25
  52.5 6.2 %collective-permute-start.17 = (bf16[8,4096]{1,0:T(8,128)(2,1)S(1)}, bf16[8,4096]{1,0:T(8,128)(2,1)S(1)}, u32[]{:S(2)}, u32[]{:S(2)}) collective-permute-start(bf16[8,4096]{1,0:T(8,128)(2,1)S(1)} %get-tuple-element.43), channel_id=1, source_target_pairs={{0,8},{4,12},{8,0},{12,4},{1,9},{5,13},{9,1},{13,5},{2,10},{6,14},... | collective-permute-start | bytes 196616 | tf_op jit(solution)/shard_map/ppermute | solution.py:25
  54.0 12.0 %collective-permute-start.21 = (bf16[16,4096]{1,0:T(8,128)(2,1)S(1)}, bf16[16,4096]{1,0:T(8,128)(2,1)S(1)}, u32[]{:S(2)}, u32[]{:S(2)}) collective-permute-start(bf16[16,4096]{1,0:T(8,128)(2,1)S(1)} %add_convert_fusion.refs_4_), channel_id=1, source_target_pairs={{0,1},{1,0},{2,3},{3,2},{4,5},{5,4},{6,7},{7,6},{8,9},{9,8},{10,11... | collective-permute-start | bytes 393224 | tf_op jit(solution)/shard_map/ppermute | solution.py:25
  58.6 7.4 %collective-permute-start.20 = (bf16[16,4096]{1,0:T(8,128)(2,1)S(1)}, bf16[16,4096]{1,0:T(8,128)(2,1)S(1)}, u32[]{:S(2)}, u32[]{:S(2)}) collective-permute-start(bf16[16,4096]{1,0:T(8,128)(2,1)S(1)} %collective-permute-done.19.refs_2_), channel_id=1, source_target_pairs={{0,1},{1,0},{2,3},{3,2},{4,5},{5,4},{6,7},{7,6},{8,9},{9,8},{10,11... | collective-permute-start | bytes 393224 | tf_op jit(solution)/shard_map/ppermute | solution.py:25
  60.1 6.0 %collective-permute-start.23 = (bf16[16,4096]{1,0:T(8,128)(2,1)S(1)}, bf16[16,4096]{1,0:T(8,128)(2,1)S(1)}, u32[]{:S(2)}, u32[]{:S(2)}) collective-permute-start(bf16[16,4096]{1,0:T(8,128)(2,1)S(1)} %collective-permute-done.22.refs_6_), channel_id=1, source_target_pairs={{0,1},{1,0},{2,3},{3,2},{4,5},{5,4},{6,7},{7,6},{8,9},{9,8},{10,11... | collective-permute-start | bytes 393224 | tf_op jit(solution)/shard_map/ppermute | solution.py:25
  60.7 1.7 %collective-permute-start.9 = (bf16[8,4096]{1,0:T(8,128)(2,1)S(1)}, bf16[8,4096]{1,0:T(8,128)(2,1)S(1)}, u32[]{:S(2)}, u32[]{:S(2)}) collective-permute-start(bf16[8,4096]{1,0:T(8,128)(2,1)S(1)} %get-tuple-element.44), channel_id=1, source_target_pairs={{0,4},{4,0},{8,12},{12,8},{1,5},{5,1},{9,13},{13,9},{2,6},{6,2},{1... | collective-permute-start | bytes 196616 | tf_op jit(solution)/shard_map/ppermute | solution.py:25
  60.7 3.9 %collective-permute-start.18 = (bf16[8,4096]{1,0:T(8,128)(2,1)S(1)}, bf16[8,4096]{1,0:T(8,128)(2,1)S(1)}, u32[]{:S(2)}, u32[]{:S(2)}) collective-permute-start(bf16[8,4096]{1,0:T(8,128)(2,1)S(1)} %get-tuple-element.42), channel_id=1, source_target_pairs={{0,12},{4,8},{8,4},{12,0},{1,13},{5,9},{9,5},{13,1},{2,14},{6,10},... | collective-permute-start | bytes 196616 | tf_op jit(solution)/shard_map/ppermute | solution.py:25

commit v5 on v4

--- a/solution.py
+++ b/solution.py
@@ -202,30 +202,37 @@
 
 
 def combine_kernel(count, *refs):
-    rows, weighted_ref, out_ref = refs[:count], refs[count], refs[count + 1]
-    weighted = weighted_ref[...]
-    width = out_ref.shape[1]
-    step = 1024
-    for start in range(0, width, step):
-        part = slice(start, start + step)
+    rows, weighted_ref = refs[:count], refs[count]
+    out_hbm, buffer, sems = refs[count + 1 :]
+    weighted = weighted_ref[...].T
+    steps, width = buffer.shape[0], buffer.shape[2]
+    copies = []
+    for i in range(steps):
+        part = slice(i * width, (i + 1) * width)
         x = jnp.concatenate([r[:, part] for r in rows], axis=0)
-        out_ref[:, part] = lax.dot_general(
-            weighted,
-            jnp.concatenate([x, x, x], axis=0),
-            (((0,), (0,)), ((), ())),
-            preferred_element_type=jnp.float32,
-        ).astype(out_ref.dtype)
+        buffer[i] = jnp.dot(
+            weighted, jnp.concatenate([x, x, x], axis=0), preferred_element_type=jnp.float32
+        ).astype(buffer.dtype)
+        copies.append(pltpu.make_async_copy(buffer.at[i], out_hbm.at[:, part], sems.at[i]))
+        copies[-1].start()
+    for copy in copies:
+        copy.wait()
 
 
 def combine(rows, weighted):
     count = len(rows)
     width = rows[0].shape[1]
     tok_count = weighted.shape[1]
+    step = 1024
     return pl.pallas_call(
         functools.partial(combine_kernel, count),
         out_shape=jax.ShapeDtypeStruct((tok_count, width), jnp.bfloat16),
         in_specs=[VMEM] * (count + 1),
-        out_specs=VMEM,
+        out_specs=HBM,
+        scratch_shapes=[
+            pltpu.VMEM((width // step, tok_count, step), jnp.bfloat16),
+            pltpu.SemaphoreType.DMA((width // step,)),
+        ],
         compiler_params=pltpu.CompilerParams(vmem_limit_bytes=8 * MIB),
         cost_estimate=pl.CostEstimate(
             flops=2 * weighted.shape[0] * tok_count * width,
@@ -237,18 +244,18 @@
 
 def gram_kernel(count, scaling, place_ref, *refs):
     blocks = refs[:count]
-    out_hbm, all_ref, own_ref, buffer, sems = refs[count:]
+    out_hbm, own_ref, buffer, sems = refs[count:]
     own = blocks[0].shape[0]
+    width = own_ref.shape[1]
+    columns = pl.ds(pl.multiple_of(place_ref[0] * width, width), width)
     for r in range(count):
-        all_ref[r * own : (r + 1) * own, :] = blocks[r][...]
-    width = own_ref.shape[1]
-    own_ref[...] = all_ref[:, pl.ds(pl.multiple_of(place_ref[0] * width, width), width)]
+        own_ref[r * own : (r + 1) * own, :] = blocks[r][:, columns]
     steps, height = buffer.shape[:2]
     copies = []
     for i in range(steps):
         part = slice(i * height, (i + 1) * height)
         product = lax.dot_general(
-            all_ref[:, part],
+            jnp.concatenate([block[:, part] for block in blocks], axis=0),
             own_ref[...],
             (((0,), (0,)), ((), ())),
             preferred_element_type=jnp.float32,
@@ -271,7 +278,6 @@
         in_specs=[SMEM] + [VMEM] * count,
         out_specs=HBM,
         scratch_shapes=[
-            pltpu.VMEM((count * own, width), jnp.bfloat16),
             pltpu.VMEM((count * own, col_width), jnp.bfloat16),
             pltpu.VMEM((steps, height, col_width), jnp.bfloat16),
             pltpu.SemaphoreType.DMA((steps,)),
@@ -335,7 +341,7 @@
     gram_rows = rows_a + rows_b
     scaling = EXPERTS_ALL / (TOPK * tok_count * owner_count * shard_count)
     gram_out = gram(dp_place, gram_rows, feat_width // shard_count, scaling)
-    combined = combine(returned, weighted)
+    combined = combine([after(returned[0], b[bits[-1]], rows_a[1])] + returned[1:], weighted)
     return (combined, gram_out)
 
 

time: 70.3 us -> 70.1 us (level)
  no operation moved by 1% of the time
where the time goes in v5:
time: 70.1 us; the launch traced here: 69.7 us
  starting transfers between devices  27.7 us (40%)
  waiting for transfers between devices  26.7 us (38%)
  Pallas kernels  14.2 us (20%)
  between operations  0.78 us (1%)
    ppermute x24, starting transfers between devices, swap(): return lax.ppermute(x, axis, [(i, i ^ k) for i in range(n)])  27.7 us
    ppermute x24, waiting for transfers between devices, swap(): return lax.ppermute(x, axis, [(i, i ^ k) for i in range(n)])  26.7 us
    pallas_call x1, Pallas kernels, load(): pl.pallas_call(functools.partial(load_kernel, count), out_shape=[jax.Shap...  3.79 us
    pallas_call x1, Pallas kernels, gram(): pl.pallas_call(functools.partial(gram_kernel, count, scaling), out_shape=...  3.74 us
    pallas_call x2, Pallas kernels, expert(): pl.pallas_call(functools.partial(expert_kernel, count), out_shape=[jax.Sh...  3.72 us
    pallas_call x1, Pallas kernels, pack(): pl.pallas_call(functools.partial(pack_kernel, count), out_shape=[jax.Shap...  1.73 us
  transfers between devices with their start and end apart: 24, of which 11 were waited for; matrix products, arithmetic and copies ran while one was open for 0% of the time, Pallas kernels for 13%

profile of v5, /device:TPU:0, one launch (start us, length us, event | category | flops | bytes accessed | tf_op | source)
XLA Modules:
  0.0 69.7 jit_solution(558158927344451168)
XLA Ops:
  0.6 1.7 %shard_map.86 = (bf16[8,4096]{1,0:T(8,128)(2,1)S(1)}, bf16[8,4096]{1,0:T(8,128)(2,1)S(1)}, bf16[8,4096]{1,0:T(8,128)(2,1)S(1)}, bf16[8,4096]{1,0:T(8,128)(2,1)S(1)}, bf16[96,128]{1,0:T(8,128)(2,1)S(1)}) custom-call(s32[1]{0:T(128)} %bitcast.place_ref, s32[4]{0:T(128)} %window_hbm.1, s32[8,128]{1,0:T(8,128)} %bitcast.4, f32[8,128]{1,0:T(8,128)} %bitcast.5, ...), custom_call_target="tpu_custom_call" | custom-call | flops 33554432 | bytes 2097152 | tf_op jit(solution)/shard_map/pallas_call | solution.py:109
  2.9 2.6 %collective-permute-start.3 = (bf16[8,4096]{1,0:T(8,128)(2,1)S(1)}, bf16[8,4096]{1,0:T(8,128)(2,1)S(1)}, u32[]{:S(2)}, u32[]{:S(2)}) collective-permute-start(bf16[8,4096]{1,0:T(8,128)(2,1)S(1)} %get-tuple-element.25), channel_id=1, source_target_pairs={{0,8},{4,12},{8,0},{12,4},{1,9},{5,13},{9,1},{13,5},{2,10},{6,14},... | collective-permute-start | bytes 196616 | tf_op jit(solution)/shard_map/ppermute | solution.py:25
  5.6 1.8 %collective-permute-start.1 = (bf16[16,4096]{1,0:T(8,128)(2,1)S(1)}, bf16[16,4096]{1,0:T(8,128)(2,1)S(1)}, u32[]{:S(2)}, u32[]{:S(2)}) collective-permute-start(bf16[16,4096]{1,0:T(8,128)(2,1)S(1)} %constant_dynamic-update-slice_fusion.refs_0_), channel_id=1, source_target_pairs={{0,1},{1,0},{2,3},{3,2},{4,5},{5,4},{6,7},{7,6},{8,9},{9,8},{10,11... | collective-permute-start | bytes 393224 | tf_op jit(solution)/shard_map/ppermute | solution.py:25
  7.4 2.6 %collective-permute-start.2 = (bf16[16,4096]{1,0:T(8,128)(2,1)S(1)}, bf16[16,4096]{1,0:T(8,128)(2,1)S(1)}, u32[]{:S(2)}, u32[]{:S(2)}) collective-permute-start(bf16[16,4096]{1,0:T(8,128)(2,1)S(1)} %constant_dynamic-update-slice_fusion.refs_0_), channel_id=1, source_target_pairs={{0,2},{1,3},{2,0},{3,1},{4,6},{5,7},{6,4},{7,5},{8,10},{9,11},{10,... | collective-permute-start | bytes 393224 | tf_op jit(solution)/shard_map/ppermute | solution.py:25
  10.1 3.8 %shard_map.87 = (bf16[1,4096,384]{2,1,0:T(8,128)(2,1)S(1)}, bf16[1,4096,384]{2,1,0:T(8,128)(2,1)S(1)}, bf16[1,384,4096]{2,1,0:T(8,128)(2,1)S(1)}) custom-call(bf16[1,4096,384]{2,1,0:T(8,128)(2,1)} %refs_0_.1, bf16[1,4096,384]{2,1,0:T(8,128)(2,1)} %refs_1_.1, bf16[1,384,4096]{2,1,0:T(8,128)(2,1)} %refs_2_.1, ...), custom_call_target="tpu_custom_call" | custom-call | bytes 18874368 | tf_op jit(solution)/shard_map/pallas_call | solution.py:146
  13.9 2.8 %collective-permute-done.2.refs_2_ = bf16[16,4096]{1,0:T(8,128)(2,1)S(1)} collective-permute-done((bf16[16,4096]{1,0:T(8,128)(2,1)S(1)}, bf16[16,4096]{1,0:T(8,128)(2,1)S(1)}, u32[]{:S(2)}, u32[]{:S(2)}) %collective-permute-start.2) | collective-permute-done | bytes 131104 | tf_op jit(solution)/shard_map/ppermute | solution.py:25
  17.0 2.7 %collective-permute-start.5 = (bf16[16,4096]{1,0:T(8,128)(2,1)S(1)}, bf16[16,4096]{1,0:T(8,128)(2,1)S(1)}, u32[]{:S(2)}, u32[]{:S(2)}) collective-permute-start(bf16[16,4096]{1,0:T(8,128)(2,1)S(1)} %collective-permute-done.2.refs_2_), channel_id=1, source_target_pairs={{0,1},{1,0},{2,3},{3,2},{4,5},{5,4},{6,7},{7,6},{8,9},{9,8},{10,11... | collective-permute-start | bytes 393224 | tf_op jit(solution)/shard_map/ppermute | solution.py:25
  19.7 4.3 %collective-permute-done.10.refs_2_ = bf16[16,4096]{1,0:T(8,128)(2,1)S(1)} collective-permute-done((bf16[16,4096]{1,0:T(8,128)(2,1)S(1)}, bf16[16,4096]{1,0:T(8,128)(2,1)S(1)}, u32[]{:S(2)}, u32[]{:S(2)}) %collective-permute-start.10) | collective-permute-done | bytes 131104 | tf_op jit(solution)/shard_map/ppermute | solution.py:25
  25.4 1.9 %shard_map.88 = (f32[16,4096]{1,0:T(8,128)S(1)}, bf16[16,4096]{1,0:T(8,128)(2,1)S(1)}, f32[16,4096]{1,0:T(8,128)S(1)}, bf16[16,4096]{1,0:T(8,128)(2,1)S(1)}) custom-call(bf16[16,4096]{1,0:T(8,128)(2,1)S(1)} %constant_dynamic-update-slice_fusion.refs_0_, bf16[16,4096]{1,0:T(8,128)(2,1)S(1)} %collective-permute-done.1.refs_1_, ...), custom_call_target="tpu_custom_call" | custom-call | flops 1207959552 | bytes 11010048 | tf_op jit(solution)/shard_map/pallas_call | solution.py:187
  29.3 1.4 %collective-permute-done.11.refs_3_ = bf16[16,4096]{1,0:T(8,128)(2,1)S(1)} collective-permute-done((bf16[16,4096]{1,0:T(8,128)(2,1)S(1)}, bf16[16,4096]{1,0:T(8,128)(2,1)S(1)}, u32[]{:S(2)}, u32[]{:S(2)}) %collective-permute-start.11) | collective-permute-done | bytes 131104 | tf_op jit(solution)/shard_map/ppermute | solution.py:25
  30.8 1.9 %shard_map.89 = (f32[16,4096]{1,0:T(8,128)S(1)}, bf16[16,4096]{1,0:T(8,128)(2,1)S(1)}, f32[16,4096]{1,0:T(8,128)S(1)}, bf16[16,4096]{1,0:T(8,128)(2,1)S(1)}) custom-call(bf16[16,4096]{1,0:T(8,128)(2,1)S(1)} %constant_dynamic-update-slice_fusion.2.refs_3_.refs_0_, bf16[16,4096]{1,0:T(8,128)(2,1)S(1)} %collective-permute-done.9.refs_1_, ...), custom_call_target="tpu_custom_call" | custom-call | flops 1207959552 | bytes 11010048 | tf_op jit(solution)/shard_map/pallas_call | solution.py:187
  33.8 2.0 %collective-permute-start.8 = (bf16[16,4096]{1,0:T(8,128)(2,1)S(1)}, bf16[16,4096]{1,0:T(8,128)(2,1)S(1)}, u32[]{:S(2)}, u32[]{:S(2)}) collective-permute-start(bf16[16,4096]{1,0:T(8,128)(2,1)S(1)} %add_convert_fusion.3), channel_id=1, source_target_pairs={{0,2},{1,3},{2,0},{3,1},{4,6},{5,7},{6,4},{7,5},{8,10},{9,11},{10,... | collective-permute-start | bytes 393224 | tf_op jit(solution)/shard_map/ppermute | solution.py:25
  35.7 1.6 %collective-permute-start.12 = (bf16[16,4096]{1,0:T(8,128)(2,1)S(1)}, bf16[16,4096]{1,0:T(8,128)(2,1)S(1)}, u32[]{:S(2)}, u32[]{:S(2)}) collective-permute-start(bf16[16,4096]{1,0:T(8,128)(2,1)S(1)} %get-tuple-element.37), channel_id=1, source_target_pairs={{0,1},{1,0},{2,3},{3,2},{4,5},{5,4},{6,7},{7,6},{8,9},{9,8},{10,11... | collective-permute-start | bytes 393224 | tf_op jit(solution)/shard_map/ppermute | solution.py:25
  37.3 5.5 %collective-permute-done.13 = bf16[16,4096]{1,0:T(8,128)(2,1)S(1)} collective-permute-done((bf16[16,4096]{1,0:T(8,128)(2,1)S(1)}, bf16[16,4096]{1,0:T(8,128)(2,1)S(1)}, u32[]{:S(2)}, u32[]{:S(2)}) %collective-permute-start.13) | collective-permute-done | bytes 131104 | tf_op jit(solution)/shard_map/ppermute | solution.py:25
  43.2 3.2 %collective-permute-start.15 = (bf16[16,4096]{1,0:T(8,128)(2,1)S(1)}, bf16[16,4096]{1,0:T(8,128)(2,1)S(1)}, u32[]{:S(2)}, u32[]{:S(2)}) collective-permute-start(bf16[16,4096]{1,0:T(8,128)(2,1)S(1)} %add_convert_fusion.2.refs_0_), channel_id=1, source_target_pairs={{0,1},{1,0},{2,3},{3,2},{4,5},{5,4},{6,7},{7,6},{8,9},{9,8},{10,11... | collective-permute-start | bytes 393224 | tf_op jit(solution)/shard_map/ppermute | solution.py:25
  46.5 1.5 %collective-permute-done.12 = bf16[16,4096]{1,0:T(8,128)(2,1)S(1)} collective-permute-done((bf16[16,4096]{1,0:T(8,128)(2,1)S(1)}, bf16[16,4096]{1,0:T(8,128)(2,1)S(1)}, u32[]{:S(2)}, u32[]{:S(2)}) %collective-permute-start.12) | collective-permute-done | bytes 131104 | tf_op jit(solution)/shard_map/ppermute | solution.py:25
  48.0 3.6 %collective-permute-done.14 = bf16[16,4096]{1,0:T(8,128)(2,1)S(1)} collective-permute-done((bf16[16,4096]{1,0:T(8,128)(2,1)S(1)}, bf16[16,4096]{1,0:T(8,128)(2,1)S(1)}, u32[]{:S(2)}, u32[]{:S(2)}) %collective-permute-start.14) | collective-permute-done | bytes 131104 | tf_op jit(solution)/shard_map/ppermute | solution.py:25
  52.5 1.6 %collective-permute-start.17 = (bf16[8,4096]{1,0:T(8,128)(2,1)S(1)}, bf16[8,4096]{1,0:T(8,128)(2,1)S(1)}, u32[]{:S(2)}, u32[]{:S(2)}) collective-permute-start(bf16[8,4096]{1,0:T(8,128)(2,1)S(1)} %get-tuple-element.45), channel_id=1, source_target_pairs={{0,8},{4,12},{8,0},{12,4},{1,9},{5,13},{9,1},{13,5},{2,10},{6,14},... | collective-permute-start | bytes 196616 | tf_op jit(solution)/shard_map/ppermute | solution.py:25
  54.0 1.8 %collective-permute-start.22 = (bf16[16,4096]{1,0:T(8,128)(2,1)S(1)}, bf16[16,4096]{1,0:T(8,128)(2,1)S(1)}, u32[]{:S(2)}, u32[]{:S(2)}) collective-permute-start(bf16[16,4096]{1,0:T(8,128)(2,1)S(1)} %add_convert_fusion.refs_4_), channel_id=1, source_target_pairs={{0,1},{1,0},{2,3},{3,2},{4,5},{5,4},{6,7},{7,6},{8,9},{9,8},{10,11... | collective-permute-start | bytes 393224 | tf_op jit(solution)/shard_map/ppermute | solution.py:25
  55.8 2.8 %collective-permute-done.20.refs_2_ = bf16[16,4096]{1,0:T(8,128)(2,1)S(1)} collective-permute-done((bf16[16,4096]{1,0:T(8,128)(2,1)S(1)}, bf16[16,4096]{1,0:T(8,128)(2,1)S(1)}, u32[]{:S(2)}, u32[]{:S(2)}) %collective-permute-start.20) | collective-permute-done | bytes 131104 | tf_op jit(solution)/shard_map/ppermute | solution.py:25
  58.6 1.4 %collective-permute-done.16.refs_6_ = bf16[16,4096]{1,0:T(8,128)(2,1)S(1)} collective-permute-done((bf16[16,4096]{1,0:T(8,128)(2,1)S(1)}, bf16[16,4096]{1,0:T(8,128)(2,1)S(1)}, u32[]{:S(2)}, u32[]{:S(2)}) %collective-permute-start.16) | collective-permute-done | bytes 131104 | tf_op jit(solution)/shard_map/ppermute | solution.py:25
  60.7 1.6 %collective-permute-start.19 = (bf16[8,4096]{1,0:T(8,128)(2,1)S(1)}, bf16[8,4096]{1,0:T(8,128)(2,1)S(1)}, u32[]{:S(2)}, u32[]{:S(2)}) collective-permute-start(bf16[8,4096]{1,0:T(8,128)(2,1)S(1)} %get-tuple-element.44), channel_id=1, source_target_pairs={{0,12},{4,8},{8,4},{12,0},{1,13},{5,9},{9,5},{13,1},{2,14},{6,10},... | collective-permute-start | bytes 196616 | tf_op jit(solution)/shard_map/ppermute | solution.py:25
  62.4 2.3 %collective-permute-done.19.refs_3_ = bf16[8,4096]{1,0:T(8,128)(2,1)S(1)} collective-permute-done((bf16[8,4096]{1,0:T(8,128)(2,1)S(1)}, bf16[8,4096]{1,0:T(8,128)(2,1)S(1)}, u32[]{:S(2)}, u32[]{:S(2)}) %collective-permute-start.19) | collective-permute-done | bytes 65568 | tf_op jit(solution)/shard_map/ppermute | solution.py:25
  65.9 3.7 %shard_map.91 = bf16[1,4096,1024]{2,1,0:T(8,128)(2,1)} custom-call(s32[1]{0:T(128)} %bitcast.3.place_ref, bf16[16,4096]{1,0:T(8,128)(2,1)S(1)} %add_convert_fusion.2.refs_0_, bf16[16,4096]{1,0:T(8,128)(2,1)S(1)} %collective-permute-done.15.refs_1_, bf16[16,4096]{1,0:T(8,128)(2,1)S(1)} %collective-permute-done.20.refs_2_, ...), custom_call_target="tpu_custom_call" | custom-call | flops 1073741824 | bytes 9437184 | tf_op jit(solution)/shard_map/pallas_call | solution.py:275
  (40 shorter events, 8.8 us)
Async XLA Ops:
  2.4 3.2 %collective-permute-start = (bf16[8,4096]{1,0:T(8,128)(2,1)S(1)}, bf16[8,4096]{1,0:T(8,128)(2,1)S(1)}, u32[]{:S(2)}, u32[]{:S(2)}) collective-permute-start(bf16[8,4096]{1,0:T(8,128)(2,1)S(1)} %get-tuple-element.24), channel_id=1, source_target_pairs={{0,4},{4,0},{8,12},{12,8},{1,5},{5,1},{9,13},{13,9},{2,6},{6,2},{1... | collective-permute-start | bytes 196616 | tf_op jit(solution)/shard_map/ppermute | solution.py:25
  2.9 7.1 %collective-permute-start.3 = (bf16[8,4096]{1,0:T(8,128)(2,1)S(1)}, bf16[8,4096]{1,0:T(8,128)(2,1)S(1)}, u32[]{:S(2)}, u32[]{:S(2)}) collective-permute-start(bf16[8,4096]{1,0:T(8,128)(2,1)S(1)} %get-tuple-element.25), channel_id=1, source_target_pairs={{0,8},{4,12},{8,0},{12,4},{1,9},{5,13},{9,1},{13,5},{2,10},{6,14},... | collective-permute-start | bytes 196616 | tf_op jit(solution)/shard_map/ppermute | solution.py:25
  5.5 4.5 %collective-permute-start.4 = (bf16[8,4096]{1,0:T(8,128)(2,1)S(1)}, bf16[8,4096]{1,0:T(8,128)(2,1)S(1)}, u32[]{:S(2)}, u32[]{:S(2)}) collective-permute-start(bf16[8,4096]{1,0:T(8,128)(2,1)S(1)} %get-tuple-element.26), channel_id=1, source_target_pairs={{0,12},{4,8},{8,4},{12,0},{1,13},{5,9},{9,5},{13,1},{2,14},{6,10},... | collective-permute-start | bytes 196616 | tf_op jit(solution)/shard_map/ppermute | solution.py:25
  5.6 11.1 %collective-permute-start.1 = (bf16[16,4096]{1,0:T(8,128)(2,1)S(1)}, bf16[16,4096]{1,0:T(8,128)(2,1)S(1)}, u32[]{:S(2)}, u32[]{:S(2)}) collective-permute-start(bf16[16,4096]{1,0:T(8,128)(2,1)S(1)} %constant_dynamic-update-slice_fusion.refs_0_), channel_id=1, source_target_pairs={{0,1},{1,0},{2,3},{3,2},{4,5},{5,4},{6,7},{7,6},{8,9},{9,8},{10,11... | collective-permute-start | bytes 393224 | tf_op jit(solution)/shard_map/ppermute | solution.py:25
  7.4 9.2 %collective-permute-start.2 = (bf16[16,4096]{1,0:T(8,128)(2,1)S(1)}, bf16[16,4096]{1,0:T(8,128)(2,1)S(1)}, u32[]{:S(2)}, u32[]{:S(2)}) collective-permute-start(bf16[16,4096]{1,0:T(8,128)(2,1)S(1)} %constant_dynamic-update-slice_fusion.refs_0_), channel_id=1, source_target_pairs={{0,2},{1,3},{2,0},{3,1},{4,6},{5,7},{6,4},{7,5},{8,10},{9,11},{10,... | collective-permute-start | bytes 393224 | tf_op jit(solution)/shard_map/ppermute | solution.py:25
  16.7 7.3 %collective-permute-start.10 = (bf16[16,4096]{1,0:T(8,128)(2,1)S(1)}, bf16[16,4096]{1,0:T(8,128)(2,1)S(1)}, u32[]{:S(2)}, u32[]{:S(2)}) collective-permute-start(bf16[16,4096]{1,0:T(8,128)(2,1)S(1)} %constant_dynamic-update-slice_fusion.2.refs_3_.refs_0_), channel_id=1, source_target_pairs={{0,2},{1,3},{2,0},{3,1},{4,6},{5,7},{6,4},{7,5},{8,10},{9,11},{10,... | collective-permute-start | bytes 393224 | tf_op jit(solution)/shard_map/ppermute | solution.py:25
  17.0 8.4 %collective-permute-start.5 = (bf16[16,4096]{1,0:T(8,128)(2,1)S(1)}, bf16[16,4096]{1,0:T(8,128)(2,1)S(1)}, u32[]{:S(2)}, u32[]{:S(2)}) collective-permute-start(bf16[16,4096]{1,0:T(8,128)(2,1)S(1)} %collective-permute-done.2.refs_2_), channel_id=1, source_target_pairs={{0,1},{1,0},{2,3},{3,2},{4,5},{5,4},{6,7},{7,6},{8,9},{9,8},{10,11... | collective-permute-start | bytes 393224 | tf_op jit(solution)/shard_map/ppermute | solution.py:25
  19.7 9.7 %collective-permute-start.9 = (bf16[16,4096]{1,0:T(8,128)(2,1)S(1)}, bf16[16,4096]{1,0:T(8,128)(2,1)S(1)}, u32[]{:S(2)}, u32[]{:S(2)}) collective-permute-start(bf16[16,4096]{1,0:T(8,128)(2,1)S(1)} %constant_dynamic-update-slice_fusion.2.refs_3_.refs_0_), channel_id=1, source_target_pairs={{0,1},{1,0},{2,3},{3,2},{4,5},{5,4},{6,7},{7,6},{8,9},{9,8},{10,11... | collective-permute-start | bytes 393224 | tf_op jit(solution)/shard_map/ppermute | solution.py:25
  24.0 6.8 %collective-permute-start.11 = (bf16[16,4096]{1,0:T(8,128)(2,1)S(1)}, bf16[16,4096]{1,0:T(8,128)(2,1)S(1)}, u32[]{:S(2)}, u32[]{:S(2)}) collective-permute-start(bf16[16,4096]{1,0:T(8,128)(2,1)S(1)} %collective-permute-done.10.refs_2_), channel_id=1, source_target_pairs={{0,1},{1,0},{2,3},{3,2},{4,5},{5,4},{6,7},{7,6},{8,9},{9,8},{10,11... | collective-permute-start | bytes 393224 | tf_op jit(solution)/shard_map/ppermute | solution.py:25
  27.3 6.5 %collective-permute-start.7 = (bf16[16,4096]{1,0:T(8,128)(2,1)S(1)}, bf16[16,4096]{1,0:T(8,128)(2,1)S(1)}, u32[]{:S(2)}, u32[]{:S(2)}) collective-permute-start(bf16[16,4096]{1,0:T(8,128)(2,1)S(1)} %get-tuple-element.34), channel_id=1, source_target_pairs={{0,1},{1,0},{2,3},{3,2},{4,5},{5,4},{6,7},{7,6},{8,9},{9,8},{10,11... | collective-permute-start | bytes 393224 | tf_op jit(solution)/shard_map/ppermute | solution.py:25
  28.1 15.1 %collective-permute-start.6 = (bf16[16,4096]{1,0:T(8,128)(2,1)S(1)}, bf16[16,4096]{1,0:T(8,128)(2,1)S(1)}, u32[]{:S(2)}, u32[]{:S(2)}) collective-permute-start(bf16[16,4096]{1,0:T(8,128)(2,1)S(1)} %get-tuple-element.32), channel_id=1, source_target_pairs={{0,1},{1,0},{2,3},{3,2},{4,5},{5,4},{6,7},{7,6},{8,9},{9,8},{10,11... | collective-permute-start | bytes 393224 | tf_op jit(solution)/shard_map/ppermute | solution.py:25
  32.7 10.1 %collective-permute-start.13 = (bf16[16,4096]{1,0:T(8,128)(2,1)S(1)}, bf16[16,4096]{1,0:T(8,128)(2,1)S(1)}, u32[]{:S(2)}, u32[]{:S(2)}) collective-permute-start(bf16[16,4096]{1,0:T(8,128)(2,1)S(1)} %get-tuple-element.39), channel_id=1, source_target_pairs={{0,1},{1,0},{2,3},{3,2},{4,5},{5,4},{6,7},{7,6},{8,9},{9,8},{10,11... | collective-permute-start | bytes 393224 | tf_op jit(solution)/shard_map/ppermute | solution.py:25
  33.8 9.4 %collective-permute-start.8 = (bf16[16,4096]{1,0:T(8,128)(2,1)S(1)}, bf16[16,4096]{1,0:T(8,128)(2,1)S(1)}, u32[]{:S(2)}, u32[]{:S(2)}) collective-permute-start(bf16[16,4096]{1,0:T(8,128)(2,1)S(1)} %add_convert_fusion.3), channel_id=1, source_target_pairs={{0,2},{1,3},{2,0},{3,1},{4,6},{5,7},{6,4},{7,5},{8,10},{9,11},{10,... | collective-permute-start | bytes 393224 | tf_op jit(solution)/shard_map/ppermute | solution.py:25
  35.7 12.2 %collective-permute-start.12 = (bf16[16,4096]{1,0:T(8,128)(2,1)S(1)}, bf16[16,4096]{1,0:T(8,128)(2,1)S(1)}, u32[]{:S(2)}, u32[]{:S(2)}) collective-permute-start(bf16[16,4096]{1,0:T(8,128)(2,1)S(1)} %get-tuple-element.37), channel_id=1, source_target_pairs={{0,1},{1,0},{2,3},{3,2},{4,5},{5,4},{6,7},{7,6},{8,9},{9,8},{10,11... | collective-permute-start | bytes 393224 | tf_op jit(solution)/shard_map/ppermute | solution.py:25
  42.8 8.8 %collective-permute-start.14 = (bf16[16,4096]{1,0:T(8,128)(2,1)S(1)}, bf16[16,4096]{1,0:T(8,128)(2,1)S(1)}, u32[]{:S(2)}, u32[]{:S(2)}) collective-permute-start(bf16[16,4096]{1,0:T(8,128)(2,1)S(1)} %add_convert_fusion.1), channel_id=1, source_target_pairs={{0,2},{1,3},{2,0},{3,1},{4,6},{5,7},{6,4},{7,5},{8,10},{9,11},{10,... | collective-permute-start | bytes 393224 | tf_op jit(solution)/shard_map/ppermute | solution.py:25
  43.2 8.5 %collective-permute-start.15 = (bf16[16,4096]{1,0:T(8,128)(2,1)S(1)}, bf16[16,4096]{1,0:T(8,128)(2,1)S(1)}, u32[]{:S(2)}, u32[]{:S(2)}) collective-permute-start(bf16[16,4096]{1,0:T(8,128)(2,1)S(1)} %add_convert_fusion.2.refs_0_), channel_id=1, source_target_pairs={{0,1},{1,0},{2,3},{3,2},{4,5},{5,4},{6,7},{7,6},{8,9},{9,8},{10,11... | collective-permute-start | bytes 393224 | tf_op jit(solution)/shard_map/ppermute | solution.py:25
  46.4 12.2 %collective-permute-start.20 = (bf16[16,4096]{1,0:T(8,128)(2,1)S(1)}, bf16[16,4096]{1,0:T(8,128)(2,1)S(1)}, u32[]{:S(2)}, u32[]{:S(2)}) collective-permute-start(bf16[16,4096]{1,0:T(8,128)(2,1)S(1)} %add_convert_fusion.2.refs_0_), channel_id=1, source_target_pairs={{0,2},{1,3},{2,0},{3,1},{4,6},{5,7},{6,4},{7,5},{8,10},{9,11},{10,... | collective-permute-start | bytes 393224 | tf_op jit(solution)/shard_map/ppermute | solution.py:25
  51.7 8.4 %collective-permute-start.16 = (bf16[16,4096]{1,0:T(8,128)(2,1)S(1)}, bf16[16,4096]{1,0:T(8,128)(2,1)S(1)}, u32[]{:S(2)}, u32[]{:S(2)}) collective-permute-start(bf16[16,4096]{1,0:T(8,128)(2,1)S(1)} %add_convert_fusion.refs_4_), channel_id=1, source_target_pairs={{0,2},{1,3},{2,0},{3,1},{4,6},{5,7},{6,4},{7,5},{8,10},{9,11},{10,... | collective-permute-start | bytes 393224 | tf_op jit(solution)/shard_map/ppermute | solution.py:25
  52.5 6.2 %collective-permute-start.17 = (bf16[8,4096]{1,0:T(8,128)(2,1)S(1)}, bf16[8,4096]{1,0:T(8,128)(2,1)S(1)}, u32[]{:S(2)}, u32[]{:S(2)}) collective-permute-start(bf16[8,4096]{1,0:T(8,128)(2,1)S(1)} %get-tuple-element.45), channel_id=1, source_target_pairs={{0,8},{4,12},{8,0},{12,4},{1,9},{5,13},{9,1},{13,5},{2,10},{6,14},... | collective-permute-start | bytes 196616 | tf_op jit(solution)/shard_map/ppermute | solution.py:25
  54.0 11.9 %collective-permute-start.22 = (bf16[16,4096]{1,0:T(8,128)(2,1)S(1)}, bf16[16,4096]{1,0:T(8,128)(2,1)S(1)}, u32[]{:S(2)}, u32[]{:S(2)}) collective-permute-start(bf16[16,4096]{1,0:T(8,128)(2,1)S(1)} %add_convert_fusion.refs_4_), channel_id=1, source_target_pairs={{0,1},{1,0},{2,3},{3,2},{4,5},{5,4},{6,7},{7,6},{8,9},{9,8},{10,11... | collective-permute-start | bytes 393224 | tf_op jit(solution)/shard_map/ppermute | solution.py:25
  58.6 7.3 %collective-permute-start.21 = (bf16[16,4096]{1,0:T(8,128)(2,1)S(1)}, bf16[16,4096]{1,0:T(8,128)(2,1)S(1)}, u32[]{:S(2)}, u32[]{:S(2)}) collective-permute-start(bf16[16,4096]{1,0:T(8,128)(2,1)S(1)} %collective-permute-done.20.refs_2_), channel_id=1, source_target_pairs={{0,1},{1,0},{2,3},{3,2},{4,5},{5,4},{6,7},{7,6},{8,9},{9,8},{10,11... | collective-permute-start | bytes 393224 | tf_op jit(solution)/shard_map/ppermute | solution.py:25
  60.1 5.9 %collective-permute-start.23 = (bf16[16,4096]{1,0:T(8,128)(2,1)S(1)}, bf16[16,4096]{1,0:T(8,128)(2,1)S(1)}, u32[]{:S(2)}, u32[]{:S(2)}) collective-permute-start(bf16[16,4096]{1,0:T(8,128)(2,1)S(1)} %collective-permute-done.16.refs_6_), channel_id=1, source_target_pairs={{0,1},{1,0},{2,3},{3,2},{4,5},{5,4},{6,7},{7,6},{8,9},{9,8},{10,11... | collective-permute-start | bytes 393224 | tf_op jit(solution)/shard_map/ppermute | solution.py:25
  60.7 1.7 %collective-permute-start.18 = (bf16[8,4096]{1,0:T(8,128)(2,1)S(1)}, bf16[8,4096]{1,0:T(8,128)(2,1)S(1)}, u32[]{:S(2)}, u32[]{:S(2)}) collective-permute-start(bf16[8,4096]{1,0:T(8,128)(2,1)S(1)} %get-tuple-element.46), channel_id=1, source_target_pairs={{0,4},{4,0},{8,12},{12,8},{1,5},{5,1},{9,13},{13,9},{2,6},{6,2},{1... | collective-permute-start | bytes 196616 | tf_op jit(solution)/shard_map/ppermute | solution.py:25
  60.7 3.9 %collective-permute-start.19 = (bf16[8,4096]{1,0:T(8,128)(2,1)S(1)}, bf16[8,4096]{1,0:T(8,128)(2,1)S(1)}, u32[]{:S(2)}, u32[]{:S(2)}) collective-permute-start(bf16[8,4096]{1,0:T(8,128)(2,1)S(1)} %get-tuple-element.44), channel_id=1, source_target_pairs={{0,12},{4,8},{8,4},{12,0},{1,13},{5,9},{9,5},{13,1},{2,14},{6,10},... | collective-permute-start | bytes 196616 | tf_op jit(solution)/shard_map/ppermute | solution.py:25
